TPU v7x, 128 devices: a whole 4x4x4 slice. The times are simulated.
128 devices in a mesh: dp: 4 (over y), seq: 32 (over x, z, core).
Axes of the slice: x: 4, y: 4, z: 4, core: 2. Of those that a mesh axis runs over, the one named last changes fastest.
Arguments:
- tokens: bfloat16 [4, 8192, 576], P('dp', 'seq'), may hold values from -6 to 6
- segments: int32 [4, 8192], P('dp', 'seq'), may hold values from 0 to 2, as said below
- positions: int32 [4, 8192], P('dp', 'seq'), may hold values from 0 to 8189, as said below
- norm_gain: float32 [576], replicated, may hold values from 0.5 to 1.5
- query_weight: bfloat16 [576, 576], replicated, may hold values from -0.25 to 0.25
- key_weight: bfloat16 [576, 192], replicated, may hold values from -0.25 to 0.25
- value_weight: bfloat16 [576, 192], replicated, may hold values from -0.25 to 0.25
- output_weight: bfloat16 [576, 576], replicated, may hold values from -4 to 4
- mlp_gain: float32 [576], replicated, may hold values from 0.5 to 1.5
- gate_weight: bfloat16 [576, 1536], replicated, may hold values from -0.25 to 0.25
- up_weight: bfloat16 [576, 1536], replicated, may hold values from -0.25 to 0.25
- down_weight: bfloat16 [1536, 576], replicated, may hold values from -0.15625 to 0.15625
- cotangent: bfloat16 [4, 8192, 576], P('dp', 'seq'), may hold values from -6 to 6
Outputs:
- layer_output: bfloat16 [4, 8192, 576], P('dp', 'seq')
- input_grad: bfloat16 [4, 8192, 576], P('dp', 'seq')
- grad_norm_gain: float32 [576], replicated
- grad_query_weight: float32 [576, 576], replicated
- grad_key_weight: float32 [576, 192], replicated
- grad_value_weight: float32 [576, 192], replicated
- grad_output_weight: float32 [576, 576], replicated
- grad_mlp_gain: float32 [576], replicated
- grad_gate_weight: float32 [576, 1536], replicated
- grad_up_weight: float32 [576, 1536], replicated
- grad_down_weight: float32 [1536, 576], replicated
Inputs may be any that keep to these rules, and one draw needn't show every extreme that they name: `segments`: in each row segment 0 is a fragment within the first 256 tokens, segment 1 a document from there to within the last 256 tokens, segment 2 the rest; ids never fall. Within a segment positions rise by one from token to token; in every row segment 1 ends at position 8189, the other segments start at an offset below 1024.
All inputs are finite; a program needn't handle non-finite values.
Results may differ from a plain program's by a relative error of at most 0.019.
Values may be sent and summed in bfloat16 or wider, within the bound.
No kernel may reach another device: no remote copies, remote signals or barrier semaphores. Data moves between devices by JAX's collectives and lax.ppermute only.
A program may use at most 128 MiB of HBM per device.

v0:
```python
from functools import partial
import math

import jax
import jax.numpy as jnp
from jax import lax
from jax.sharding import PartitionSpec as P

H = 9
KVH = 3
HD = 64


EPSILON = 1e-05
ROPE_BASE = 10000.0
NEGATIVE = -1000000000.0


def normed(values, gain):
    return values * lax.rsqrt(jnp.mean(values * values, axis=-1, keepdims=True) + EPSILON) * gain


def rotate(values, places):
    half_dim = values.shape[-1] // 2
    freqs = ROPE_BASE ** (-2.0 * jnp.arange(half_dim).astype(jnp.float32) / values.shape[-1])
    angles = places.astype(jnp.float32)[:, None] * freqs[None, :]
    cosine = jnp.cos(angles)[:, None, :]
    sine = jnp.sin(angles)[:, None, :]
    first_half = values[..., :half_dim]
    second_half = values[..., half_dim:]
    return jnp.concatenate(
        [first_half * cosine - second_half * sine, second_half * cosine + first_half * sine],
        axis=-1,
    )


def swiglu(gate_value, up_value):
    return jax.nn.silu(gate_value) * up_value


def masked_scores(queries, key_block, query_rows, key_rows, query_segs, key_segs):
    scaling = queries.shape[-1] ** (-0.5)
    raw_scores = (
        jnp.einsum("qkgd,skd->kgqs", queries, key_block, preferred_element_type=jnp.float32)
        * scaling
    )
    allowed = (key_rows[None, :] <= query_rows[:, None]) & (
        key_segs[None, :] == query_segs[:, None]
    )
    return (jnp.where(allowed[None, None], raw_scores, NEGATIVE), allowed)


def split_blocks(shards, first_row, head_shape):
    key_part, value_part, seg_part = shards
    row_count = key_part.shape[0]
    block_rows = math.gcd(row_count, 1024)
    block_count = row_count // block_rows
    key_blocks = key_part.reshape((block_count, block_rows) + head_shape)
    value_blocks = value_part.reshape((block_count, block_rows) + head_shape)
    seg_blocks = seg_part.astype(jnp.float32).reshape(block_count, block_rows)
    row_blocks = first_row + jnp.arange(row_count, dtype=jnp.int32).reshape(block_count, block_rows)
    return (key_blocks, value_blocks, seg_blocks, row_blocks)


def fold_keys(running, shards, first_row, queries, query_rows, query_segs):
    head_shape = (queries.shape[1], queries.shape[-1])

    def fold_work(fold_state, block_data):
        run_max, denominator, weighted = fold_state
        key_block, value_block, seg_block, row_block = block_data
        scores, allowed = masked_scores(
            queries, key_block, query_rows, row_block, query_segs, seg_block
        )
        new_max = jnp.maximum(run_max, jnp.max(scores, axis=-1, keepdims=True))
        weights_exp = jnp.where(allowed[None, None], jnp.exp(scores - new_max), 0.0)
        factor = jnp.exp(run_max - new_max)
        denominator = denominator * factor + jnp.sum(weights_exp, axis=-1, keepdims=True)
        weighted = weighted * factor + jnp.einsum(
            "kgqs,skd->kgqd",
            weights_exp.astype(jnp.bfloat16),
            value_block,
            preferred_element_type=jnp.float32,
        )
        return (new_max, denominator, weighted)

    def fold_step(fold_state, block_data):
        needed = block_data[3][0] <= query_rows[-1]
        updated = lax.cond(needed, fold_work, lambda state, data: state, fold_state, block_data)
        return (updated, None)

    folded, unused = lax.scan(fold_step, running, split_blocks(shards, first_row, head_shape))
    return folded


def key_gradients(gathered, queries, grad_attn, log_norm, row_delta, query_rows, query_segs):
    head_shape = (queries.shape[1], queries.shape[-1])
    scaling = queries.shape[-1] ** (-0.5)
    blocks = split_blocks(gathered, 0, head_shape)
    block_rows = blocks[0].shape[1]
    stack_width = 2 * head_shape[0] * head_shape[1]

    def back_work(query_sum, block_data):
        key_block, value_block, seg_block, row_block = block_data
        scores, allowed = masked_scores(
            queries, key_block, query_rows, row_block, query_segs, seg_block
        )
        prob_block = jnp.where(allowed[None, None], jnp.exp(scores - log_norm), 0.0)
        grad_probs = jnp.einsum(
            "qkgd,skd->kgqs", grad_attn, value_block, preferred_element_type=jnp.float32
        )
        grad_scores = (prob_block * (grad_probs - row_delta)).astype(jnp.bfloat16)
        query_sum = (
            query_sum
            + jnp.einsum(
                "kgqs,skd->qkgd", grad_scores, key_block, preferred_element_type=jnp.float32
            )
            * scaling
        )
        grad_keys = (
            jnp.einsum("kgqs,qkgd->skd", grad_scores, queries, preferred_element_type=jnp.float32)
            * scaling
        )
        grad_values = jnp.einsum(
            "kgqs,qkgd->skd",
            prob_block.astype(jnp.bfloat16),
            grad_attn,
            preferred_element_type=jnp.float32,
        )
        stacked = jnp.concatenate(
            [grad_keys.reshape(block_rows, -1), grad_values.reshape(block_rows, -1)], axis=1
        )
        return (query_sum, stacked)

    def skip_work(query_sum, block_data):
        return (query_sum, jnp.zeros((block_rows, stack_width), jnp.float32))

    def back_step(query_sum, block_data):
        needed = block_data[3][0] <= query_rows[-1]
        return lax.cond(needed, back_work, skip_work, query_sum, block_data)

    start_sum = jnp.zeros(queries.shape, jnp.float32)
    grad_query, key_terms = lax.scan(back_step, start_sum, blocks)
    return (grad_query, key_terms.reshape(-1, key_terms.shape[-1]))


def body(
    tokens,
    segments,
    positions,
    norm_gain,
    query_weight,
    key_weight,
    value_weight,
    output_weight,
    mlp_gain,
    gate_weight,
    up_weight,
    down_weight,
    cotangent,
):
    length = tokens.shape[1]
    group = H // KVH
    kv_width = KVH * HD
    inputs = tokens[0].astype(jnp.float32)
    places = positions[0]
    query_rows = lax.axis_index("seq") * length + jnp.arange(length, dtype=jnp.int32)
    query_segs = segments[0].astype(jnp.float32)
    first_norm, norm_pull = jax.vjp(normed, inputs, norm_gain)
    activation = first_norm.astype(jnp.bfloat16)
    query_raw = jnp.dot(activation, query_weight, preferred_element_type=jnp.float32).reshape(
        length, H, HD
    )
    query_rot, query_pull = jax.vjp(partial(rotate, places=places), query_raw)
    queries = query_rot.astype(jnp.bfloat16).reshape(length, KVH, group, HD)
    key_raw = jnp.dot(activation, key_weight, preferred_element_type=jnp.float32).reshape(
        length, KVH, HD
    )
    key_rot, key_pull = jax.vjp(partial(rotate, places=places), key_raw)
    key_flat = key_rot.astype(jnp.bfloat16).reshape(length, kv_width)
    value_flat = jnp.dot(activation, value_weight, preferred_element_type=jnp.float32).astype(
        jnp.bfloat16
    )
    seg_wire = segments[0].astype(jnp.bfloat16)
    initial = (
        jnp.full((KVH, group, length, 1), NEGATIVE, jnp.float32),
        jnp.zeros((KVH, group, length, 1), jnp.float32),
        jnp.zeros((KVH, group, length, HD), jnp.float32),
    )
    folder = partial(fold_keys, queries=queries, query_rows=query_rows, query_segs=query_segs)
    run_max, denominator, weighted = folder(
        initial,
        (
            lax.all_gather(key_flat, "seq", axis=0, tiled=True),
            lax.all_gather(value_flat, "seq", axis=0, tiled=True),
            lax.all_gather(seg_wire, "seq", axis=0, tiled=True),
        ),
        jnp.int32(0),
    )
    attn_heads = (weighted / denominator).transpose(2, 0, 1, 3)
    log_norm = run_max + jnp.log(denominator)
    attn_low = attn_heads.reshape(length, H * HD).astype(jnp.bfloat16)
    middle = inputs + jnp.dot(attn_low, output_weight, preferred_element_type=jnp.float32)
    second_norm, mlp_pull = jax.vjp(normed, middle, mlp_gain)
    activation_two = second_norm.astype(jnp.bfloat16)
    gate_value = jnp.dot(activation_two, gate_weight, preferred_element_type=jnp.float32)
    up_value = jnp.dot(activation_two, up_weight, preferred_element_type=jnp.float32)
    hidden_full, swiglu_pull = jax.vjp(swiglu, gate_value, up_value)
    hidden = hidden_full.astype(jnp.bfloat16)
    result = middle + jnp.dot(hidden, down_weight, preferred_element_type=jnp.float32)
    out_low = cotangent[0]
    grad_down = jnp.einsum("tf,td->fd", hidden, out_low, preferred_element_type=jnp.float32)
    grad_hidden = jnp.einsum("td,fd->tf", out_low, down_weight, preferred_element_type=jnp.float32)
    grad_gate, grad_up = swiglu_pull(grad_hidden)
    gate_low = grad_gate.astype(jnp.bfloat16)
    up_low = grad_up.astype(jnp.bfloat16)
    grad_gate_weight = jnp.einsum(
        "td,tf->df", activation_two, gate_low, preferred_element_type=jnp.float32
    )
    grad_up_weight = jnp.einsum(
        "td,tf->df", activation_two, up_low, preferred_element_type=jnp.float32
    )
    grad_act_two = jnp.einsum(
        "tf,df->td", gate_low, gate_weight, preferred_element_type=jnp.float32
    ) + jnp.einsum("tf,df->td", up_low, up_weight, preferred_element_type=jnp.float32)
    grad_middle_norm, grad_mlp_gain = mlp_pull(grad_act_two)
    grad_middle = out_low.astype(jnp.float32) + grad_middle_norm
    middle_low = grad_middle.astype(jnp.bfloat16)
    grad_output_weight = jnp.einsum(
        "te,td->ed", attn_low, middle_low, preferred_element_type=jnp.float32
    )
    grad_attn = (
        jnp.einsum("td,ed->te", middle_low, output_weight, preferred_element_type=jnp.float32)
        .astype(jnp.bfloat16)
        .reshape(length, KVH, group, HD)
    )
    row_delta = jnp.einsum("qkgd,qkgd->kgq", grad_attn.astype(jnp.float32), attn_heads)[..., None]
    gathered = (
        lax.all_gather(key_flat, "seq", axis=0, tiled=True),
        lax.all_gather(value_flat, "seq", axis=0, tiled=True),
        lax.all_gather(seg_wire, "seq", axis=0, tiled=True),
    )
    grad_query, key_terms = key_gradients(
        gathered, queries, grad_attn, log_norm, row_delta, query_rows, query_segs
    )
    key_shares = lax.psum_scatter(
        key_terms.astype(jnp.bfloat16), "seq", scatter_dimension=0, tiled=True
    ).astype(jnp.float32)
    (grad_key_raw,) = key_pull(key_shares[:, :kv_width].reshape(length, KVH, HD))
    key_low = grad_key_raw.reshape(length, kv_width).astype(jnp.bfloat16)
    value_low = key_shares[:, kv_width:].astype(jnp.bfloat16)
    (grad_query_raw,) = query_pull(grad_query.reshape(length, H, HD))
    query_low = grad_query_raw.reshape(length, H * HD).astype(jnp.bfloat16)
    grad_query_weight = jnp.einsum(
        "td,te->de", activation, query_low, preferred_element_type=jnp.float32
    )
    grad_key_weight = jnp.einsum(
        "td,te->de", activation, key_low, preferred_element_type=jnp.float32
    )
    grad_value_weight = jnp.einsum(
        "td,te->de", activation, value_low, preferred_element_type=jnp.float32
    )
    grad_activation = (
        jnp.einsum("te,de->td", query_low, query_weight, preferred_element_type=jnp.float32)
        + jnp.einsum("te,de->td", key_low, key_weight, preferred_element_type=jnp.float32)
        + jnp.einsum("te,de->td", value_low, value_weight, preferred_element_type=jnp.float32)
    )
    grad_input_norm, grad_norm_gain = norm_pull(grad_activation)
    grad_input = grad_middle + grad_input_norm
    totals = lax.psum(
        (
            grad_norm_gain,
            grad_query_weight,
            grad_key_weight,
            grad_value_weight,
            grad_output_weight,
            grad_mlp_gain,
            grad_gate_weight,
            grad_up_weight,
            grad_down,
        ),
        ("dp", "seq"),
    )
    return (
        result.astype(jnp.bfloat16)[None],
        grad_input.astype(jnp.bfloat16)[None],
        totals[0],
        totals[1],
        totals[2],
        totals[3],
        totals[4],
        totals[5],
        totals[6],
        totals[7],
        totals[8],
    )


def solution(mesh):
    return jax.shard_map(
        body,
        mesh=mesh,
        in_specs=(
            P("dp", "seq", None),
            P("dp", "seq"),
            P("dp", "seq"),
            P(),
            P(),
            P(),
            P(),
            P(),
            P(),
            P(),
            P(),
            P(),
            P("dp", "seq", None),
        ),
        out_specs=(
            P("dp", "seq", None),
            P("dp", "seq", None),
            P(),
            P(),
            P(),
            P(),
            P(),
            P(),
            P(),
            P(),
            P(),
        ),
        check_vma=False,
    )
```

profile of v0, /device:TPU:1, one launch (start us, length us, event | category | flops | bytes accessed | tf_op | source)
XLA Modules:
  0.0 673.3 jit_solution(8394087583773581849)
XLA Ops:
  7.3 1.2 fusion.59
  9.4 1.4 fusion.74
  11.6 2.0 convolution_convert_fusion.1
  13.7 0.8 fusion.94
  14.5 26.8 %all-gather = bf16[1,8192]{1,0:T(2,128)(2,1)S(1)} all-gather(bf16[1,256]{1,0:T(2,128)(2,1)S(1)} %get-tuple-element.504), channel_id=2, replica_groups=mesh['dp'=4,'seq'=32] {'seq'}, dimensions={1}, use_global_device_ids=true | all-gather | bytes 16896 | tf_op jit(solution)/shard_map/all_gather | solution.py:195
  41.3 1.5 copy.46
  44.2 18.1 %all-gather.4.cloned.1.call-done = bf16[8192,192]{0,1:T(8,128)(2,1)} async-done(((bf16[256,192]{0,1:T(8,128)(2,1)}), bf16[8192,192]{0,1:T(8,128)(2,1)}) %all-gather.4.cloned.1.call-update) | async-done | bytes 3145744 | tf_op jit(solution)/shard_map/all_gather | solution.py:193
  62.3 4.1 copy.82
  66.4 3.4 copy.47
  69.8 41.7 %all-gather.6.cloned.1.call-done = bf16[8192,192]{0,1:T(8,128)(2,1)} async-done(((bf16[256,192]{0,1:T(8,128)(2,1)}), bf16[8192,192]{0,1:T(8,128)(2,1)}) %all-gather.6.cloned.1.call-update) | async-done | bytes 3145744 | tf_op jit(solution)/shard_map/all_gather | solution.py:194
  111.5 4.1 copy.83
  115.5 3.4 copy.48
  119.0 28.8 %while.29 = (s32[]{:T(128)}, f32[3,3,256,1]{2,1,0,3:T(4,128)S(1)}, f32[3,3,256,1]{2,1,0,3:T(4,128)S(1)}, f32[3,3,256,64]{2,3,1,0:T(8,128)S(1)}, s32[8,1024]{1,0:...) while((s32[]{:T(128)}, f32[3,3,256,1]{2,1,0,3:T(4,128)S(1)}, ...), condition=%wide.region_6.7_spmd, body=%wide.region_1.6_spmd.sunk | while | flops 635738880 | bytes 31796536 | solution.py:91
  121.6 9.0 %conditional.4 = ((f32[3,3,256,1]{2,1,0,3:T(4,128)S(1)}, f32[3,3,256,1]{2,1,0,3:T(4,128)S(1)}, f32[3,3,256,64]{2,3,1,0:T(8,128)S(1)})) conditional(s32[]{:T(128)} %convert_element_type.274, (f32[3,3,256,1]{2,1,0,3:T(4,128)S(1)}, f32[3,3,256,1]{2,1,0,3:T(4,128)S(1)}, f32[3,3,256,64]{2,3,1,0:T(8,128)S(1)}) %tuple.85, (s32[1,1024]{1,0:T(1,128)S(1)}, ...), branch_computations={%region_2.2_spmd, %region_3.5_spmd} | conditional | flops 635738880 | bytes 31788068 | solution.py:88
  122.0 2.6 fusion
  124.7 2.2 fusion.2
  127.0 3.6 fusion.6
  149.6 0.8 fusion.95
  150.4 0.8 fusion.96
  151.2 2.4 multiply_convert_fusion
  154.2 0.8 multiply_reduce_fusion
  155.3 0.8 copy-done.5
  156.6 0.9 broadcast_in_dim.125
  157.5 45.6 %while.30 = (s32[]{:T(128)}, f32[256,3,3,64]{0,3,2,1:T(8,128)}, bf16[8,1024,384]{2,1,0:T(8,128)(2,1)}, s32[8,1024]{1,0:T(8,128)S(1)}, s32[256]{0:T(256)S(1)}, /*...) while((s32[]{:T(128)}, f32[256,3,3,64]{0,3,2,1:T(8,128)}, ...), condition=%wide.region_12.13_spmd, body=%wide.region_9.12_spmd.sunk | while | flops 1541308416 | bytes 53534016 | solution.py:142
  159.8 15.6 %conditional.5 = (f32[256,3,3,64]{0,3,2,1:T(8,128)}, bf16[1,1024,384]{1,2,0:T(8,128)(2,1)S(1)}) conditional(s32[]{:T(128)} %convert_element_type.275, f32[256,3,3,64]{0,3,2,1:T(8,128)} %get-tuple-element.726, (s32[1,1024]{1,0:T(1,128)S(1)}, s32[256]{0:T(256)S(1)}, f32[8,1024]{1,0:T(8,128)S(1)}, s32[]{:T(128)}, f32[256]{0:T(256)S(1)}, ...), branch_computations={%region_10.10_spmd, %region_11.11_spmd} | conditional | flops 1541308416 | bytes 50379312 | solution.py:139
  159.8 2.6 fusion.34
  162.8 4.6 fusion.21
  167.3 2.9 fusion.31
  170.2 2.6 fusion.26
  172.9 2.5 fusion.29
  175.8 1.0 constant_dynamic-update-slice_fusion.2
  179.6 1.0 constant_dynamic-update-slice_fusion.2
  183.3 1.0 constant_dynamic-update-slice_fusion.2
  187.1 1.0 constant_dynamic-update-slice_fusion.2
  190.8 1.0 constant_dynamic-update-slice_fusion.2
  194.6 1.0 constant_dynamic-update-slice_fusion.2
  198.3 1.0 constant_dynamic-update-slice_fusion.2
  202.1 1.0 constant_dynamic-update-slice_fusion.2
  203.1 8.6 %copy.52 = bf16[8192,384]{0,1:T(8,128)(2,1)} copy(bf16[8192,384]{1,0:T(8,128)(2,1)} %bitcast.240) | data formatting | bytes 12582912 | tf_op jit(solution)/shard_map/convert_element_type | solution.py:246
  212.5 1.1 multiply_add_fusion.1
  213.7 1.6 fusion.78
  215.3 1.5 fusion.80
  216.8 2.4 fusion.99
  219.2 2.4 fusion.100
  221.7 2.4 fusion.68
  224.1 242.7 %reduce-scatter.2.cloned.1.call-done = bf16[256,384]{0,1:T(8,128)(2,1)} async-done(((bf16[8192,384]{0,1:T(8,128)(2,1)}), bf16[256,384]{0,1:T(8,128)(2,1)}) %reduce-scatter.2.cloned.1.call-update) | async-done | bytes 196624 | tf_op jit(solution)/shard_map/reduce_scatter | solution.py:245
  466.8 0.9 slice.44
  467.8 1.1 fusion.76
  468.9 2.0 fusion.83
  470.9 1.0 copy-done.4
  472.0 2.6 fusion.50
  474.6 1.2 fusion.98
  476.8 66.7 %all-reduce.4 = (f32[576]{0:T(1024)}, f32[576]{0:T(1024)}) all-reduce(f32[576]{0:T(1024)S(1)} %get-tuple-element.427, f32[576]{0:T(1024)S(1)} %get-tuple-element.425), channel_id=1, replica_groups=mesh['dp'=4,'seq'=32] {'dp','seq'}, use_global_device_ids=true, to_apply=%region_16.17 | all-reduce | flops 1152 | bytes 9216 | tf_op jit(solution)/shard_map/psum | solution.py:269
  543.4 0.9 fusion.67
  544.3 107.6 %all-reduce.8.cloned.1.call-done = (f32[576,576]{1,0:T(8,128)}, f32[576,192]{0,1:T(8,128)}, f32[576,192]{0,1:T(8,128)}, f32[576,576]{1,0:T(8,128)}, f32[576,1536...) async-done(((f32[576,576]{1,0:T(8,128)}, f32[576,192]{0,1:T(8,128)}, f32[576,192]{0,1:T(8,128)}, f32[576,576]{1,0:T(8,128)}, f32[576,1536]{1,0:T(8,128)}, ...) | async-done | bytes 14155792 | tf_op jit(solution)/shard_map/psum | solution.py:269
  651.9 2.7 copy.127
  654.7 1.8 copy.128
  656.5 0.8 copy.129
  657.3 1.1 copy.130
  658.4 1.8 copy.131
  660.2 1.5 copy-done.12
  661.7 1.8 copy.132
  663.5 1.5 copy-done.11
  664.9 1.8 copy.133
  (215 shorter events, 31.0 us)
Async XLA Ops:
  7.2 144.0 %copy-start = (bf16[1536,576]{0,1:T(8,128)(2,1)S(1)}, bf16[1536,576]{0,1:T(8,128)(2,1)}, u32[]{:S(2)}) copy-start(bf16[1536,576]{0,1:T(8,128)(2,1)} %param.32) | copy-start | bytes 5308420
  7.2 35.6 %copy-start.1 = (bf16[1,256,576]{1,2,0:T(8,128)(2,1)S(1)}, bf16[1,256,576]{1,2,0:T(8,128)(2,1)}, u32[]{:S(2)}) copy-start(bf16[1,256,576]{1,2,0:T(8,128)(2,1)} %param.21) | copy-start | bytes 884740
  7.2 35.6 %copy-start.39 = (f32[576]{0:T(1024)S(1)}, f32[576]{0:T(1024)}, u32[]{:S(2)}) copy-start(f32[576]{0:T(1024)} %param.24) | copy-start | bytes 6916
  7.2 55.1 %all-gather.4.cloned.1.call-start = ((), (), s32[]{:S(2)}) async-start(), calls=%async_computation.1 | async-start | bytes 3244032 | tf_op jit(solution)/shard_map/all_gather | solution.py:193
  8.5 6.0 copy-start.44
  8.5 35.7 %copy-start.42 = (f32[256]{0:T(256)}, f32[256]{0:T(256)S(1)}, u32[]{:S(2)}) copy-start(f32[256]{0:T(256)S(1)} %fusion.88) | copy-start | bytes 3076
  9.4 34.8 %copy-start.29 = (f32[256,32]{0,1:T(8,128)}, f32[256,32]{0,1:T(8,128)S(1)}, u32[]{:S(2)}) copy-start(f32[256,32]{0,1:T(8,128)S(1)} %get-tuple-element.501) | copy-start | bytes 98308
  9.4 34.8 %copy-start.32 = (f32[256,32]{0,1:T(8,128)}, f32[256,32]{0,1:T(8,128)S(1)}, u32[]{:S(2)}) copy-start(f32[256,32]{0,1:T(8,128)S(1)} %get-tuple-element.502) | copy-start | bytes 98308
  11.5 99.9 %all-gather.6.cloned.1.call-start = ((), (), s32[]{:S(2)}) async-start(), calls=%async_computation.2 | async-start | bytes 3244032 | tf_op jit(solution)/shard_map/all_gather | solution.py:194
  13.6 453.1 %reduce-scatter.2.cloned.1.call-start = ((), (), s32[]{:S(2)}) async-start(), calls=%async_computation.3 | async-start | bytes 6488064 | tf_op jit(solution)/shard_map/reduce_scatter | solution.py:245
  119.0 29.0 %copy-start.19 = (bf16[576,576]{1,0:T(8,128)(2,1)S(1)}, bf16[576,576]{1,0:T(8,128)(2,1)}, u32[]{:S(2)}) copy-start(bf16[576,576]{1,0:T(8,128)(2,1)} %param.28) | copy-start | bytes 1990660
  119.0 29.7 %copy-start.41 = (f32[576]{0:T(1024)S(1)}, f32[576]{0:T(1024)}, u32[]{:S(2)}) copy-start(f32[576]{0:T(1024)} %param.29) | copy-start | bytes 6916
  147.9 1.7 copy-start.10
  147.9 2.5 copy-start.9
  148.0 0.7 copy-start.21
  148.5 6.6 copy-start.3
  149.6 0.8 copy-start.7
  149.6 1.6 copy-start.24
  153.5 1.4 copy-start.14
  153.5 1.4 copy-start.17
  155.2 0.8 copy-start.5
  156.5 1.0 copy-start.26
  159.8 2.9 copy-start.27
  211.7 0.8 copy-start.30
  211.7 0.8 copy-start.33
  211.7 1.9 copy-start.2
  211.7 2.0 copy-start.40
  211.7 2.0 copy-start.43
  211.8 3.5 copy-start.6
  211.8 3.5 copy-start.22
  211.8 5.0 copy-start.8
  211.8 440.1 %all-reduce.8.cloned.1.call-start = ((), (), s32[]{:S(2)}) async-start(), calls=%async_computation.4 | async-start | bytes 29097984 | tf_op jit(solution)/shard_map/psum | solution.py:269
  211.9 5.0 copy-start.18
  215.3 4.0 copy-start.15
  216.8 4.9 copy-start.16
  216.8 4.9 copy-start.25
  221.7 246.0 %copy-start.31 = (f32[256,32]{0,1:T(8,128)S(1)}, f32[256,32]{0,1:T(8,128)}, u32[]{:S(2)}) copy-start(f32[256,32]{0,1:T(8,128)} %copy-done.29) | copy-start | bytes 98308
  221.7 246.0 %copy-start.34 = (f32[256,32]{0,1:T(8,128)S(1)}, f32[256,32]{0,1:T(8,128)}, u32[]{:S(2)}) copy-start(f32[256,32]{0,1:T(8,128)} %copy-done.32) | copy-start | bytes 98308
  467.8 3.1 copy-start.28
  470.9 1.1 copy-start.4
  472.0 2.6 copy-start.37
  472.0 3.8 copy-start.20
  472.0 4.3 copy-start.36
  472.0 4.3 copy-start.38
  472.0 71.4 %copy-start.45 = (f32[256]{0:T(256)S(1)}, f32[256]{0:T(256)}, u32[]{:S(2)}) copy-start(f32[256]{0:T(256)} %copy-done.44) | copy-start | bytes 3076
  651.9 4.6 copy-start.35
  651.9 5.4 copy-start.23
  651.9 6.5 copy-start.13
  658.4 3.3 copy-start.12
  661.7 3.3 copy-start.11
Sparse Core Ops, SparseCore 0:
  11.7 50.6 all-gather.3
  65.1 46.3 all-gather.5
  211.9 254.8 reduce-scatter.1
  475.1 176.7 all-reduce.7
where the time goes:
time: 676 us; the launch traced here: 673 us
  waiting for transfers between devices  410 us (61%)
  blocking collectives  93.4 us (14%)
  local copies, waits for them, and re-layouts  74.2 us (11%)
  matrix products  49.8 us (7%)
  loops' own time  21 us (3%)
  between operations  14.4 us (2%)
  other arithmetic  10.1 us (1%)
    reduce_scatter x1, waiting for transfers between devices, body(): lax.psum_scatter(key_terms.astype(jnp.bfloat16), 'seq', scatter_dimension...  243 us
    psum x1, waiting for transfers between devices, body(): lax.psum((grad_norm_gain, grad_query_weight, grad_key_weight, grad_value_...  108 us
    psum x1, blocking collectives, body(): lax.psum((grad_norm_gain, grad_query_weight, grad_key_weight, grad_value_...  66.7 us
    all_gather x1, waiting for transfers between devices, body(): lax.all_gather(value_flat, 'seq', axis=0, tiled=True)  41.7 us
    unnamed x100, local copies, waits for them, and re-layouts  28 us
    all_gather x1, blocking collectives, body(): lax.all_gather(seg_wire, 'seq', axis=0, tiled=True)  26.8 us
    all_gather x1, waiting for transfers between devices, body(): lax.all_gather(key_flat, 'seq', axis=0, tiled=True)  18.1 us
  transfers between devices with their start and end apart: 4, of which 4 were waited for; matrix products, arithmetic and copies ran while one was open for 4% of the time, Pallas kernels for 0%

commit v1 on v0

v1 whole, which is shorter than its diff:
```python
from functools import partial

import jax
import jax.numpy as jnp
from jax import lax
from jax.experimental import pallas as pl
from jax.experimental.pallas import tpu as pltpu
from jax.sharding import Mesh
from jax.sharding import PartitionSpec as P

D = 576
H = 9
KVH = 3
GROUP = H // KVH
HD = 64
FF = 1536
EPSILON = 1e-05
ROPE_BASE = 10000.0
LOG2E = 1.4426950408889634
MASKED = -1e30

TOK = 256
CHUNK = TOK // 2
UNITS = 32
COLS = GROUP * CHUNK
PADROWS = TOK + 16

SEQ = ("x", "z", "core")
ALL = ("dp", "x", "z", "core")
BF = jnp.bfloat16
F32 = jnp.float32
VMEM_LIMIT = 56 * 1024 * 1024

NT = (((1,), (1,)), ((), ()))
NN = (((1,), (0,)), ((), ()))
TN = (((0,), (0,)), ((), ()))


def mm(left, right, dims=NN):
    return lax.dot_general(left, right, dims, preferred_element_type=F32)


def column_info(scalars, marks_ref, kv_ref):
    lo_idx = scalars[0]
    first_len = kv_ref[0, TOK : TOK + 16, 0:128].astype(F32)[0:1, :].astype(jnp.int32)
    first_len = jnp.concatenate([first_len] * (2 * GROUP), axis=1)
    marks = jnp.concatenate([marks_ref[1 - lo_idx, 0:1, :], marks_ref[lo_idx, 0:1, :]], axis=1)
    first_key = jnp.where(marks < 0, first_len, marks)
    lane = lax.broadcasted_iota(jnp.int32, (1, 2 * COLS), 1)
    start = jnp.where(lane < COLS, scalars[2], scalars[1]) * CHUNK
    return first_key, start + lax.rem(lane, CHUNK)


def full_mask(tile, first_key, place, cols):
    keys = tile * TOK + lax.broadcasted_iota(jnp.int32, (TOK, cols), 0)
    return (keys >= first_key[:, :cols]) & (keys <= place[:, :cols])


def tiles(scalars, step):
    lo_diag = scalars[1] // 2
    hi_diag = scalars[2] // 2
    step(0, 2 * COLS, True)

    @pl.loop(1, lo_diag)
    def _(t):
        step(t, 2 * COLS, False)

    @pl.when(lo_diag > 0)
    def _():
        step(lo_diag, 2 * COLS, True)

    @pl.loop(lo_diag + 1, hi_diag)
    def _(t):
        step(t, COLS, False)

    step(hi_diag, COLS, True)


def untranspose(columns, heads_ref, out_ref, scalars):
    for part in range(2):
        index = (1 - scalars[0]) if part == 0 else scalars[0]
        for pair in range(0, H, 2):
            rows = []
            for head in range(pair, min(pair + 2, H)):
                g, j = head // GROUP, head % GROUP
                at = part * COLS + j * CHUNK
                rows.append(heads_ref[g, :, at : at + CHUNK])
            block = jnp.concatenate(rows, axis=0) if len(rows) > 1 else rows[0]
            block = jnp.transpose(block).astype(out_ref.dtype)
            out_ref[index, :, pair * HD : pair * HD + block.shape[1]] = block


def forward_kernel(scalars, marks_ref, q_ref, kv_ref, out_ref, ot_ref, lse_ref, qcat, acc, run_max, heads):
    first_key, place = column_info(scalars, marks_ref, kv_ref)
    lo_idx = scalars[0]
    qcat[:, 0:COLS, :] = q_ref[1 - lo_idx]
    qcat[:, COLS:, :] = q_ref[lo_idx]

    @pl.loop(0, KVH)
    def _(g):
        lanes = pl.ds(pl.multiple_of(g * 128, 128), 128)
        acc[...] = jnp.zeros_like(acc)
        run_max[...] = jnp.full_like(run_max, MASKED)

        def step(tile, cols, whole):
            block = kv_ref[tile, 0:TOK, lanes]
            scores = mm(block, qcat[g, 0:cols, :], NT) * LOG2E
            old_max = run_max[0:1, 0:cols]
            if whole:
                scores = jnp.where(full_mask(tile, first_key, place, cols), scores, MASKED)
                new_max = jnp.maximum(old_max, jnp.max(scores, axis=0, keepdims=True))
                shift = new_max
            else:
                seen = first_key[:, :cols] <= tile * TOK
                new_max = jnp.maximum(old_max, jnp.max(scores, axis=0, keepdims=True))
                new_max = jnp.where(seen, new_max, old_max)
                shift = jnp.where(seen, new_max, -MASKED)
            weights = jnp.exp2(scores - shift).astype(BF)
            factor = jnp.exp2(old_max - new_max)
            values = jnp.concatenate([jnp.ones((16, TOK), BF), jnp.transpose(block)[HD:, :]], axis=0)
            acc[:, 0:cols] = acc[:, 0:cols] * factor + mm(values, weights)
            run_max[0:1, 0:cols] = new_max

        tiles(scalars, step)
        total = acc[0:1, :]
        heads[g] = acc[16:, :] / total
        norm = run_max[0:1, :] + jnp.log2(total)
        for part in range(2):
            index = (1 - lo_idx) if part == 0 else lo_idx
            span = slice(part * COLS, (part + 1) * COLS)
            ot_ref[index, g] = heads[g, :, span]
            lse_ref[index, g] = jnp.broadcast_to(norm[:, span], (8, COLS))

    untranspose(None, heads, out_ref, scalars)


def backward_kernel(
    scalars, marks_ref, q_ref, do_ref, ot_ref, lse_ref, kv_ref, dq_ref, dkv_ref, qcat, docat, heads, norm, delta
):
    first_key, place = column_info(scalars, marks_ref, kv_ref)
    lo_idx = scalars[0]
    qcat[:, 0:COLS, :] = q_ref[1 - lo_idx]
    qcat[:, COLS:, :] = q_ref[lo_idx]
    docat[:, 0:COLS, :] = do_ref[1 - lo_idx]
    docat[:, COLS:, :] = do_ref[lo_idx]
    hi_diag = scalars[2] // 2

    @pl.loop(0, KVH)
    def _(g):
        lanes = pl.ds(pl.multiple_of(g * 128, 128), 128)
        heads[g] = jnp.zeros((HD, 2 * COLS), F32)
        for part in range(2):
            index = (1 - lo_idx) if part == 0 else lo_idx
            span = slice(part * COLS, (part + 1) * COLS)
            grads = jnp.transpose(docat[g, span, :])[HD:, :].astype(F32)
            delta[0:1, span] = jnp.sum(grads * ot_ref[index, g], axis=0, keepdims=True)
            norm[0:1, span] = lse_ref[index, g, 0:1, :]

        def step(tile, cols, whole):
            block = kv_ref[tile, 0:TOK, lanes]
            q_part = qcat[g, 0:cols, :]
            do_part = docat[g, 0:cols, :]
            scores = mm(block, q_part, NT) * LOG2E
            if whole:
                scores = jnp.where(full_mask(tile, first_key, place, cols), scores, MASKED)
                shift = norm[0:1, 0:cols]
            else:
                shift = jnp.where(first_key[:, :cols] <= tile * TOK, norm[0:1, 0:cols], -MASKED)
            probs = jnp.exp2(scores - shift)
            grad_probs = mm(block, do_part, NT)
            grad_scores = (probs * (grad_probs - delta[0:1, 0:cols])).astype(BF)
            grads = mm(grad_scores, q_part) + mm(probs.astype(BF), do_part)
            keys = jnp.transpose(block)[0:HD, :]
            heads[g, :, 0:cols] = heads[g, :, 0:cols] + mm(keys, grad_scores)
            grads = grads.astype(BF)
            dkv_ref[tile, 0:CHUNK, lanes] = grads[0:CHUNK]
            dkv_ref[UNITS - 1 - tile, CHUNK:, lanes] = grads[CHUNK:]

        tiles(scalars, step)

        @pl.loop(hi_diag + 1, UNITS)
        def _(t):
            zero = jnp.zeros((CHUNK, 128), BF)
            dkv_ref[t, 0:CHUNK, lanes] = zero
            dkv_ref[UNITS - 1 - t, CHUNK:, lanes] = zero

        heads[g] = heads[g] * (HD**-0.5)

    untranspose(None, heads, dq_ref, scalars)


def vmem(count):
    return [pl.BlockSpec(memory_space=pltpu.VMEM)] * count


def attend(scalars, marks, queries, keys_values):
    return pl.pallas_call(
        forward_kernel,
        out_shape=(
            jax.ShapeDtypeStruct((2, CHUNK, D), BF),
            jax.ShapeDtypeStruct((2, KVH, HD, COLS), F32),
            jax.ShapeDtypeStruct((2, KVH, 8, COLS), F32),
        ),
        in_specs=[pl.BlockSpec(memory_space=pltpu.SMEM)] + vmem(3),
        out_specs=tuple(vmem(3)),
        scratch_shapes=[
            pltpu.VMEM((KVH, 2 * COLS, 128), BF),
            pltpu.VMEM((16 + HD, 2 * COLS), F32),
            pltpu.VMEM((8, 2 * COLS), F32),
            pltpu.VMEM((KVH, HD, 2 * COLS), F32),
        ],
        compiler_params=pltpu.CompilerParams(vmem_limit_bytes=VMEM_LIMIT),
        cost_estimate=pl.CostEstimate(flops=10 * 10**9, bytes_accessed=7 * 10**6, transcendentals=10**7),
        name="attention_forward",
    )(scalars, marks, queries, keys_values)


def attend_back(scalars, marks, queries, grad_out, attended, norm, keys_values):
    return pl.pallas_call(
        backward_kernel,
        out_shape=(
            jax.ShapeDtypeStruct((2, CHUNK, D), F32),
            jax.ShapeDtypeStruct((UNITS, TOK, 2 * KVH * HD), BF),
        ),
        in_specs=[pl.BlockSpec(memory_space=pltpu.SMEM)] + vmem(6),
        out_specs=tuple(vmem(2)),
        scratch_shapes=[
            pltpu.VMEM((KVH, 2 * COLS, 128), BF),
            pltpu.VMEM((KVH, 2 * COLS, 128), BF),
            pltpu.VMEM((KVH, HD, 2 * COLS), F32),
            pltpu.VMEM((8, 2 * COLS), F32),
            pltpu.VMEM((8, 2 * COLS), F32),
        ],
        compiler_params=pltpu.CompilerParams(vmem_limit_bytes=VMEM_LIMIT),
        cost_estimate=pl.CostEstimate(flops=25 * 10**9, bytes_accessed=14 * 10**6, transcendentals=10**7),
        name="attention_backward",
    )(scalars, marks, queries, grad_out, attended, norm, keys_values)


def mirror(values):
    return lax.ppermute(values, SEQ, [(i, UNITS - 1 - i) for i in range(UNITS)])


def zigzag(values):
    return jnp.concatenate([values[:CHUNK], mirror(values[CHUNK:])], axis=0)


def turns(places):
    half = HD // 2
    freqs = ROPE_BASE ** (-2.0 * jnp.arange(half).astype(F32) / HD)
    angles = places.astype(F32)[:, None] * freqs[None, :]
    return jnp.cos(angles)[:, None, :], jnp.sin(angles)[:, None, :]


def rotate(values, turn, sign=1.0):
    cosine, sine = turn
    sine = sine * sign
    half = HD // 2
    first, second = values[..., :half], values[..., half:]
    return jnp.concatenate([first * cosine - second * sine, second * cosine + first * sine], axis=-1)


def normed(values, gain):
    return values * lax.rsqrt(jnp.mean(values * values, axis=-1, keepdims=True) + EPSILON) * gain


def swiglu(gate_value, up_value):
    return jax.nn.silu(gate_value) * up_value


def pad_heads(values, left):
    heads = values.reshape(2, CHUNK, KVH, GROUP, HD).transpose(0, 2, 3, 1, 4).reshape(2, KVH, COLS, HD)
    return jnp.pad(heads, ((0, 0), (0, 0), (0, 0), (HD, 0) if left else (0, HD)))


def body(
    tokens,
    segments,
    positions,
    norm_gain,
    query_weight,
    key_weight,
    value_weight,
    output_weight,
    mlp_gain,
    gate_weight,
    up_weight,
    down_weight,
    cotangent,
):
    unit = (lax.axis_index("x") * 4 + lax.axis_index("z")) * 2 + lax.axis_index("core")
    tokens = tokens[0]
    segments = segments[0]
    positions = positions[0]

    own = tokens.astype(F32)
    own_act = normed(own, norm_gain).astype(BF)
    own_turn = turns(positions)
    keys = rotate(mm(own_act, key_weight).reshape(TOK, KVH, HD), own_turn).astype(BF)
    values = mm(own_act, value_weight).astype(BF).reshape(TOK, KVH, HD)
    packed = jnp.concatenate([keys, values], axis=-1).reshape(TOK, 2 * KVH * HD)
    first_len = jnp.sum((segments == 0).astype(F32))
    extra = jnp.broadcast_to(first_len.astype(BF), (16, 2 * KVH * HD))
    packed = jnp.concatenate([packed, extra], axis=0)
    gathered = lax.all_gather(packed, SEQ, axis=0, tiled=False)

    third = TOK * unit + jnp.sum((segments < 2).astype(jnp.int32))
    marks = jnp.where(segments == 2, third, jnp.where(segments == 1, -1, 0))
    ints = jnp.stack([marks, positions], axis=1)
    ints = zigzag(ints)
    marks, places = ints[:, 0], ints[:, 1]
    marks = jnp.broadcast_to(jnp.tile(marks.reshape(2, 1, CHUNK), (1, 1, GROUP)), (2, 8, COLS))
    both = zigzag(jnp.concatenate([tokens, cotangent[0]], axis=1))
    inputs = both[:, :D].astype(F32)
    out_low = both[:, D:]
    chunk_a, chunk_b = 2 * unit, 2 * UNITS - 1 - 2 * unit
    lo_idx = (chunk_a > chunk_b).astype(jnp.int32)
    scalars = jnp.stack([lo_idx, jnp.minimum(chunk_a, chunk_b), jnp.maximum(chunk_a, chunk_b), 0])

    first_norm, norm_pull = jax.vjp(normed, inputs, norm_gain)
    activation = first_norm.astype(BF)
    turn = turns(places)
    queries = rotate(mm(activation, query_weight).reshape(TOK, H, HD), turn).astype(BF)
    queries = pad_heads((queries * jnp.asarray(HD**-0.5, BF)).reshape(TOK, D), False)

    attn_low, attended, norm = attend(scalars, marks, queries, gathered)
    attn_low = attn_low.reshape(TOK, D)

    middle = inputs + mm(attn_low, output_weight)
    second_norm, mlp_pull = jax.vjp(normed, middle, mlp_gain)
    activation_two = second_norm.astype(BF)
    gate_value = mm(activation_two, gate_weight)
    up_value = mm(activation_two, up_weight)
    hidden_full, swiglu_pull = jax.vjp(swiglu, gate_value, up_value)
    hidden = hidden_full.astype(BF)
    result = (middle + mm(hidden, down_weight)).astype(BF)
    grad_down = mm(hidden, out_low, TN)
    grad_hidden = mm(out_low, down_weight, NT)
    grad_gate, grad_up = swiglu_pull(grad_hidden)
    gate_low = grad_gate.astype(BF)
    up_low = grad_up.astype(BF)
    grad_gate_weight = mm(activation_two, gate_low, TN)
    grad_up_weight = mm(activation_two, up_low, TN)
    grad_act_two = mm(gate_low, gate_weight, NT) + mm(up_low, up_weight, NT)
    grad_middle_norm, grad_mlp_gain = mlp_pull(grad_act_two)
    grad_middle = out_low.astype(F32) + grad_middle_norm
    middle_low = grad_middle.astype(BF)
    grad_output_weight = mm(attn_low, middle_low, TN)
    grad_attn = pad_heads(mm(middle_low, output_weight, NT).astype(BF), True)

    early = lax.psum(
        tuple(v.astype(BF) for v in (grad_output_weight, grad_gate_weight, grad_up_weight, grad_down)), ALL
    )

    grad_query, key_terms = attend_back(scalars, marks, queries, grad_attn, attended, norm, gathered)
    shares = lax.psum_scatter(key_terms, SEQ, scatter_dimension=0, tiled=False)
    shares = shares.astype(F32).reshape(TOK, KVH, 2 * HD)
    key_low = rotate(shares[..., :HD], turn, -1.0).reshape(TOK, KVH * HD).astype(BF)
    value_low = shares[..., HD:].reshape(TOK, KVH * HD).astype(BF)
    query_low = rotate(grad_query.reshape(TOK, H, HD), turn, -1.0).reshape(TOK, D).astype(BF)
    grad_query_weight = mm(activation, query_low, TN)
    grad_key_weight = mm(activation, key_low, TN)
    grad_value_weight = mm(activation, value_low, TN)
    grad_activation = (
        mm(query_low, query_weight, NT) + mm(key_low, key_weight, NT) + mm(value_low, value_weight, NT)
    )
    grad_input_norm, grad_norm_gain = norm_pull(grad_activation)
    grad_input = (grad_middle + grad_input_norm).astype(BF)
    late = lax.psum(
        tuple(
            v.astype(BF)
            for v in (grad_query_weight, grad_key_weight, grad_value_weight, grad_norm_gain, grad_mlp_gain)
        ),
        ALL,
    )
    early = [v.astype(F32) for v in early]
    late = [v.astype(F32) for v in late]
    result = zigzag(result)
    grad_input = zigzag(grad_input)
    return (
        result[None],
        grad_input[None],
        late[3],
        late[0],
        late[1],
        late[2],
        early[0],
        late[4],
        early[1],
        early[2],
        early[3],
    )


def solution(mesh):
    inner = Mesh(mesh.devices.reshape(4, 4, 4, 2), ALL)
    row = P("dp", SEQ, None)
    flat = P("dp", SEQ)
    return jax.shard_map(
        body,
        mesh=inner,
        in_specs=(row, flat, flat) + (P(),) * 9 + (row,),
        out_specs=(row, row) + (P(),) * 9,
        check_vma=False,
    )
```

time: 676 us -> 461 us (0.68)
  waiting for transfers between devices: 410 us -> 199 us
  Pallas kernels: 0 us -> 96.6 us
  local copies, waits for them, and re-layouts: 74.2 us -> 16.8 us
  blocking collectives: 93.4 us -> 66.6 us
  matrix products: 49.8 us -> 25.9 us
  loops' own time: 21 us -> 0 us
  other arithmetic: 10.1 us -> 26.3 us
  starting transfers between devices: 0.16 us -> 13.9 us
    reduce_scatter x1, waiting for transfers between devices: 243 us -> 70 us  [body(): shares = lax.psum_scatter(key_terms, SEQ, scatter_dimension=0, tiled=False)]
    pallas_call x0 -> x2, Pallas kernels: none -> 96.6 us  [the longest x1 49.3 us: attend_back(): pl.pallas_call(backward_kernel, out_shape=(jax.ShapeDtypeStruct((2, CHUNK...]
    all_gather x2 -> x1, waiting for transfers between devices: 59.8 us -> 29.7 us  [body(): gathered = lax.all_gather(packed, SEQ, axis=0, tiled=False)]
    all_gather x1 -> x0, blocking collectives: 26.8 us -> none  [body(): lax.all_gather(seg_wire, 'seq', axis=0, tiled=True)]
    unnamed x100 -> x65, local copies, waits for them, and re-layouts: 28 us -> 1.22 us
    dot_general x28 -> x21, matrix products: 49.8 us -> 25.9 us  [mm(): return lax.dot_general(left, right, dims, preferred_element_type=F32)]
    another operation x18 -> x0, loops' own time: 21 us -> none  [the longest x1 10.9 us: fold_keys(): lax.scan(fold_step, running, split_blocks(shards, first_row, head_shape))]
    psum x1, waiting for transfers between devices: 108 us -> 88 us  [body(): lax.psum(tuple((v.astype(BF) for v in (grad_query_weight, grad_key_weight...]
  transfers between devices with their start and end apart: 4 -> 7, of which waited for: 4 -> 5; matrix products, arithmetic and copies ran while one was open for 4% -> 7% of each run, Pallas kernels for 0% -> 0%
where the time goes in v1:
time: 461 us; the launch traced here: 460 us
  waiting for transfers between devices  199 us (43%)
  Pallas kernels  96.6 us (21%)
  blocking collectives  66.6 us (14%)
  other arithmetic  26.3 us (6%)
  matrix products  25.9 us (6%)
  local copies, waits for them, and re-layouts  16.8 us (4%)
  between operations  14.9 us (3%)
  starting transfers between devices  13.9 us (3%)
    psum x1, waiting for transfers between devices, body(): lax.psum(tuple((v.astype(BF) for v in (grad_query_weight, grad_key_weight...  88 us
    reduce_scatter x1, waiting for transfers between devices, body(): shares = lax.psum_scatter(key_terms, SEQ, scatter_dimension=0, tiled=False)  70 us
    psum x1, blocking collectives, body(): lax.psum(tuple((v.astype(BF) for v in (grad_query_weight, grad_key_weight...  66.6 us
    pallas_call x1, Pallas kernels, attend_back(): pl.pallas_call(backward_kernel, out_shape=(jax.ShapeDtypeStruct((2, CHUNK...  49.3 us
    pallas_call x1, Pallas kernels, attend(): pl.pallas_call(forward_kernel, out_shape=(jax.ShapeDtypeStruct((2, CHUNK,...  47.4 us
    all_gather x1, waiting for transfers between devices, body(): gathered = lax.all_gather(packed, SEQ, axis=0, tiled=False)  29.7 us
    dot_general x21, matrix products, mm(): return lax.dot_general(left, right, dims, preferred_element_type=F32)  25.9 us
    ppermute x4, starting transfers between devices, mirror(): return lax.ppermute(values, SEQ, [(i, UNITS - 1 - i) for i in range(UNITS)])  13.6 us
  transfers between devices with their start and end apart: 7, of which 5 were waited for; matrix products, arithmetic and copies ran while one was open for 7% of the time, Pallas kernels for 0%

profile of v1, /device:TPU:1, one launch (start us, length us, event | category | flops | bytes accessed | tf_op | source)
XLA Modules:
  0.0 460.2 jit_solution(10122701473401008434)
XLA Ops:
  7.3 1.4 fusion.33
  9.3 0.7 fusion.32
  10.0 0.7 pad_add_fusion.1
  10.7 7.3 %collective-permute-start.1 = (s32[128,2]{0,1:T(2,128)S(1)}, s32[128,2]{0,1:T(2,128)S(1)}, u32[]{:S(2)}, u32[]{:S(2)}) collective-permute-start(s32[128,2]{0,1:T(2,128)S(1)} %get-tuple-element.55), channel_id=1, source_target_pairs={{0,31},{1,30},{2,29},{3,28},{4,27},{5,26},{6,25},{7,24},{8,23},{9,... | collective-permute-start | bytes 3080 | tf_op jit(solution)/shard_map/ppermute | solution.py:241
  18.1 1.3 fusion.34
  19.3 1.1 fusion.9
  20.4 1.5 convolution_convert_fusion.8
  21.9 1.4 fusion.18
  23.4 0.9 broadcast_multiply_fusion
  24.5 1.4 concatenate.48.clone
  26.0 1.1 collective-permute-start
  27.1 0.6 pad_add_fusion.2.scalars
  27.7 10.3 %collective-permute-done = bf16[128,1152]{0,1:T(8,128)(2,1)S(1)} collective-permute-done((bf16[128,1152]{0,1:T(8,128)(2,1)S(1)}, bf16[128,1152]{0,1:T(8,128)(2,1)S(1)}, u32[]{:S(2)}, u32[]{:S(2)}) %collective-permute-start) | collective-permute-done | bytes 294944 | tf_op jit(solution)/shard_map/ppermute | solution.py:241
  38.1 1.7 fusion.43
  39.8 0.9 subtract_convert_fusion.1
  40.8 0.4 fusion.23
  41.2 1.1 copy.38
  42.3 0.9 pad.9.q_ref
  43.2 29.7 %all-gather.3.cloned.1.call-done = bf16[8704,384]{1,0:T(8,128)(2,1)} async-done(((bf16[272,384]{1,0:T(8,128)(2,1)}), bf16[8704,384]{1,0:T(8,128)(2,1)}) %all-gather.3.cloned.1.call-update) | async-done | bytes 6684688 | tf_op jit(solution)/shard_map/all_gather | solution.py:305
  72.9 0.6 broadcast_in_dim.25.marks_ref
  73.5 47.4 %attention_forward.1 = (bf16[2,128,576]{2,1,0:T(8,128)(2,1)}, f32[2,3,64,384]{3,2,1,0:T(8,128)}, f32[2,3,8,384]{3,2,1,0:T(8,128)}) custom-call(s32[4]{0:T(128)} %pad_add_fusion.2.scalars, s32[2,8,384]{2,1,0:T(8,128)} %broadcast_in_dim.25.marks_ref, bf16[2,3,384,128]{3,2,1,0:T(8,128)(2,1)} %pad.9.q_ref, bf16[32,272,384]{2,1,0:T(8,128)(2,1)} %bitcast.110), custom_call_target="tpu_custom_call" | custom-call | flops 10000000000 | bytes 7000000 | tf_op jit(solution)/shard_map/attention_forward/pallas_call | solution.py:197
  120.9 1.6 multiply_reduce_fusion.2
  122.7 0.8 fusion.49
  123.5 0.7 copy-done.1
  124.2 0.8 fusion.48
  125.0 2.3 multiply_convert_fusion
  127.3 0.7 fusion.50
  128.0 0.8 multiply_reduce_fusion
  129.2 1.1 convolution_convert_fusion.5
  130.3 1.8 reshape.307
  132.1 2.0 copy.40
  134.1 2.1 pad.10.do_ref
  136.2 49.3 %attention_backward.1 = (f32[2,128,576]{2,1,0:T(8,128)}, bf16[32,256,384]{2,1,0:T(8,128)(2,1)}) custom-call(s32[4]{0:T(128)} %pad_add_fusion.2.scalars, s32[2,8,384]{2,1,0:T(8,128)} %broadcast_in_dim.25.marks_ref, bf16[2,3,384,128]{3,2,1,0:T(8,128)(2,1)} %pad.9.q_ref, bf16[2,3,384,128]{3,2,1,0:T(8,128)(2,1)} %pad.10.do_ref, ...), custom_call_target="tpu_custom_call" | custom-call | flops 24999999488 | bytes 14000000 | tf_op jit(solution)/shard_map/attention_backward/pallas_call | solution.py:219
  185.8 2.1 copy.41
  187.9 2.3 reshape.309
  190.3 1.2 subtract_convert_fusion
  191.5 1.3 convolution_convert_fusion.4
  192.8 1.3 convolution_convert_fusion.3
  194.2 1.8 convolution_convert_fusion
  196.0 1.8 convolution_convert_fusion.1
  197.8 1.8 convolution_convert_fusion.2
  199.7 70.0 %reduce-scatter.2.cloned.1.call-done = bf16[1,256,384]{2,1,0:T(8,128)(2,1)} async-done(((bf16[32,256,384]{2,1,0:T(8,128)(2,1)}), bf16[1,256,384]{2,1,0:T(8,128)(2,1)}) %reduce-scatter.2.cloned.1.call-update) | async-done | bytes 196624 | tf_op jit(solution)/shard_map/reduce_scatter | solution.py:356
  269.6 1.1 copy.42
  270.7 0.8 subtract_convert_fusion.2
  271.6 1.0 convolution_convert_fusion.7
  272.6 1.0 convolution_convert_fusion.6
  273.7 1.9 fusion.4
  275.6 4.7 %collective-permute-start.2 = (bf16[128,576]{0,1:T(8,128)(2,1)S(1)}, bf16[128,576]{0,1:T(8,128)(2,1)S(1)}, u32[]{:S(2)}, u32[]{:S(2)}) collective-permute-start(bf16[128,576]{0,1:T(8,128)(2,1)S(1)} %get-tuple-element.50), channel_id=1, source_target_pairs={{0,31},{1,30},{2,29},{3,28},{4,27},{5,26},{6,25},{7,24},{8,23},{9,... | collective-permute-start | bytes 442376 | tf_op jit(solution)/shard_map/ppermute | solution.py:241
  281.1 0.5 fusion.8
  281.8 0.5 collective-permute-start.3
  282.4 1.2 collective-permute-done.2
  283.6 0.7 maximum_bitcast_fusion
  284.3 66.6 %all-reduce.3 = (bf16[576]{0:T(1024)(128)(2,1)S(1)}, bf16[576]{0:T(1024)(128)(2,1)S(1)}) all-reduce(bf16[576]{0:T(1024)(128)(2,1)S(1)} %get-tuple-element.23, bf16[576]{0:T(1024)(128)(2,1)S(1)} %get-tuple-element.21), channel_id=1, replica_groups=mesh['dp'=4,'x'=4,'z'=4,'core'=2] {'dp','x','z','core'}, use_global_device_ids=true, to_apply=%region_9.10 | all-reduce | flops 1152 | bytes 4608 | tf_op jit(solution)/shard_map/psum | solution.py:369
  350.9 0.6 convert_element_type.196
  351.5 0.6 convert_element_type.206
  352.1 0.7 maximum_bitcast_fusion.1
  352.9 88.0 %all-reduce.7.cloned.1.call-done = (bf16[576,576]{1,0:T(8,128)(2,1)}, bf16[576,192]{0,1:T(8,128)(2,1)}, bf16[576,192]{0,1:T(8,128)(2,1)}, bf16[576,576]{1,0:T(8,...) async-done(((bf16[576,576]{1,0:T(8,128)(2,1)}, bf16[576,192]{0,1:T(8,128)(2,1)}, bf16[576,192]{0,1:T(8,128)(2,1)}, ...) | async-done | bytes 7077904 | tf_op jit(solution)/shard_map/psum | solution.py:369
  440.9 1.9 convert_element_type.200
  442.7 1.8 convert_element_type.202
  444.5 1.2 convert_element_type.198
  445.7 1.2 convert_element_type.204
  446.9 2.3 convert_element_type.208
  449.2 2.3 convert_element_type.210
  451.4 2.3 convert_element_type.212
  (97 shorter events, 2.6 us)
Async XLA Ops:
  7.2 117.8 %copy-start = (bf16[1536,576]{0,1:T(8,128)(2,1)S(1)}, bf16[1536,576]{0,1:T(8,128)(2,1)}, u32[]{:S(2)}) copy-start(bf16[1536,576]{0,1:T(8,128)(2,1)} %param.24) | copy-start | bytes 5308420
  7.2 16.2 %copy-start.30 = (s32[1,256]{1,0:T(1,128)S(1)}, s32[1,256]{1,0:T(1,128)}, u32[]{:S(2)}) copy-start(s32[1,256]{1,0:T(1,128)} %param.15) | copy-start | bytes 3076
  7.2 65.7 %all-gather.3.cloned.1.call-start = ((), (), s32[]{:S(2)}) async-start(), calls=%async_computation.2 | async-start | bytes 6893568 | tf_op jit(solution)/shard_map/all_gather | solution.py:305
  10.7 12.7 %collective-permute-start.1 = (s32[128,2]{0,1:T(2,128)S(1)}, s32[128,2]{0,1:T(2,128)S(1)}, u32[]{:S(2)}, u32[]{:S(2)}) collective-permute-start(s32[128,2]{0,1:T(2,128)S(1)} %get-tuple-element.55), channel_id=1, source_target_pairs={{0,31},{1,30},{2,29},{3,28},{4,27},{5,26},{6,25},{7,24},{8,23},{9,... | collective-permute-start | bytes 3080 | tf_op jit(solution)/shard_map/ppermute | solution.py:241
  20.4 5.5 %copy-start.22 = (bf16[1,256,576]{1,2,0:T(8,128)(2,1)S(1)}, bf16[1,256,576]{1,2,0:T(8,128)(2,1)}, u32[]{:S(2)}) copy-start(bf16[1,256,576]{1,2,0:T(8,128)(2,1)} %param.13) | copy-start | bytes 884740
  20.4 5.5 %copy-start.25 = (bf16[1,256,576]{1,2,0:T(8,128)(2,1)S(1)}, bf16[1,256,576]{1,2,0:T(8,128)(2,1)}, u32[]{:S(2)}) copy-start(bf16[1,256,576]{1,2,0:T(8,128)(2,1)} %param.25) | copy-start | bytes 884740
  24.3 13.8 %copy-start.29 = (f32[576]{0:T(1024)S(1)}, f32[576]{0:T(1024)}, u32[]{:S(2)}) copy-start(f32[576]{0:T(1024)} %param.16) | copy-start | bytes 6916
  25.9 243.8 %reduce-scatter.2.cloned.1.call-start = ((), (), s32[]{:S(2)}) async-start(), calls=%async_computation.1 | async-start | bytes 6488064 | tf_op jit(solution)/shard_map/reduce_scatter | solution.py:356
  26.0 99.0 %copy-start.3 = (bf16[128,1152]{0,1:T(8,128)(2,1)}, bf16[128,1152]{0,1:T(8,128)(2,1)S(1)}, u32[]{:S(2)}) copy-start(bf16[128,1152]{0,1:T(8,128)(2,1)S(1)} %get-tuple-element.43) | copy-start | bytes 884740
  26.0 12.0 %collective-permute-start = (bf16[128,1152]{0,1:T(8,128)(2,1)S(1)}, bf16[128,1152]{0,1:T(8,128)(2,1)S(1)}, u32[]{:S(2)}, u32[]{:S(2)}) collective-permute-start(bf16[128,1152]{0,1:T(8,128)(2,1)S(1)} %get-tuple-element.44), channel_id=1, source_target_pairs={{0,31},{1,30},{2,29},{3,28},{4,27},{5,26},{6,25},{7,24},{8,23},{9,... | collective-permute-start | bytes 884744 | tf_op jit(solution)/shard_map/ppermute | solution.py:241
  38.0 87.0 %copy-start.15 = (bf16[128,1152]{0,1:T(8,128)(2,1)}, bf16[128,1152]{0,1:T(8,128)(2,1)S(1)}, u32[]{:S(2)}) copy-start(bf16[128,1152]{0,1:T(8,128)(2,1)S(1)} %collective-permute-done) | copy-start | bytes 884740
  73.5 47.4 %copy-start.11 = (bf16[576,576]{1,0:T(8,128)(2,1)S(1)}, bf16[576,576]{1,0:T(8,128)(2,1)}, u32[]{:S(2)}) copy-start(bf16[576,576]{1,0:T(8,128)(2,1)} %param.20) | copy-start | bytes 1990660
  120.9 1.6 copy-start.28
  120.9 1.8 copy-start.2
  122.7 1.5 copy-start.1
  127.3 1.5 copy-start.7
  127.3 1.5 copy-start.9
  128.0 1.0 copy-start.4
  128.0 1.0 copy-start.16
  185.5 255.3 %all-reduce.7.cloned.1.call-start = ((), (), s32[]{:S(2)}) async-start(), calls=%async_computation.3 | async-start | bytes 14548992 | tf_op jit(solution)/shard_map/psum | solution.py:369
  190.3 2.6 copy-start.21
  191.4 2.7 copy-start.5
  191.4 2.7 copy-start.6
  191.5 2.7 copy-start.17
  191.5 1.3 copy-start.13
  194.1 1.9 copy-start.10
  196.0 1.8 copy-start.8
  273.7 6.7 %copy-start.27 = (bf16[576,192]{0,1:T(8,128)(2,1)S(1)}, bf16[576,192]{0,1:T(8,128)(2,1)}, u32[]{:S(2)}) copy-start(bf16[576,192]{0,1:T(8,128)(2,1)} %param.18) | copy-start | bytes 663556
  273.7 7.0 %copy-start.12 = (bf16[576,576]{1,0:T(8,128)(2,1)S(1)}, bf16[576,576]{1,0:T(8,128)(2,1)}, u32[]{:S(2)}) copy-start(bf16[576,576]{1,0:T(8,128)(2,1)} %param.17) | copy-start | bytes 1990660
  273.7 7.0 %copy-start.14 = (bf16[256,9,64]{0,2,1:T(8,128)(2,1)S(1)}, bf16[256,9,64]{0,2,1:T(8,128)(2,1)}, u32[]{:S(2)}) copy-start(bf16[256,9,64]{0,2,1:T(8,128)(2,1)} %copy-done.13) | copy-start | bytes 884740
  275.6 5.5 %copy-start.26 = (bf16[576,192]{0,1:T(8,128)(2,1)S(1)}, bf16[576,192]{0,1:T(8,128)(2,1)}, u32[]{:S(2)}) copy-start(bf16[576,192]{0,1:T(8,128)(2,1)} %param.19) | copy-start | bytes 663556
  275.6 8.0 %collective-permute-start.2 = (bf16[128,576]{0,1:T(8,128)(2,1)S(1)}, bf16[128,576]{0,1:T(8,128)(2,1)S(1)}, u32[]{:S(2)}, u32[]{:S(2)}) collective-permute-start(bf16[128,576]{0,1:T(8,128)(2,1)S(1)} %get-tuple-element.50), channel_id=1, source_target_pairs={{0,31},{1,30},{2,29},{3,28},{4,27},{5,26},{6,25},{7,24},{8,23},{9,... | collective-permute-start | bytes 442376 | tf_op jit(solution)/shard_map/ppermute | solution.py:241
  281.8 70.3 %collective-permute-start.3 = (bf16[128,576]{0,1:T(8,128)(2,1)S(1)}, bf16[128,576]{0,1:T(8,128)(2,1)S(1)}, u32[]{:S(2)}, u32[]{:S(2)}) collective-permute-start(bf16[128,576]{0,1:T(8,128)(2,1)S(1)} %get-tuple-element.48), channel_id=1, source_target_pairs={{0,31},{1,30},{2,29},{3,28},{4,27},{5,26},{6,25},{7,24},{8,23},{9,... | collective-permute-start | bytes 442376 | tf_op jit(solution)/shard_map/ppermute | solution.py:241
  440.8 3.6 copy-start.24
  440.8 4.8 %copy-start.23 = (bf16[576,576]{1,0:T(8,128)(2,1)S(1)}, bf16[576,576]{1,0:T(8,128)(2,1)}, u32[]{:S(2)}) copy-start(bf16[576,576]{1,0:T(8,128)(2,1)} %get-tuple-element.30) | copy-start | bytes 1990660
  444.5 2.4 copy-start.20
  446.9 2.3 copy-start.19
  449.2 2.3 copy-start.18
Sparse Core Ops, SparseCore 0:
  26.0 46.8 all-gather.2
  185.7 83.9 reduce-scatter.1
  278.2 162.6 all-reduce.6

commit v2 on v1

v2 whole, which is shorter than its diff:
```python
from functools import partial

import jax
import jax.numpy as jnp
from jax import lax
from jax.experimental import pallas as pl
from jax.experimental.pallas import tpu as pltpu
from jax.sharding import Mesh
from jax.sharding import PartitionSpec as P

D = 576
H = 9
KVH = 3
GROUP = H // KVH
HD = 64
HALF = HD // 2
FF = 1536
KVW = KVH * HD
EPSILON = 1e-05
ROPE_BASE = 10000.0
LOG2E = 1.4426950408889634
MASKED = -1e30
SCALE = HD**-0.5

TOK = 256
CHUNK = TOK // 2
UNITS = 32
COLS = GROUP * CHUNK
PADROWS = TOK + 16
LATE = 1024
FF_BLOCK = 512

SEQ = ("x", "z", "core")
ALL = ("dp", "x", "z", "core")
BF = jnp.bfloat16
F32 = jnp.float32

NT = (((1,), (1,)), ((), ()))
NN = (((1,), (0,)), ((), ()))
TN = (((0,), (0,)), ((), ()))


def mm(left, right, dims=NN):
    return lax.dot_general(left, right, dims, preferred_element_type=F32)


def vmem(count):
    return [pl.BlockSpec(memory_space=pltpu.VMEM)] * count


def smem():
    return pl.BlockSpec(memory_space=pltpu.SMEM)


def call(kernel, name, out_shape, scalars, arrays, scratch=(), flops=10**8, moved=10**6):
    outs = out_shape if isinstance(out_shape, (tuple, list)) else (out_shape,)
    given = ([] if scalars is None else [scalars]) + list(arrays)
    specs = ([] if scalars is None else [smem()]) + vmem(len(arrays))
    return pl.pallas_call(
        kernel,
        out_shape=out_shape,
        in_specs=specs,
        out_specs=tuple(vmem(len(outs))) if isinstance(out_shape, (tuple, list)) else vmem(1)[0],
        scratch_shapes=list(scratch),
        compiler_params=pltpu.CompilerParams(vmem_limit_bytes=56 * 1024 * 1024),
        cost_estimate=pl.CostEstimate(flops=flops, bytes_accessed=moved, transcendentals=0),
        name=name,
    )(*given)


def shape(*dims, dtype=BF):
    return jax.ShapeDtypeStruct(dims, dtype)


def column_info(scalars, marks_ref, kv_ref):
    lo_idx = scalars[0]
    first_len = kv_ref[0, TOK : TOK + 16, 0:128].astype(F32)[0:1, :].astype(jnp.int32)
    first_len = jnp.concatenate([first_len] * (2 * GROUP), axis=1)
    hi, lo = marks_ref[1 - lo_idx, 0:1, :], marks_ref[lo_idx, 0:1, :]
    marks = jnp.concatenate([hi] * GROUP + [lo] * GROUP, axis=1)
    first_key = jnp.where(marks < 0, first_len, marks)
    lane = lax.broadcasted_iota(jnp.int32, (1, 2 * COLS), 1)
    start = jnp.where(lane < COLS, scalars[2], scalars[1]) * CHUNK
    return first_key, start + lax.rem(lane, CHUNK)


def full_mask(tile, first_key, place, rows, cols):
    keys = tile * TOK + lax.broadcasted_iota(jnp.int32, (rows, cols), 0)
    return (keys >= first_key[:, :cols]) & (keys <= place[:, :cols])


def tiles(scalars, step):
    lo_diag = scalars[1] // 2
    hi_diag = scalars[2] // 2

    @pl.loop(0, jnp.where(lo_diag > 0, 2, 1))
    def _(j):
        step(j * lo_diag, 1, 2 * COLS, True)

    @pl.loop(1, lo_diag)
    def _(t):
        step(t, 1, 2 * COLS, False)

    @pl.loop(0, (hi_diag - lo_diag - 1) // 2)
    def _(j):
        step(lo_diag + 1 + 2 * j, 2, COLS, False)

    step(hi_diag, 1, COLS, True)


def gather_columns(cat_ref, source_ref, scalars, first_row):
    cat_ref[...] = jnp.zeros_like(cat_ref)
    lo_idx = scalars[0]
    for part in range(2):
        index = (1 - lo_idx) if part == 0 else lo_idx
        lanes = pl.ds(pl.multiple_of(index * CHUNK, CHUNK), CHUNK)
        for head in range(H):
            at = part * COLS + (head % GROUP) * CHUNK
            block = source_ref[head * HD : (head + 1) * HD, lanes]
            cat_ref[head // GROUP, first_row : first_row + HD, at : at + CHUNK] = block


def scatter_columns(out_ref, values, group, scalars):
    lo_idx = scalars[0]
    for part in range(2):
        index = (1 - lo_idx) if part == 0 else lo_idx
        lanes = pl.ds(pl.multiple_of(index * CHUNK, CHUNK), CHUNK)
        for j in range(GROUP):
            head = group * GROUP + j
            at = part * COLS + j * CHUNK
            out_ref[head * HD : (head + 1) * HD, lanes] = values[:, at : at + CHUNK]


def forward_kernel(scalars, marks_ref, q_ref, kv_ref, out_ref, lse_ref, qcat, acc, run_max):
    first_key, place = column_info(scalars, marks_ref, kv_ref)
    gather_columns(qcat, q_ref, scalars, 0)
    acc[...] = jnp.zeros_like(acc)
    run_max[...] = jnp.full_like(run_max, MASKED)

    def step(tile, count, cols, whole):
        rows = count * TOK
        if whole:
            allowed = full_mask(tile, first_key, place, rows, cols)
        else:
            seen = first_key[:, :cols] <= tile * TOK
        for g in range(KVH):
            lanes = slice(g * 128, (g + 1) * 128)
            block = kv_ref[pl.ds(tile, count), 0:TOK, lanes].reshape(rows, 128)
            scores = mm(block, qcat[g, :, 0:cols]) * LOG2E
            old_max = run_max[g, 0:1, 0:cols]
            if whole:
                scores = jnp.where(allowed, scores, MASKED)
                new_max = jnp.maximum(old_max, jnp.max(scores, axis=0, keepdims=True))
                shift = new_max
            else:
                new_max = jnp.maximum(old_max, jnp.max(scores, axis=0, keepdims=True))
                new_max = jnp.where(seen, new_max, old_max)
                shift = jnp.where(seen, new_max, -MASKED)
            weights = jnp.exp2(scores - shift).astype(BF)
            factor = jnp.exp2(old_max - new_max)
            values = jnp.concatenate([jnp.ones((16, rows), BF), jnp.transpose(block)[HD:, :]], axis=0)
            acc[g, :, 0:cols] = acc[g, :, 0:cols] * factor + mm(values, weights)
            run_max[g, 0:1, 0:cols] = new_max

    tiles(scalars, step)
    for g in range(KVH):
        total = acc[g, 0:1, :]
        scatter_columns(out_ref, acc[g, 16:, :] / total, g, scalars)
        lse_ref[g] = jnp.broadcast_to(run_max[g, 0:1, :] + jnp.log2(total), (8, 2 * COLS))


def backward_kernel(
    scalars, marks_ref, q_ref, do_ref, out_ref, lse_ref, kv_ref, dq_ref, mine_ref, other_ref, qcat, docat, acc, delta
):
    first_key, place = column_info(scalars, marks_ref, kv_ref)
    gather_columns(qcat, q_ref, scalars, 0)
    gather_columns(docat, do_ref, scalars, HD)
    lo_idx = scalars[0]
    hi_diag = scalars[2] // 2
    my_x, my_z, my_c = scalars[3], scalars[4], scalars[5]
    acc[...] = jnp.zeros_like(acc)
    for part in range(2):
        index = (1 - lo_idx) if part == 0 else lo_idx
        lanes = pl.ds(pl.multiple_of(index * CHUNK, CHUNK), CHUNK)
        for head in range(H):
            rows = slice(head * HD, (head + 1) * HD)
            at = part * COLS + (head % GROUP) * CHUNK
            terms = do_ref[rows, lanes].astype(F32) * out_ref[rows, lanes]
            delta[head // GROUP, 0:1, at : at + CHUNK] = jnp.sum(terms, axis=0, keepdims=True)

    def store(tile, lanes, grads):
        mirrored = UNITS - 1 - tile
        kx, kz = (tile // 8 - my_x) & 3, ((tile // 2) % 4 - my_z) & 3
        mx, mz = (mirrored // 8 - my_x) & 3, ((mirrored // 2) % 4 - my_z) & 3
        same = lax.rem(tile, 2) == my_c

        @pl.when(same)
        def _():
            mine_ref[0, kx, kz, :, lanes] = grads[0:CHUNK]
            other_ref[1, mz, mx, :, lanes] = grads[CHUNK:TOK]

        @pl.when(jnp.logical_not(same))
        def _():
            other_ref[0, kx, kz, :, lanes] = grads[0:CHUNK]
            mine_ref[1, mz, mx, :, lanes] = grads[CHUNK:TOK]

    def step(tile, count, cols, whole):
        rows = count * TOK
        if whole:
            allowed = full_mask(tile, first_key, place, rows, cols)
        else:
            seen = first_key[:, :cols] <= tile * TOK
        all_grads = []
        for g in range(KVH):
            lanes = slice(g * 128, (g + 1) * 128)
            block = kv_ref[pl.ds(tile, count), 0:TOK, lanes].reshape(rows, 128)
            q_part = qcat[g, :, 0:cols]
            do_part = docat[g, :, 0:cols]
            scores = mm(block, q_part) * LOG2E
            shift = lse_ref[g, 0:1, 0:cols]
            if whole:
                scores = jnp.where(allowed, scores, MASKED)
            else:
                shift = jnp.where(seen, shift, -MASKED)
            probs = jnp.exp2(scores - shift)
            grad_probs = mm(block, do_part)
            grad_scores = (probs * (grad_probs - delta[g, 0:1, 0:cols])).astype(BF)
            grads = mm(grad_scores, q_part, NT) + mm(probs.astype(BF), do_part, NT)
            keys = jnp.transpose(block)[0:HD, :]
            acc[g, :, 0:cols] = acc[g, :, 0:cols] + mm(keys, grad_scores)
            all_grads.append(grads.astype(BF))
        grads = jnp.concatenate(all_grads, axis=1)
        for i in range(count):
            store(tile + i, slice(None), grads[i * TOK : (i + 1) * TOK])

    tiles(scalars, step)

    @pl.loop(hi_diag + 1, UNITS)
    def _(t):
        store(t, slice(None), jnp.zeros((TOK, 2 * KVW), BF))

    for g in range(KVH):
        scatter_columns(dq_ref, acc[g] * SCALE, g, scalars)


def attend(scalars, marks, queries, keys_values):
    return call(
        forward_kernel,
        "attention_forward",
        (shape(D, TOK, dtype=F32), shape(KVH, 8, 2 * COLS, dtype=F32)),
        scalars,
        (marks, queries, keys_values),
        (
            pltpu.VMEM((KVH, 128, 2 * COLS), BF),
            pltpu.VMEM((KVH, 16 + HD, 2 * COLS), F32),
            pltpu.VMEM((KVH, 8, 2 * COLS), F32),
        ),
        flops=20 * 10**9,
        moved=7 * 10**6,
    )


def attend_back(scalars, marks, queries, grad_out, attended, norm, keys_values):
    blocks = shape(2, 4, 4, CHUNK, 2 * KVW)
    return call(
        backward_kernel,
        "attention_backward",
        (shape(D, TOK, dtype=F32), blocks, blocks),
        scalars,
        (marks, queries, grad_out, attended, norm, keys_values),
        (
            pltpu.VMEM((KVH, 128, 2 * COLS), BF),
            pltpu.VMEM((KVH, 128, 2 * COLS), BF),
            pltpu.VMEM((KVH, HD, 2 * COLS), F32),
            pltpu.VMEM((KVH, 8, 2 * COLS), F32),
        ),
        flops=40 * 10**9,
        moved=14 * 10**6,
    )


def inverse_rms(values):
    return lax.rsqrt(jnp.mean(values * values, axis=0, keepdims=True) + EPSILON)


def rotated(values, turn, sign):
    cosine, sine = turn[0:HALF], turn[HALF:] * sign
    first, second = values[:HALF], values[HALF:]
    return jnp.concatenate([first * cosine - second * sine, second * cosine + first * sine], axis=0)


def row_sums(values):
    ones = jnp.ones((16, TOK), BF)
    high = values.astype(BF)
    low = (values - high.astype(F32)).astype(BF)
    return mm(ones, high, NT) + mm(ones, low, NT)


def keys_kernel(x_ref, gain_ref, turn_ref, key_ref, value_ref, seg_ref, out_ref):
    x = x_ref[...].astype(F32)
    act = (x * inverse_rms(x) * gain_ref[...]).astype(BF)
    keys = mm(key_ref[...], act)
    values = mm(value_ref[...], act)
    turn = turn_ref[...]
    for g in range(KVH):
        rows = slice(g * HD, (g + 1) * HD)
        block = jnp.concatenate([rotated(keys[rows], turn, 1.0), values[rows]], axis=0)
        out_ref[0:TOK, g * 128 : (g + 1) * 128] = jnp.transpose(block).astype(BF)
    first_len = jnp.sum((seg_ref[...] == 0).astype(F32), axis=1, keepdims=True)
    out_ref[TOK:, :] = jnp.broadcast_to(first_len, (16, 2 * KVW)).astype(BF)


def queries_kernel(x_ref, gain_ref, turn_ref, weight_ref, act_ref, out_ref):
    x = x_ref[...].astype(F32)
    act = (x * inverse_rms(x) * gain_ref[...]).astype(BF)
    act_ref[...] = act
    queries = mm(weight_ref[...], act, TN)
    turn = turn_ref[...]
    for head in range(H):
        rows = slice(head * HD, (head + 1) * HD)
        low = rotated(queries[rows], turn, 1.0).astype(BF)
        out_ref[rows, :] = low * jnp.asarray(SCALE, BF)


def mlp_kernel(
    x_ref, c_ref, attn_ref, gain_ref, out_weight, gate_ref, up_ref, down_ref,
    result_ref, dmid_ref, dattn_ref, gout_ref, ggate_ref, gup_ref, gdown_ref, ggain_ref,
    mid, act, act_cols, c_cols, result, dact,
):
    block = pl.program_id(0)

    @pl.when(block == 0)
    def _():
        low = attn_ref[...].astype(BF)
        middle = x_ref[...].astype(F32) + mm(out_weight[...], low, TN)
        mid[...] = middle
        normal = (middle * inverse_rms(middle) * gain_ref[...]).astype(BF)
        act_cols[...] = normal
        act[...] = jnp.transpose(normal)
        c_cols[...] = jnp.transpose(c_ref[...])
        result[...] = jnp.zeros_like(result)
        dact[...] = jnp.zeros_like(dact)

    gate = mm(act[...], gate_ref[...])
    up = mm(act[...], up_ref[...])
    sigmoid = 1.0 / (1.0 + jnp.exp(-gate))
    silu = gate * sigmoid
    hidden = (silu * up).astype(BF)
    dhidden = mm(c_cols[...], down_ref[...])
    dup = (dhidden * silu).astype(BF)
    dgate = (dhidden * up * (sigmoid * (1.0 + gate * (1.0 - sigmoid)))).astype(BF)
    result[...] += mm(down_ref[...], hidden, NT)
    gdown_ref[...] = mm(c_ref[...], hidden).astype(BF)
    ggate_ref[...] = mm(act_cols[...], dgate).astype(BF)
    gup_ref[...] = mm(act_cols[...], dup).astype(BF)
    dact[...] += mm(gate_ref[...], dgate, NT) + mm(up_ref[...], dup, NT)

    @pl.when(block == FF // FF_BLOCK - 1)
    def _():
        middle = mid[...]
        gain = gain_ref[...]
        rms = inverse_rms(middle)
        grads = dact[...]
        result_ref[...] = (middle + result[...]).astype(BF)
        ggain_ref[...] = row_sums(grads * middle * rms)
        pulled = grads * gain
        inner = jnp.mean(pulled * middle, axis=0, keepdims=True)
        dmid = c_ref[...].astype(F32) + (pulled * rms - middle * (rms * rms * rms * inner))
        dmid_ref[...] = dmid
        low = dmid.astype(BF)
        gout_ref[...] = mm(attn_ref[...].astype(BF), low, NT).astype(BF)
        dattn_ref[...] = mm(out_weight[...], low).astype(BF)


def feed_forward(x, cotangent, attended, gain, out_weight, gate_weight, up_weight, down_weight):
    whole = lambda *dims: pl.BlockSpec(dims, lambda f: (0,) * len(dims))
    part = pl.BlockSpec((D, FF_BLOCK), lambda f: (0, f))
    return pl.pallas_call(
        mlp_kernel,
        grid=(FF // FF_BLOCK,),
        out_shape=(
            shape(D, TOK), shape(D, TOK, dtype=F32), shape(D, TOK), shape(D, D),
            shape(D, FF), shape(D, FF), shape(D, FF), shape(16, D, dtype=F32),
        ),
        in_specs=[whole(D, TOK), whole(D, TOK), whole(D, TOK), whole(D, 1), whole(D, D), part, part, part],
        out_specs=(whole(D, TOK), whole(D, TOK), whole(D, TOK), whole(D, D), part, part, part, whole(16, D)),
        scratch_shapes=[
            pltpu.VMEM((D, TOK), F32), pltpu.VMEM((TOK, D), BF), pltpu.VMEM((D, TOK), BF),
            pltpu.VMEM((TOK, D), BF), pltpu.VMEM((D, TOK), F32), pltpu.VMEM((D, TOK), F32),
        ],
        compiler_params=pltpu.CompilerParams(vmem_limit_bytes=56 * 1024 * 1024),
        cost_estimate=pl.CostEstimate(flops=5 * 10**9, bytes_accessed=14 * 10**6, transcendentals=10**6),
        name="feed_forward",
    )(x, cotangent, attended, gain, out_weight, gate_weight, up_weight, down_weight)


def query_tail_kernel(dq_ref, turn_ref, act_ref, weight_ref, gquery_ref, dact_ref):
    turn = turn_ref[...]
    heads = [rotated(dq_ref[h * HD : (h + 1) * HD, :], turn, -1.0).astype(BF) for h in range(H)]
    low = jnp.concatenate(heads, axis=0)
    gquery_ref[...] = mm(act_ref[...], low, NT).astype(BF)
    dact_ref[...] = mm(weight_ref[...], low)


def tail_kernel(
    scalars, a0, a1, a2, a3, b0, b1, b2, b3, turn_ref, act_ref, x_ref, gain_ref, key_ref, value_ref, dact_ref, dmid_ref,
    gquery_ref, ggain_ref, grad_ref, mine_ref, other_ref, late,
):
    turn = turn_ref[...]
    summed = []
    for parts in ((a0, a1, a2, a3), (b0, b1, b2, b3)):
        total = parts[0][...].astype(F32)
        for part in parts[1:]:
            total = total + part[...].astype(F32)
        summed.append(total)
    keys, values = [], []
    for g in range(KVH):
        columns = [jnp.transpose(t[:, g * 128 : (g + 1) * 128]) for t in summed]
        columns = jnp.concatenate(columns, axis=1)
        keys.append(rotated(columns[:HD], turn, -1.0).astype(BF))
        values.append(columns[HD:].astype(BF))
    keys, values = jnp.concatenate(keys, axis=0), jnp.concatenate(values, axis=0)
    act = act_ref[...]
    half = LATE // 2
    late[0:D, :] = gquery_ref[...]
    late[D : D + KVW, :] = mm(keys, act, NT).astype(BF)
    late[D + KVW : D + 2 * KVW, :] = mm(values, act, NT).astype(BF)
    grads = dact_ref[...] + mm(key_ref[...], keys, TN) + mm(value_ref[...], values, TN)
    x = x_ref[...].astype(F32)
    rms = inverse_rms(x)
    pulled = grads * gain_ref[...]
    inner = jnp.mean(pulled * x, axis=0, keepdims=True)
    grad_ref[...] = (dmid_ref[...] + (pulled * rms - x * (rms * rms * rms * inner))).astype(BF)
    at = D + 2 * KVW
    late[at : at + 16, :] = ggain_ref[...].astype(BF)
    late[at + 16 : at + 32, :] = row_sums(grads * x * rms).astype(BF)
    late[at + 32 :, :] = jnp.zeros((LATE - at - 32, D), BF)
    core = scalars[5]
    mine_ref[...] = late[pl.ds(pl.multiple_of(core * half, half), half), :]
    other_ref[...] = late[pl.ds(pl.multiple_of((1 - core) * half, half), half), :]


def shift(values, axis, by):
    return lax.ppermute(values, axis, [(i, (i + by) % 4) for i in range(4)])


def swap(values):
    return lax.ppermute(values, "core", [(0, 1), (1, 0)])


def mirror(values):
    return lax.ppermute(values, SEQ, [(i, UNITS - 1 - i) for i in range(UNITS)])


def zigzag(values):
    return jnp.concatenate([values[:, :CHUNK], mirror(values[:, CHUNK:])], axis=1)


def add_pick_kernel(count, scalars, *refs):
    total = refs[0][...].astype(F32)
    for ref in refs[1:count]:
        total = total + ref[...].astype(F32)
    scratch = refs[-1]
    scratch[...] = total.astype(BF).reshape(scratch.shape)
    for k, out in enumerate(refs[count:-1]):
        out[...] = scratch[(scalars[0] + k) & 3]


def add_pick(parts, index):
    rows, width = parts[0].shape
    out = shape(rows // 4, width)
    return call(
        partial(add_pick_kernel, len(parts)), "sum_and_split", (out,) * 4, index, parts,
        (pltpu.VMEM((4, rows // 4, width), BF),),
    )


def place_kernel(count, scalars, *refs):
    out = refs[count]
    for k in range(count):
        out[(scalars[0] - k + 4) & (count - 1)] = refs[k][...]


def place(parts, index):
    rows, width = parts[0].shape
    stacked = call(partial(place_kernel, len(parts)), "place", shape(len(parts), rows, width), index, parts)
    return stacked.reshape(len(parts) * rows, width)


def add_placed_kernel(scalars, p0, p1, p2, p3, out, scratch):
    for k, ref in enumerate((p0, p1, p2, p3)):
        scratch[(scalars[0] - k + 4) & 3] = ref[...].astype(F32)
    out[...] = ((scratch[0] + scratch[1]) + (scratch[2] + scratch[3])).astype(BF)


def add_placed(parts, index):
    rows, width = parts[0].shape
    return call(
        add_placed_kernel, "sum", shape(rows, width), index, parts, (pltpu.VMEM((4, rows, width), F32),)
    )


def plain_sum_kernel(*refs):
    total = refs[0][...].astype(F32)
    for ref in refs[1:-1]:
        total = total + ref[...].astype(F32)
    refs[-1][...] = total.astype(refs[-1].dtype)


def plain_sum(parts):
    return call(plain_sum_kernel, "sum", shape(*parts[0].shape), None, parts)


def sum_everywhere(mine, other, at):
    pieces = add_pick([mine, swap(other)], at["x"])
    pieces = add_pick([pieces[0]] + [shift(pieces[k], "x", k) for k in (1, 2, 3)], at["dp"])
    small = plain_sum([pieces[0]] + [shift(pieces[k], "dp", k) for k in (1, 2, 3)])
    small = add_placed([small] + [shift(small, "z", k) for k in (1, 2, 3)], at["z"])
    part = place([small] + [shift(small, "dp", k) for k in (1, 2, 3)], at["dp"])
    part = place([part] + [shift(part, "x", k) for k in (1, 2, 3)], at["x"])
    return place([part, swap(part)], at["core"])


def turns(places):
    freqs = ROPE_BASE ** (-2.0 * jnp.arange(HALF).astype(F32) / HD)
    angles = freqs[:, None] * places.astype(F32)
    return jnp.concatenate([jnp.cos(angles), jnp.sin(angles)], axis=0)


def body(
    tokens,
    segments,
    positions,
    norm_gain,
    query_weight,
    key_weight,
    value_weight,
    output_weight,
    mlp_gain,
    gate_weight,
    up_weight,
    down_weight,
    cotangent,
):
    axis = {name: lax.axis_index(name) for name in ALL}
    at = {name: index.reshape(1) for name, index in axis.items()}
    unit = (axis["x"] * 4 + axis["z"]) * 2 + axis["core"]
    x_own = tokens[0].T
    key_cols, value_cols, down_cols = key_weight.T, value_weight.T, down_weight.T
    norm_gain = norm_gain.reshape(D, 1)
    mlp_gain = mlp_gain.reshape(D, 1)

    packed = call(
        keys_kernel, "keys_values", shape(PADROWS, 2 * KVW), None,
        (x_own, norm_gain, turns(positions), key_cols, value_cols, segments),
    )
    gathered = lax.all_gather(packed, SEQ, axis=0, tiled=False)

    third = TOK * unit + jnp.sum((segments < 2).astype(jnp.int32))
    marks = jnp.where(segments == 2, third, jnp.where(segments == 1, -1, 0))
    ints = zigzag(jnp.concatenate([marks, positions], axis=0))
    marks, places = ints[0:1], ints[1:2]
    marks = jnp.broadcast_to(marks.reshape(2, 1, CHUNK), (2, 8, CHUNK))
    both = zigzag(jnp.concatenate([x_own, cotangent[0].T], axis=0))
    x, out_grad = both[:D], both[D:]
    chunk_a, chunk_b = 2 * unit, 2 * UNITS - 1 - 2 * unit
    scalars = jnp.stack([
        (chunk_a > chunk_b).astype(jnp.int32), jnp.minimum(chunk_a, chunk_b), jnp.maximum(chunk_a, chunk_b),
        axis["x"], axis["z"], axis["core"],
    ])
    turn = turns(places)
    act, queries = call(
        queries_kernel, "queries", (shape(D, TOK), shape(D, TOK)), None, (x, norm_gain, turn, query_weight)
    )

    attended, norm = attend(scalars, marks, queries, gathered)
    result, dmid, dattn, gout, ggate, gup, gdown, ggain = feed_forward(
        x, out_grad, attended, mlp_gain, output_weight, gate_weight, up_weight, down_cols
    )
    gout, ggate, gup, gdown = lax.psum((gout, ggate, gup, gdown), ALL)

    dq, mine, other = attend_back(scalars, marks, queries, dattn, attended, norm, gathered)

    came = swap(other)
    add = lambda *parts: sum(p.astype(F32) for p in parts).astype(BF)
    first = [add(mine[0, k], came[0, k]) for k in range(4)]
    second = [add(mine[1, k], came[1, k]) for k in range(4)]
    first = [first[0]] + [shift(first[k], "x", k) for k in (1, 2, 3)]
    second = [second[0]] + [shift(second[k], "z", k) for k in (1, 2, 3)]
    gquery, dact = call(
        query_tail_kernel, "queries_back", (shape(D, D), shape(D, TOK, dtype=F32)), None,
        (dq, turn, act, query_weight),
    )
    first = [add(*(p[k] for p in first)) for k in range(4)]
    second = [add(*(p[k] for p in second)) for k in range(4)]
    first = [first[0]] + [shift(first[k], "z", k) for k in (1, 2, 3)]
    second = [second[0]] + [shift(second[k], "x", k) for k in (1, 2, 3)]

    input_grad, mine, other = call(
        tail_kernel, "tail", (shape(D, TOK), shape(LATE // 2, D), shape(LATE // 2, D)), scalars,
        (*first, *second, turn, act, x, norm_gain, key_cols, value_cols, dact, dmid, gquery, ggain),
        (pltpu.VMEM((LATE, D), BF),),
    )
    late = sum_everywhere(mine, other, at)
    result = zigzag(result)
    input_grad = zigzag(input_grad)
    at_gain = D + 2 * KVW
    return (
        result.T[None],
        input_grad.T[None],
        late[at_gain + 16].astype(F32),
        late[0:D].astype(F32),
        late[D : D + KVW].T.astype(F32),
        late[D + KVW : D + 2 * KVW].T.astype(F32),
        gout.astype(F32),
        late[at_gain].astype(F32),
        ggate.astype(F32),
        gup.astype(F32),
        gdown.T.astype(F32),
    )


def solution(mesh):
    inner = Mesh(mesh.devices.reshape(4, 4, 4, 2), ALL)
    row = P("dp", SEQ, None)
    flat = P("dp", SEQ)
    return jax.shard_map(
        body,
        mesh=inner,
        in_specs=(row, flat, flat) + (P(),) * 9 + (row,),
        out_specs=(row, row) + (P(),) * 9,
        check_vma=False,
    )
```

time: 461 us -> 355 us (0.77)
  blocking collectives: 66.6 us -> 0 us
  waiting for transfers between devices: 199 us -> 141 us
  starting transfers between devices: 13.9 us -> 58.1 us
  matrix products: 25.9 us -> 0 us
    reduce_scatter x1 -> x0, waiting for transfers between devices: 70 us -> none  [body(): shares = lax.psum_scatter(key_terms, SEQ, scatter_dimension=0, tiled=False)]
    psum x1 -> x0, blocking collectives: 66.6 us -> none  [body(): lax.psum(tuple((v.astype(BF) for v in (grad_query_weight, grad_key_weight...]
    ppermute x0 -> x30, waiting for transfers between devices: none -> 54.6 us  [the longest x27 47 us: shift(): return lax.ppermute(values, axis, [(i, (i + by) % 4) for i in range(4)])]
    psum x1, waiting for transfers between devices: 88 us -> 40.9 us  [body(): gout, ggate, gup, gdown = lax.psum((gout, ggate, gup, gdown), ALL)]
    ppermute x0 -> x30, starting transfers between devices: none -> 41.3 us  [the longest x27 34.3 us: shift(): return lax.ppermute(values, axis, [(i, (i + by) % 4) for i in range(4)])]
    dot_general x21 -> x0, matrix products: 25.9 us -> none  [mm(): return lax.dot_general(left, right, dims, preferred_element_type=F32)]
    all_gather x1, waiting for transfers between devices: 29.7 us -> 34.7 us  [body(): gathered = lax.all_gather(packed, SEQ, axis=0, tiled=False)]
    pallas_call x2 -> x14, Pallas kernels: 96.6 us -> 101 us  [the longest x13 89.4 us: call(): pl.pallas_call(kernel, out_shape=out_shape, in_specs=specs, out_specs=tup...]
  transfers between devices with their start and end apart: 7 -> 36, of which waited for: 5 -> 23; matrix products, arithmetic and copies ran while one was open for 7% -> 7% of each run, Pallas kernels for 0% -> 6%
where the time goes in v2:
time: 355 us; the launch traced here: 354 us
  waiting for transfers between devices  141 us (40%)
  Pallas kernels  101 us (28%)
  starting transfers between devices  58.1 us (16%)
  other arithmetic  25.9 us (7%)
  between operations  14.9 us (4%)
  local copies, waits for them, and re-layouts  12.9 us (4%)
    pallas_call x13, Pallas kernels, call(): pl.pallas_call(kernel, out_shape=out_shape, in_specs=specs, out_specs=tup...  89.4 us
    ppermute x27, waiting for transfers between devices, shift(): return lax.ppermute(values, axis, [(i, (i + by) % 4) for i in range(4)])  47 us
    psum x1, waiting for transfers between devices, body(): gout, ggate, gup, gdown = lax.psum((gout, ggate, gup, gdown), ALL)  40.9 us
    all_gather x1, waiting for transfers between devices, body(): gathered = lax.all_gather(packed, SEQ, axis=0, tiled=False)  34.7 us
    ppermute x27, starting transfers between devices, shift(): return lax.ppermute(values, axis, [(i, (i + by) % 4) for i in range(4)])  34.3 us
    ppermute x4, starting transfers between devices, mirror(): return lax.ppermute(values, SEQ, [(i, UNITS - 1 - i) for i in range(UNITS)])  16.7 us
    pallas_call x1, Pallas kernels, feed_forward(): pl.pallas_call(mlp_kernel, grid=(FF // FF_BLOCK,), out_shape=(shape(D, TO...  12 us
    ppermute x4, waiting for transfers between devices, mirror(): return lax.ppermute(values, SEQ, [(i, UNITS - 1 - i) for i in range(UNITS)])  10.5 us
  transfers between devices with their start and end apart: 36, of which 23 were waited for; matrix products, arithmetic and copies ran while one was open for 7% of the time, Pallas kernels for 6%

profile of v2, /device:TPU:1, one launch (start us, length us, event | category | flops | bytes accessed | tf_op | source)
XLA Modules:
  0.0 353.9 jit_solution(13636777583268778302)
XLA Ops:
  7.3 1.4 fusion.44
  10.6 7.3 %collective-permute-start.1 = (s32[2,128]{1,0:T(2,128)S(1)}, s32[2,128]{1,0:T(2,128)S(1)}, u32[]{:S(2)}, u32[]{:S(2)}) collective-permute-start(s32[2,128]{1,0:T(2,128)S(1)} %get-tuple-element.101), channel_id=1, source_target_pairs={{0,31},{1,30},{2,29},{3,28},{4,27},{5,26},{6,25},{7,24},{8,23},{9,... | collective-permute-start | bytes 3080 | tf_op jit(solution)/shard_map/ppermute | solution.py:452
  18.7 1.5 reshape.193.gain_ref
  21.2 2.5 keys_values.1
  23.8 4.2 %collective-permute-start = (bf16[1152,128]{1,0:T(8,128)(2,1)S(1)}, bf16[1152,128]{1,0:T(8,128)(2,1)S(1)}, u32[]{:S(2)}, u32[]{:S(2)}) collective-permute-start(bf16[1152,128]{1,0:T(8,128)(2,1)S(1)} %get-tuple-element.93), channel_id=1, source_target_pairs={{0,31},{1,30},{2,29},{3,28},{4,27},{5,26},{6,25},{7,24},{8,23},{9,... | collective-permute-start | bytes 884744 | tf_op jit(solution)/shard_map/ppermute | solution.py:452
  30.1 5.6 %collective-permute-done = bf16[1152,128]{1,0:T(8,128)(2,1)S(1)} collective-permute-done((bf16[1152,128]{1,0:T(8,128)(2,1)S(1)}, bf16[1152,128]{1,0:T(8,128)(2,1)S(1)}, u32[]{:S(2)}, u32[]{:S(2)}) %collective-permute-start) | collective-permute-done | bytes 294944 | tf_op jit(solution)/shard_map/ppermute | solution.py:452
  36.5 2.6 queries.1
  39.1 34.7 %all-gather.3.cloned.1.call-done = bf16[8704,384]{1,0:T(8,128)(2,1)} async-done(((bf16[272,384]{1,0:T(8,128)(2,1)}), bf16[8704,384]{1,0:T(8,128)(2,1)}) %all-gather.3.cloned.1.call-update) | async-done | bytes 6684688 | tf_op jit(solution)/shard_map/all_gather | solution.py:557
  74.4 28.5 %attention_forward.1 = (f32[576,256]{1,0:T(8,128)}, f32[3,8,768]{2,1,0:T(8,128)}) custom-call(s32[6]{0:T(128)} %stack.31.scalars, s32[2,8,128]{2,1,0:T(8,128)} %broadcast_in_dim.31.marks_ref, bf16[576,256]{1,0:T(8,128)(2,1)} %get-tuple-element.39.q_ref, bf16[32,272,384]{2,1,0:T(8,128)(2,1)} %bitcast.124), custom_call_target="tpu_custom_call" | custom-call | flops 20000000000 | bytes 7000000 | tf_op jit(solution)/shard_map/attention_forward/pallas_call | solution.py:59
  102.9 12.0 %feed_forward.1 = (bf16[576,256]{1,0:T(8,128)(2,1)}, f32[576,256]{1,0:T(8,128)}, bf16[576,256]{1,0:T(8,128)(2,1)}, bf16[576,576]{1,0:T(8,128)(2,1)}, bf16[576,15...) custom-call(bf16[576,256]{1,0:T(8,128)(2,1)} %get-tuple-element.92.x_ref, ...), custom_call_target="tpu_custom_call" | custom-call | flops 5000000000 | bytes 14000000 | tf_op jit(solution)/shard_map/feed_forward/pallas_call | solution.py:378
  114.9 34.8 %attention_backward.1 = (f32[576,256]{1,0:T(8,128)}, bf16[2,4,4,128,384]{4,3,2,1,0:T(8,128)(2,1)}, bf16[2,4,4,128,384]{4,3,2,1,0:T(8,128)(2,1)}) custom-call(s32[6]{0:T(128)} %stack.31.scalars, s32[2,8,128]{2,1,0:T(8,128)} %broadcast_in_dim.31.marks_ref, bf16[576,256]{1,0:T(8,128)(2,1)} %get-tuple-element.39.q_ref, ...), custom_call_target="tpu_custom_call" | custom-call | flops 40000000000 | bytes 14000000 | tf_op jit(solution)/shard_map/attention_backward/pallas_call | solution.py:59
  149.8 6.0 %collective-permute-done.3 = bf16[2,4,4,128,384]{4,3,2,1,0:T(8,128)(2,1)} collective-permute-done((bf16[2,4,4,128,384]{4,3,2,1,0:T(8,128)(2,1)}, bf16[2,4,4,128,384]{4,3,2,1,0:T(8,128)(2,1)}, u32[]{:S(2)}, u32[]{:S(2)}) %collective-permute-start.3) | collective-permute-done | bytes 3145760 | tf_op jit(solution)/shard_map/ppermute | solution.py:448
  155.7 2.9 add_convert_fusion.3
  158.6 3.4 collective-permute-start.12
  163.5 3.3 collective-permute-start.5
  166.8 6.0 %collective-permute-done.12 = bf16[4,128,384]{2,1,0:T(8,128)(2,1)S(1)} collective-permute-done((bf16[4,128,384]{2,1,0:T(8,128)(2,1)S(1)}, bf16[4,128,384]{2,1,0:T(8,128)(2,1)S(1)}, u32[]{:S(2)}, u32[]{:S(2)}) %collective-permute-start.12) | collective-permute-done | bytes 393248 | tf_op jit(solution)/shard_map/ppermute | solution.py:444
  172.8 2.7 collective-permute-start.4
  175.5 1.1 collective-permute-done.11
  176.6 9.6 %collective-permute-done.10 = bf16[4,128,384]{2,1,0:T(8,128)(2,1)S(1)} collective-permute-done((bf16[4,128,384]{2,1,0:T(8,128)(2,1)S(1)}, bf16[4,128,384]{2,1,0:T(8,128)(2,1)S(1)}, u32[]{:S(2)}, u32[]{:S(2)}) %collective-permute-start.10) | collective-permute-done | bytes 393248 | tf_op jit(solution)/shard_map/ppermute | solution.py:444
  187.7 3.4 collective-permute-start.14
  192.0 1.1 collective-permute-start.9
  193.1 1.6 collective-permute-start.8
  194.7 3.2 queries_back.1
  198.8 3.4 collective-permute-done.7.a1
  202.9 4.5 %tail.1 = (bf16[576,256]{1,0:T(8,128)(2,1)}, bf16[512,576]{1,0:T(8,128)(2,1)}, bf16[512,576]{1,0:T(8,128)(2,1)}) custom-call(s32[6]{0:T(128)} %stack.31.scalars, bf16[128,384]{1,0:T(8,128)(2,1)} %get-tuple-element.88.a0, bf16[128,384]{1,0:T(8,128)(2,1)} %copy-done.20, bf16[128,384]{1,0:T(8,128)(2,1)} %copy-done.19, bf16[128,384]{1,0:T(8,128)(2,1)} %copy-done.18, ...), custom_call_target="tpu_custom_call" | custom-call | flops 100000000 | bytes 1000000 | tf_op jit(solution)/shard_map/tail/pallas_call | solution.py:59
  207.4 1.3 copy.32
  208.7 1.2 collective-permute-start.17
  209.9 1.6 collective-permute-done.17
  212.6 2.4 sum_and_split.2
  215.5 3.1 collective-permute-start.19
  219.1 3.3 collective-permute-done.18.refs_1_
  222.4 4.5 %collective-permute-done.19.refs_2_ = bf16[128,576]{1,0:T(8,128)(2,1)S(1)} collective-permute-done((bf16[128,576]{1,0:T(8,128)(2,1)}, bf16[128,576]{1,0:T(8,128)(2,1)S(1)}, u32[]{:S(2)}, u32[]{:S(2)}) %collective-permute-start.19) | collective-permute-done | bytes 147488 | tf_op jit(solution)/shard_map/ppermute | solution.py:444
  227.6 1.9 sum_and_split.3
  229.5 1.5 collective-permute-start.21
  231.1 2.1 collective-permute-start.22
  233.2 1.3 collective-permute-start.23
  234.5 1.3 collective-permute-done.22.refs_2_
  235.8 1.1 collective-permute-done.23.refs_3_
  237.5 1.5 sum.2.p0
  240.5 1.6 collective-permute-done.26.p3
  242.1 1.7 collective-permute-done.25.p2
  245.3 1.5 sum.3.refs_0_
  246.8 2.3 collective-permute-start.29
  250.6 3.3 collective-permute-done.28.refs_2_
  255.1 1.5 place.3
  256.6 2.6 collective-permute-start.32
  259.8 3.9 %collective-permute-done.32.refs_3_ = bf16[128,576]{1,0:T(8,128)(2,1)S(1)} collective-permute-done((bf16[128,576]{1,0:T(8,128)(2,1)}, bf16[128,576]{1,0:T(8,128)(2,1)S(1)}, u32[]{:S(2)}, u32[]{:S(2)}) %collective-permute-start.32) | collective-permute-done | bytes 147488 | tf_op jit(solution)/shard_map/ppermute | solution.py:444
  263.7 1.6 collective-permute-done.31.refs_2_
  265.3 1.9 collective-permute-done.30.refs_1_
  267.9 2.1 place.4
  269.9 1.3 copy.34
  271.3 5.8 %collective-permute-start.33 = (bf16[512,576]{0,1:T(8,128)(2,1)S(1)}, bf16[512,576]{0,1:T(8,128)(2,1)S(1)}, u32[]{:S(2)}, u32[]{:S(2)}) collective-permute-start(bf16[512,576]{0,1:T(8,128)(2,1)S(1)} %copy.34), channel_id=1, source_target_pairs={{0,1},{1,0},{2,3},{3,2},{4,5},{5,4},{6,7},{7,6},{8,9},{9,8},{10,11... | collective-permute-start | bytes 1769480 | tf_op jit(solution)/shard_map/ppermute | solution.py:448
  277.0 1.1 collective-permute-start.2
  278.2 4.1 %collective-permute-start.16 = (bf16[576,128]{1,0:T(8,128)(2,1)S(1)}, bf16[576,128]{1,0:T(8,128)(2,1)S(1)}, u32[]{:S(2)}, u32[]{:S(2)}) collective-permute-start(bf16[576,128]{1,0:T(8,128)(2,1)S(1)} %get-tuple-element.96), channel_id=1, source_target_pairs={{0,31},{1,30},{2,29},{3,28},{4,27},{5,26},{6,25},{7,24},{8,23},{9,... | collective-permute-start | bytes 442376 | tf_op jit(solution)/shard_map/ppermute | solution.py:452
  282.3 4.9 %collective-permute-done.2 = bf16[576,128]{1,0:T(8,128)(2,1)S(1)} collective-permute-done((bf16[576,128]{1,0:T(8,128)(2,1)S(1)}, bf16[576,128]{1,0:T(8,128)(2,1)S(1)}, u32[]{:S(2)}, u32[]{:S(2)}) %collective-permute-start.2) | collective-permute-done | bytes 147488 | tf_op jit(solution)/shard_map/ppermute | solution.py:452
  287.9 40.9 %all-reduce.3.cloned.1.call-done = (bf16[576,576]{1,0:T(8,128)(2,1)}, bf16[576,1536]{1,0:T(8,128)(2,1)}, bf16[576,1536]{1,0:T(8,128)(2,1)}, bf16[1536,576]{0,1:T(8,128)(2,1)}) async-done(((bf16[576,576]{1,0:T(8,128)(2,1)}, bf16[576,1536]{1,0:T(8,128)(2,1)}, bf16[576,1536]{1,0:T(8,128)(2,1)}, bf16[1536,576]{0,1:T(8,128)(2,1)}), (bf16[576,576]{1,0:T(8,128)(2,1)}, bf16[576,1536]{1,0:T(8,128)(2,1)}, ...) | async-done | bytes 5971984 | tf_op jit(solution)/shard_map/psum | solution.py:580
  328.8 2.5 convert_element_type.411
  331.3 2.3 convert_element_type.414
  333.6 2.3 convert_element_type.415
  335.8 2.3 convert_element_type.417
  339.9 2.4 place.5
  342.4 1.4 fusion.40
  343.8 2.1 convert_bitcast_fusion
  345.9 1.2 slice_convert_fusion
  (119 shorter events, 24.9 us)
Async XLA Ops:
  7.2 16.5 %copy-start.5 = (bf16[1,256,576]{1,2,0:T(8,128)(2,1)S(1)}, bf16[1,256,576]{1,2,0:T(8,128)(2,1)}, u32[]{:S(2)}) copy-start(bf16[1,256,576]{1,2,0:T(8,128)(2,1)} %param.13) | copy-start | bytes 884740
  7.2 16.5 %copy-start.8 = (bf16[1,256,576]{1,2,0:T(8,128)(2,1)S(1)}, bf16[1,256,576]{1,2,0:T(8,128)(2,1)}, u32[]{:S(2)}) copy-start(bf16[1,256,576]{1,2,0:T(8,128)(2,1)} %param.25) | copy-start | bytes 884740
  7.2 20.7 %copy-start.21 = (f32[576]{0:T(1024)S(1)}, f32[576]{0:T(1024)}, u32[]{:S(2)}) copy-start(f32[576]{0:T(1024)} %param.21) | copy-start | bytes 6916
  7.2 66.6 %all-gather.3.cloned.1.call-start = ((), (), s32[]{:S(2)}) async-start(), calls=%async_computation | async-start | bytes 6893568 | tf_op jit(solution)/shard_map/all_gather | solution.py:557
  10.6 9.6 %collective-permute-start.1 = (s32[2,128]{1,0:T(2,128)S(1)}, s32[2,128]{1,0:T(2,128)S(1)}, u32[]{:S(2)}, u32[]{:S(2)}) collective-permute-start(s32[2,128]{1,0:T(2,128)S(1)} %get-tuple-element.101), channel_id=1, source_target_pairs={{0,31},{1,30},{2,29},{3,28},{4,27},{5,26},{6,25},{7,24},{8,23},{9,... | collective-permute-start | bytes 3080 | tf_op jit(solution)/shard_map/ppermute | solution.py:452
  23.7 305.2 %all-reduce.3.cloned.1.call-start = ((), (), s32[]{:S(2)}) async-start(), calls=%async_computation.1 | async-start | bytes 12091392 | tf_op jit(solution)/shard_map/psum | solution.py:580
  23.8 11.9 %collective-permute-start = (bf16[1152,128]{1,0:T(8,128)(2,1)S(1)}, bf16[1152,128]{1,0:T(8,128)(2,1)S(1)}, u32[]{:S(2)}, u32[]{:S(2)}) collective-permute-start(bf16[1152,128]{1,0:T(8,128)(2,1)S(1)} %get-tuple-element.93), channel_id=1, source_target_pairs={{0,31},{1,30},{2,29},{3,28},{4,27},{5,26},{6,25},{7,24},{8,23},{9,... | collective-permute-start | bytes 884744 | tf_op jit(solution)/shard_map/ppermute | solution.py:452
  149.7 6.0 %collective-permute-start.3 = (bf16[2,4,4,128,384]{4,3,2,1,0:T(8,128)(2,1)}, bf16[2,4,4,128,384]{4,3,2,1,0:T(8,128)(2,1)}, u32[]{:S(2)}, u32[]{:S(2)}) collective-permute-start(bf16[2,4,4,128,384]{4,3,2,1,0:T(8,128)(2,1)} %get-tuple-element.45), channel_id=1, source_target_pairs={{0,1},{1,0},{2,3},{3,2},{4,5},{5,4},{6,7},{7,6},{8,9},{9,8},{10,11... | collective-permute-start | bytes 9437192 | tf_op jit(solution)/shard_map/ppermute | solution.py:448
  149.7 6.0 %copy-start.1 = (bf16[2,4,4,128,384]{4,3,2,1,0:T(8,128)(2,1)S(1)}, bf16[2,4,4,128,384]{4,3,2,1,0:T(8,128)(2,1)}, u32[]{:S(2)}) copy-start(bf16[2,4,4,128,384]{4,3,2,1,0:T(8,128)(2,1)} %get-tuple-element.44) | copy-start | bytes 9437188
  158.6 14.2 %collective-permute-start.12 = (bf16[4,128,384]{2,1,0:T(8,128)(2,1)S(1)}, bf16[4,128,384]{2,1,0:T(8,128)(2,1)S(1)}, u32[]{:S(2)}, u32[]{:S(2)}) collective-permute-start(bf16[4,128,384]{2,1,0:T(8,128)(2,1)S(1)} %get-tuple-element.74), channel_id=1, source_target_pairs={{0,6},{2,0},{4,2},{6,4},{1,7},{3,1},{5,3},{7,5},{8,14},{10,8},{12,... | collective-permute-start | bytes 1179656 | tf_op jit(solution)/shard_map/ppermute | solution.py:444
  162.1 14.6 %collective-permute-start.11 = (bf16[4,128,384]{2,1,0:T(8,128)(2,1)S(1)}, bf16[4,128,384]{2,1,0:T(8,128)(2,1)S(1)}, u32[]{:S(2)}, u32[]{:S(2)}) collective-permute-start(bf16[4,128,384]{2,1,0:T(8,128)(2,1)S(1)} %get-tuple-element.75), channel_id=1, source_target_pairs={{0,4},{2,6},{4,0},{6,2},{1,5},{3,7},{5,1},{7,3},{8,12},{10,14},{12... | collective-permute-start | bytes 1179656 | tf_op jit(solution)/shard_map/ppermute | solution.py:444
  162.1 24.2 %collective-permute-start.10 = (bf16[4,128,384]{2,1,0:T(8,128)(2,1)S(1)}, bf16[4,128,384]{2,1,0:T(8,128)(2,1)S(1)}, u32[]{:S(2)}, u32[]{:S(2)}) collective-permute-start(bf16[4,128,384]{2,1,0:T(8,128)(2,1)S(1)} %get-tuple-element.76), channel_id=1, source_target_pairs={{0,2},{2,4},{4,6},{6,0},{1,3},{3,5},{5,7},{7,1},{8,10},{10,12},{12... | collective-permute-start | bytes 1179656 | tf_op jit(solution)/shard_map/ppermute | solution.py:444
  162.7 28.4 %collective-permute-start.6 = (bf16[4,128,384]{2,1,0:T(8,128)(2,1)S(1)}, bf16[4,128,384]{2,1,0:T(8,128)(2,1)S(1)}, u32[]{:S(2)}, u32[]{:S(2)}) collective-permute-start(bf16[4,128,384]{2,1,0:T(8,128)(2,1)S(1)} %get-tuple-element.77), channel_id=1, source_target_pairs={{0,24},{8,0},{16,8},{24,16},{1,25},{9,1},{17,9},{25,17},{2,26},{10... | collective-permute-start | bytes 1179656 | tf_op jit(solution)/shard_map/ppermute | solution.py:444
  163.5 27.6 %collective-permute-start.5 = (bf16[4,128,384]{2,1,0:T(8,128)(2,1)S(1)}, bf16[4,128,384]{2,1,0:T(8,128)(2,1)S(1)}, u32[]{:S(2)}, u32[]{:S(2)}) collective-permute-start(bf16[4,128,384]{2,1,0:T(8,128)(2,1)S(1)} %get-tuple-element.78), channel_id=1, source_target_pairs={{0,16},{8,24},{16,0},{24,8},{1,17},{9,25},{17,1},{25,9},{2,18},{10... | collective-permute-start | bytes 1179656 | tf_op jit(solution)/shard_map/ppermute | solution.py:444
  172.8 18.4 %collective-permute-start.4 = (bf16[4,128,384]{2,1,0:T(8,128)(2,1)S(1)}, bf16[4,128,384]{2,1,0:T(8,128)(2,1)S(1)}, u32[]{:S(2)}, u32[]{:S(2)}) collective-permute-start(bf16[4,128,384]{2,1,0:T(8,128)(2,1)S(1)} %get-tuple-element.79), channel_id=1, source_target_pairs={{0,8},{8,16},{16,24},{24,0},{1,9},{9,17},{17,25},{25,1},{2,10},{10... | collective-permute-start | bytes 1179656 | tf_op jit(solution)/shard_map/ppermute | solution.py:444
  187.1 7.6 %collective-permute-start.15 = (bf16[128,384]{1,0:T(8,128)(2,1)S(1)}, bf16[128,384]{1,0:T(8,128)(2,1)S(1)}, u32[]{:S(2)}, u32[]{:S(2)}) collective-permute-start(bf16[128,384]{1,0:T(8,128)(2,1)S(1)} %get-tuple-element.81), channel_id=1, source_target_pairs={{0,24},{8,0},{16,8},{24,16},{1,25},{9,1},{17,9},{25,17},{2,26},{10... | collective-permute-start | bytes 294920 | tf_op jit(solution)/shard_map/ppermute | solution.py:444
  187.7 10.3 %collective-permute-start.14 = (bf16[128,384]{1,0:T(8,128)(2,1)S(1)}, bf16[128,384]{1,0:T(8,128)(2,1)S(1)}, u32[]{:S(2)}, u32[]{:S(2)}) collective-permute-start(bf16[128,384]{1,0:T(8,128)(2,1)S(1)} %get-tuple-element.82), channel_id=1, source_target_pairs={{0,16},{8,24},{16,0},{24,8},{1,17},{9,25},{17,1},{25,9},{2,18},{10... | collective-permute-start | bytes 294920 | tf_op jit(solution)/shard_map/ppermute | solution.py:444
  191.1 6.8 %collective-permute-start.13 = (bf16[128,384]{1,0:T(8,128)(2,1)S(1)}, bf16[128,384]{1,0:T(8,128)(2,1)S(1)}, u32[]{:S(2)}, u32[]{:S(2)}) collective-permute-start(bf16[128,384]{1,0:T(8,128)(2,1)S(1)} %get-tuple-element.83), channel_id=1, source_target_pairs={{0,8},{8,16},{16,24},{24,0},{1,9},{9,17},{17,25},{25,1},{2,10},{10... | collective-permute-start | bytes 294920 | tf_op jit(solution)/shard_map/ppermute | solution.py:444
  192.0 5.9 %collective-permute-start.9 = (bf16[128,384]{1,0:T(8,128)(2,1)S(1)}, bf16[128,384]{1,0:T(8,128)(2,1)S(1)}, u32[]{:S(2)}, u32[]{:S(2)}) collective-permute-start(bf16[128,384]{1,0:T(8,128)(2,1)S(1)} %get-tuple-element.85), channel_id=1, source_target_pairs={{0,6},{2,0},{4,2},{6,4},{1,7},{3,1},{5,3},{7,5},{8,14},{10,8},{12,... | collective-permute-start | bytes 294920 | tf_op jit(solution)/shard_map/ppermute | solution.py:444
  193.1 5.7 %collective-permute-start.8 = (bf16[128,384]{1,0:T(8,128)(2,1)S(1)}, bf16[128,384]{1,0:T(8,128)(2,1)S(1)}, u32[]{:S(2)}, u32[]{:S(2)}) collective-permute-start(bf16[128,384]{1,0:T(8,128)(2,1)S(1)} %get-tuple-element.86), channel_id=1, source_target_pairs={{0,4},{2,6},{4,0},{6,2},{1,5},{3,7},{5,1},{7,3},{8,12},{10,14},{12... | collective-permute-start | bytes 294920 | tf_op jit(solution)/shard_map/ppermute | solution.py:444
  194.7 7.5 %copy-start.15 = (bf16[128,384]{1,0:T(8,128)(2,1)}, bf16[128,384]{1,0:T(8,128)(2,1)S(1)}, u32[]{:S(2)}) copy-start(bf16[128,384]{1,0:T(8,128)(2,1)S(1)} %collective-permute-done.15.b3) | copy-start | bytes 294916
  194.7 7.5 %collective-permute-start.7 = (bf16[128,384]{1,0:T(8,128)(2,1)S(1)}, bf16[128,384]{1,0:T(8,128)(2,1)S(1)}, u32[]{:S(2)}, u32[]{:S(2)}) collective-permute-start(bf16[128,384]{1,0:T(8,128)(2,1)S(1)} %get-tuple-element.87), channel_id=1, source_target_pairs={{0,2},{2,4},{4,6},{6,0},{1,3},{3,5},{5,7},{7,1},{8,10},{10,12},{12... | collective-permute-start | bytes 294920 | tf_op jit(solution)/shard_map/ppermute | solution.py:444
  197.9 4.3 %copy-start.16 = (bf16[128,384]{1,0:T(8,128)(2,1)}, bf16[128,384]{1,0:T(8,128)(2,1)S(1)}, u32[]{:S(2)}) copy-start(bf16[128,384]{1,0:T(8,128)(2,1)S(1)} %collective-permute-done.14.b2) | copy-start | bytes 294916
  197.9 4.3 %copy-start.17 = (bf16[128,384]{1,0:T(8,128)(2,1)}, bf16[128,384]{1,0:T(8,128)(2,1)S(1)}, u32[]{:S(2)}) copy-start(bf16[128,384]{1,0:T(8,128)(2,1)S(1)} %collective-permute-done.13.b1) | copy-start | bytes 294916
  198.0 4.3 %copy-start.18 = (bf16[128,384]{1,0:T(8,128)(2,1)}, bf16[128,384]{1,0:T(8,128)(2,1)S(1)}, u32[]{:S(2)}) copy-start(bf16[128,384]{1,0:T(8,128)(2,1)S(1)} %collective-permute-done.9.a3) | copy-start | bytes 294916
  198.8 3.5 copy-start.19
  202.3 0.6 copy-start.20
  208.7 2.9 collective-permute-start.17
  215.0 7.4 %collective-permute-start.18 = (bf16[128,576]{1,0:T(8,128)(2,1)}, bf16[128,576]{1,0:T(8,128)(2,1)S(1)}, u32[]{:S(2)}, u32[]{:S(2)}) collective-permute-start(bf16[128,576]{1,0:T(8,128)(2,1)} %get-tuple-element.56), channel_id=1, source_target_pairs={{0,8},{8,16},{16,24},{24,0},{1,9},{9,17},{17,25},{25,1},{2,10},{10... | collective-permute-start | bytes 442376 | tf_op jit(solution)/shard_map/ppermute | solution.py:444
  215.5 11.4 %collective-permute-start.19 = (bf16[128,576]{1,0:T(8,128)(2,1)}, bf16[128,576]{1,0:T(8,128)(2,1)S(1)}, u32[]{:S(2)}, u32[]{:S(2)}) collective-permute-start(bf16[128,576]{1,0:T(8,128)(2,1)} %get-tuple-element.57), channel_id=1, source_target_pairs={{0,16},{8,24},{16,0},{24,8},{1,17},{9,25},{17,1},{25,9},{2,18},{10... | collective-permute-start | bytes 442376 | tf_op jit(solution)/shard_map/ppermute | solution.py:444
  218.5 8.4 %collective-permute-start.20 = (bf16[128,576]{1,0:T(8,128)(2,1)}, bf16[128,576]{1,0:T(8,128)(2,1)S(1)}, u32[]{:S(2)}, u32[]{:S(2)}) collective-permute-start(bf16[128,576]{1,0:T(8,128)(2,1)} %get-tuple-element.58), channel_id=1, source_target_pairs={{0,24},{8,0},{16,8},{24,16},{1,25},{9,1},{17,9},{25,17},{2,26},{10... | collective-permute-start | bytes 442376 | tf_op jit(solution)/shard_map/ppermute | solution.py:444
  222.4 4.5 %copy-start.12 = (bf16[128,576]{1,0:T(8,128)(2,1)}, bf16[128,576]{1,0:T(8,128)(2,1)S(1)}, u32[]{:S(2)}) copy-start(bf16[128,576]{1,0:T(8,128)(2,1)S(1)} %collective-permute-done.18.refs_1_) | copy-start | bytes 442372
  226.9 0.7 copy-start.13
  226.9 0.7 copy-start.14
  229.5 4.9 %collective-permute-start.21 = (bf16[32,576]{1,0:T(8,128)(2,1)}, bf16[32,576]{1,0:T(8,128)(2,1)S(1)}, u32[]{:S(2)}, u32[]{:S(2)}) collective-permute-start(bf16[32,576]{1,0:T(8,128)(2,1)} %get-tuple-element.60), channel_id=1, source_target_pairs={{0,32},{32,64},{64,96},{96,0},{1,33},{33,65},{65,97},{97,1},{2,34}... | collective-permute-start | bytes 110600 | tf_op jit(solution)/shard_map/ppermute | solution.py:444
  231.1 4.7 %collective-permute-start.22 = (bf16[32,576]{1,0:T(8,128)(2,1)}, bf16[32,576]{1,0:T(8,128)(2,1)S(1)}, u32[]{:S(2)}, u32[]{:S(2)}) collective-permute-start(bf16[32,576]{1,0:T(8,128)(2,1)} %get-tuple-element.61), channel_id=1, source_target_pairs={{0,64},{32,96},{64,0},{96,32},{1,65},{33,97},{65,1},{97,33},{2,66}... | collective-permute-start | bytes 110600 | tf_op jit(solution)/shard_map/ppermute | solution.py:444
  233.2 3.7 %collective-permute-start.23 = (bf16[32,576]{1,0:T(8,128)(2,1)}, bf16[32,576]{1,0:T(8,128)(2,1)S(1)}, u32[]{:S(2)}, u32[]{:S(2)}) collective-permute-start(bf16[32,576]{1,0:T(8,128)(2,1)} %get-tuple-element.62), channel_id=1, source_target_pairs={{0,96},{32,0},{64,32},{96,64},{1,97},{33,1},{65,33},{97,65},{2,98}... | collective-permute-start | bytes 110600 | tf_op jit(solution)/shard_map/ppermute | solution.py:444
  234.5 2.5 copy-start.22
  235.8 1.1 copy-start.23
  237.5 39.5 %copy-start.6 = (bf16[576,256]{1,0:T(8,128)(2,1)S(1)}, bf16[576,256]{1,0:T(8,128)(2,1)}, u32[]{:S(2)}) copy-start(bf16[576,256]{1,0:T(8,128)(2,1)} %get-tuple-element.41) | copy-start | bytes 884740
  239.1 3.1 collective-permute-start.26
  239.3 4.6 %collective-permute-start.25 = (bf16[32,576]{1,0:T(8,128)(2,1)}, bf16[32,576]{1,0:T(8,128)(2,1)S(1)}, u32[]{:S(2)}, u32[]{:S(2)}) collective-permute-start(bf16[32,576]{1,0:T(8,128)(2,1)} %sum.2.p0), channel_id=1, source_target_pairs={{0,4},{2,6},{4,0},{6,2},{1,5},{3,7},{5,1},{7,3},{8,12},{10,14},{12... | collective-permute-start | bytes 110600 | tf_op jit(solution)/shard_map/ppermute | solution.py:444
  240.1 4.6 %collective-permute-start.24 = (bf16[32,576]{1,0:T(8,128)(2,1)}, bf16[32,576]{1,0:T(8,128)(2,1)S(1)}, u32[]{:S(2)}, u32[]{:S(2)}) collective-permute-start(bf16[32,576]{1,0:T(8,128)(2,1)} %sum.2.p0), channel_id=1, source_target_pairs={{0,2},{2,4},{4,6},{6,0},{1,3},{3,5},{5,7},{7,1},{8,10},{10,12},{12... | collective-permute-start | bytes 110600 | tf_op jit(solution)/shard_map/ppermute | solution.py:444
  242.1 2.6 copy-start.24
  243.9 0.8 copy-start.27
  244.7 0.6 copy-start.29
  246.8 31.4 %copy-start.7 = (bf16[576,256]{1,0:T(8,128)(2,1)S(1)}, bf16[576,256]{1,0:T(8,128)(2,1)}, u32[]{:S(2)}) copy-start(bf16[576,256]{1,0:T(8,128)(2,1)} %get-tuple-element.52) | copy-start | bytes 884740
  246.8 3.7 %collective-permute-start.29 = (bf16[32,576]{1,0:T(8,128)(2,1)}, bf16[32,576]{1,0:T(8,128)(2,1)S(1)}, u32[]{:S(2)}, u32[]{:S(2)}) collective-permute-start(bf16[32,576]{1,0:T(8,128)(2,1)} %sum.3.refs_0_), channel_id=1, source_target_pairs={{0,96},{32,0},{64,32},{96,64},{1,97},{33,1},{65,33},{97,65},{2,98}... | collective-permute-start | bytes 110600 | tf_op jit(solution)/shard_map/ppermute | solution.py:444
  249.1 4.7 %collective-permute-start.28 = (bf16[32,576]{1,0:T(8,128)(2,1)}, bf16[32,576]{1,0:T(8,128)(2,1)S(1)}, u32[]{:S(2)}, u32[]{:S(2)}) collective-permute-start(bf16[32,576]{1,0:T(8,128)(2,1)} %sum.3.refs_0_), channel_id=1, source_target_pairs={{0,64},{32,96},{64,0},{96,32},{1,65},{33,97},{65,1},{97,33},{2,66}... | collective-permute-start | bytes 110600 | tf_op jit(solution)/shard_map/ppermute | solution.py:444
  249.1 4.7 %collective-permute-start.27 = (bf16[32,576]{1,0:T(8,128)(2,1)}, bf16[32,576]{1,0:T(8,128)(2,1)S(1)}, u32[]{:S(2)}, u32[]{:S(2)}) collective-permute-start(bf16[32,576]{1,0:T(8,128)(2,1)} %sum.3.refs_0_), channel_id=1, source_target_pairs={{0,32},{32,64},{64,96},{96,0},{1,33},{33,65},{65,97},{97,1},{2,34}... | collective-permute-start | bytes 110600 | tf_op jit(solution)/shard_map/ppermute | solution.py:444
  250.6 3.3 copy-start.25
  256.6 7.1 %collective-permute-start.32 = (bf16[128,576]{1,0:T(8,128)(2,1)}, bf16[128,576]{1,0:T(8,128)(2,1)S(1)}, u32[]{:S(2)}, u32[]{:S(2)}) collective-permute-start(bf16[128,576]{1,0:T(8,128)(2,1)} %bitcast.117), channel_id=1, source_target_pairs={{0,24},{8,0},{16,8},{24,16},{1,25},{9,1},{17,9},{25,17},{2,26},{10... | collective-permute-start | bytes 442376 | tf_op jit(solution)/shard_map/ppermute | solution.py:444
  259.2 6.0 %collective-permute-start.31 = (bf16[128,576]{1,0:T(8,128)(2,1)}, bf16[128,576]{1,0:T(8,128)(2,1)S(1)}, u32[]{:S(2)}, u32[]{:S(2)}) collective-permute-start(bf16[128,576]{1,0:T(8,128)(2,1)} %bitcast.118), channel_id=1, source_target_pairs={{0,16},{8,24},{16,0},{24,8},{1,17},{9,25},{17,1},{25,9},{2,18},{10... | collective-permute-start | bytes 442376 | tf_op jit(solution)/shard_map/ppermute | solution.py:444
  259.7 7.5 %collective-permute-start.30 = (bf16[128,576]{1,0:T(8,128)(2,1)}, bf16[128,576]{1,0:T(8,128)(2,1)S(1)}, u32[]{:S(2)}, u32[]{:S(2)}) collective-permute-start(bf16[128,576]{1,0:T(8,128)(2,1)} %bitcast.119), channel_id=1, source_target_pairs={{0,8},{8,16},{16,24},{24,0},{1,9},{9,17},{17,25},{25,1},{2,10},{10... | collective-permute-start | bytes 442376 | tf_op jit(solution)/shard_map/ppermute | solution.py:444
  263.7 3.5 copy-start.9
  265.3 1.9 copy-start.10
  267.2 0.7 copy-start.11
  271.3 67.6 %collective-permute-start.33 = (bf16[512,576]{0,1:T(8,128)(2,1)S(1)}, bf16[512,576]{0,1:T(8,128)(2,1)S(1)}, u32[]{:S(2)}, u32[]{:S(2)}) collective-permute-start(bf16[512,576]{0,1:T(8,128)(2,1)S(1)} %copy.34), channel_id=1, source_target_pairs={{0,1},{1,0},{2,3},{3,2},{4,5},{5,4},{6,7},{7,6},{8,9},{9,8},{10,11... | collective-permute-start | bytes 1769480 | tf_op jit(solution)/shard_map/ppermute | solution.py:448
  277.0 10.1 %collective-permute-start.2 = (bf16[576,128]{1,0:T(8,128)(2,1)S(1)}, bf16[576,128]{1,0:T(8,128)(2,1)S(1)}, u32[]{:S(2)}, u32[]{:S(2)}) collective-permute-start(bf16[576,128]{1,0:T(8,128)(2,1)S(1)} %get-tuple-element.98), channel_id=1, source_target_pairs={{0,31},{1,30},{2,29},{3,28},{4,27},{5,26},{6,25},{7,24},{8,23},{9,... | collective-permute-start | bytes 442376 | tf_op jit(solution)/shard_map/ppermute | solution.py:452
  278.2 59.9 %collective-permute-start.16 = (bf16[576,128]{1,0:T(8,128)(2,1)S(1)}, bf16[576,128]{1,0:T(8,128)(2,1)S(1)}, u32[]{:S(2)}, u32[]{:S(2)}) collective-permute-start(bf16[576,128]{1,0:T(8,128)(2,1)S(1)} %get-tuple-element.96), channel_id=1, source_target_pairs={{0,31},{1,30},{2,29},{3,28},{4,27},{5,26},{6,25},{7,24},{8,23},{9,... | collective-permute-start | bytes 442376 | tf_op jit(solution)/shard_map/ppermute | solution.py:452
  328.8 2.5 copy-start.4
  331.3 2.3 copy-start.3
  333.6 2.3 copy-start.2
  342.4 3.5 copy-start
  (3 other events, 1.9 us)
Sparse Core Ops, SparseCore 0:
  23.8 49.9 all-gather.2
  149.9 178.9 all-reduce.2

commit v3 on v2

--- a/solution.py
+++ b/solution.py
@@ -27,11 +27,15 @@
 UNITS = 32
 COLS = GROUP * CHUNK
 PADROWS = TOK + 16
-LATE = 1024
+KVC = 2 * KVW + 128
+SHARD = 96
+GROUPS = 32
+LATE_SHARD = 144
 FF_BLOCK = 512
 
 SEQ = ("x", "z", "core")
 ALL = ("dp", "x", "z", "core")
+CHIPS = ("dp", "x", "z")
 BF = jnp.bfloat16
 F32 = jnp.float32
 
@@ -169,6 +173,21 @@
         lse_ref[g] = jnp.broadcast_to(run_max[g, 0:1, :] + jnp.log2(total), (8, 2 * COLS))
 
 
+def turned_back(grads, table):
+    lane = lax.broadcasted_iota(jnp.int32, table.shape, 1)
+    table = table + pltpu.roll(table, 64, 1)
+    first = (lane & HALF) == 0
+    cosine = jnp.where(lane < HD, jnp.where(first, table, pltpu.roll(table, HALF, 1)), 1.0)
+    sine = jnp.where(first, pltpu.roll(table, 128 - HALF, 1), -table)
+    sine = jnp.where(lane < HD, sine, 0.0)
+    out = []
+    for grad in grads:
+        grad = grad.astype(F32)
+        partner = jnp.where(first, pltpu.roll(grad, 128 - HALF, 1), pltpu.roll(grad, HALF, 1))
+        out.append((grad * cosine + partner * sine).astype(BF))
+    return jnp.concatenate(out, axis=1)
+
+
 def backward_kernel(
     scalars, marks_ref, q_ref, do_ref, out_ref, lse_ref, kv_ref, dq_ref, mine_ref, other_ref, qcat, docat, acc, delta
 ):
@@ -188,21 +207,24 @@
             terms = do_ref[rows, lanes].astype(F32) * out_ref[rows, lanes]
             delta[head // GROUP, 0:1, at : at + CHUNK] = jnp.sum(terms, axis=0, keepdims=True)
 
-    def store(tile, lanes, grads):
+    def store(tile, grads):
         mirrored = UNITS - 1 - tile
         kx, kz = (tile // 8 - my_x) & 3, ((tile // 2) % 4 - my_z) & 3
         mx, mz = (mirrored // 8 - my_x) & 3, ((mirrored // 2) % 4 - my_z) & 3
         same = lax.rem(tile, 2) == my_c
 
+        def put(first_ref, second_ref):
+            for g, grad in enumerate(grads):
+                first_ref[0, kx, kz, g * CHUNK : (g + 1) * CHUNK, :] = grad[0:CHUNK]
+                second_ref[1, mz, mx, g * CHUNK : (g + 1) * CHUNK, :] = grad[CHUNK:TOK]
+
         @pl.when(same)
         def _():
-            mine_ref[0, kx, kz, :, lanes] = grads[0:CHUNK]
-            other_ref[1, mz, mx, :, lanes] = grads[CHUNK:TOK]
+            put(mine_ref, other_ref)
 
         @pl.when(jnp.logical_not(same))
         def _():
-            other_ref[0, kx, kz, :, lanes] = grads[0:CHUNK]
-            mine_ref[1, mz, mx, :, lanes] = grads[CHUNK:TOK]
+            put(other_ref, mine_ref)
 
     def step(tile, count, cols, whole):
         rows = count * TOK
@@ -225,19 +247,17 @@
             probs = jnp.exp2(scores - shift)
             grad_probs = mm(block, do_part)
             grad_scores = (probs * (grad_probs - delta[g, 0:1, 0:cols])).astype(BF)
-            grads = mm(grad_scores, q_part, NT) + mm(probs.astype(BF), do_part, NT)
+            all_grads.append(mm(grad_scores, q_part, NT) + mm(probs.astype(BF), do_part, NT))
             keys = jnp.transpose(block)[0:HD, :]
             acc[g, :, 0:cols] = acc[g, :, 0:cols] + mm(keys, grad_scores)
-            all_grads.append(grads.astype(BF))
-        grads = jnp.concatenate(all_grads, axis=1)
         for i in range(count):
-            store(tile + i, slice(None), grads[i * TOK : (i + 1) * TOK])
+            store(tile + i, [grad[i * TOK : (i + 1) * TOK].astype(BF) for grad in all_grads])
 
     tiles(scalars, step)
 
     @pl.loop(hi_diag + 1, UNITS)
     def _(t):
-        store(t, slice(None), jnp.zeros((TOK, 2 * KVW), BF))
+        store(t, [jnp.zeros((TOK, 128), BF)] * KVH)
 
     for g in range(KVH):
         scatter_columns(dq_ref, acc[g] * SCALE, g, scalars)
@@ -261,7 +281,7 @@
 
 
 def attend_back(scalars, marks, queries, grad_out, attended, norm, keys_values):
-    blocks = shape(2, 4, 4, CHUNK, 2 * KVW)
+    blocks = shape(2, 4, 4, KVH * CHUNK, 128)
     return call(
         backward_kernel,
         "attention_backward",
@@ -275,7 +295,7 @@
             pltpu.VMEM((KVH, 8, 2 * COLS), F32),
         ),
         flops=40 * 10**9,
-        moved=14 * 10**6,
+        moved=24 * 10**6,
     )
 
 
@@ -290,15 +310,16 @@
 
 
 def row_sums(values):
-    ones = jnp.ones((16, TOK), BF)
+    ones = jnp.ones((16, values.shape[1]), BF)
     high = values.astype(BF)
     low = (values - high.astype(F32)).astype(BF)
     return mm(ones, high, NT) + mm(ones, low, NT)
 
 
-def keys_kernel(x_ref, gain_ref, turn_ref, key_ref, value_ref, seg_ref, out_ref):
+def keys_kernel(x_ref, gain_ref, turn_ref, key_ref, value_ref, seg_ref, out_ref, act_ref):
     x = x_ref[...].astype(F32)
     act = (x * inverse_rms(x) * gain_ref[...]).astype(BF)
+    act_ref[...] = act
     keys = mm(key_ref[...], act)
     values = mm(value_ref[...], act)
     turn = turn_ref[...]
@@ -306,8 +327,10 @@
         rows = slice(g * HD, (g + 1) * HD)
         block = jnp.concatenate([rotated(keys[rows], turn, 1.0), values[rows]], axis=0)
         out_ref[0:TOK, g * 128 : (g + 1) * 128] = jnp.transpose(block).astype(BF)
+    high = turn.astype(BF).astype(F32)
+    out_ref[0:TOK, 2 * KVW :] = jnp.transpose(jnp.concatenate([high, turn - high], axis=0)).astype(BF)
     first_len = jnp.sum((seg_ref[...] == 0).astype(F32), axis=1, keepdims=True)
-    out_ref[TOK:, :] = jnp.broadcast_to(first_len, (16, 2 * KVW)).astype(BF)
+    out_ref[TOK:, :] = jnp.broadcast_to(first_len, (16, KVC)).astype(BF)
 
 
 def queries_kernel(x_ref, gain_ref, turn_ref, weight_ref, act_ref, out_ref):
@@ -323,11 +346,28 @@
 
 
 def mlp_kernel(
-    x_ref, c_ref, attn_ref, gain_ref, out_weight, gate_ref, up_ref, down_ref,
-    result_ref, dmid_ref, dattn_ref, gout_ref, ggate_ref, gup_ref, gdown_ref, ggain_ref,
-    mid, act, act_cols, c_cols, result, dact,
+    scalars, x_ref, c_ref, attn_ref, gain_ref, out_weight, gate_ref, up_ref, down_ref,
+    result_ref, dmid_ref, dattn_ref, ggain_ref, mine_ref, other_ref,
+    mid, act, act_cols, c_cols, result, dact, shards, sems,
 ):
     block = pl.program_id(0)
+    my_c = scalars[5]
+
+    def put(group, values):
+        for k in range(values.shape[1] // 128):
+            for i in range(values.shape[0] // SHARD):
+                j = k * (values.shape[0] // SHARD) + i
+                piece = values[i * SHARD : (i + 1) * SHARD, k * 128 : (k + 1) * 128]
+                shards[group + j // 8, j % 8] = piece
+
+    def send(group):
+        @pl.when(group // 16 == my_c)
+        def _():
+            pltpu.make_async_copy(shards.at[group], mine_ref.at[group % 16], sems.at[0]).start()
+
+        @pl.when(group // 16 != my_c)
+        def _():
+            pltpu.make_async_copy(shards.at[group], other_ref.at[group % 16], sems.at[1]).start()
 
     @pl.when(block == 0)
     def _():
@@ -350,9 +390,11 @@
     dup = (dhidden * silu).astype(BF)
     dgate = (dhidden * up * (sigmoid * (1.0 + gate * (1.0 - sigmoid)))).astype(BF)
     result[...] += mm(down_ref[...], hidden, NT)
-    gdown_ref[...] = mm(c_ref[...], hidden).astype(BF)
-    ggate_ref[...] = mm(act_cols[...], dgate).astype(BF)
-    gup_ref[...] = mm(act_cols[...], dup).astype(BF)
+    put(block * 9, mm(act_cols[...], dgate).astype(BF))
+    put(block * 9 + 3, mm(act_cols[...], dup).astype(BF))
+    put(block * 9 + 6, mm(c_ref[...], hidden).astype(BF))
+    for group in range(9):
+        send(block * 9 + group)
     dact[...] += mm(gate_ref[...], dgate, NT) + mm(up_ref[...], dup, NT)
 
     @pl.when(block == FF // FF_BLOCK - 1)
@@ -368,76 +410,200 @@
         dmid = c_ref[...].astype(F32) + (pulled * rms - middle * (rms * rms * rms * inner))
         dmid_ref[...] = dmid
         low = dmid.astype(BF)
-        gout_ref[...] = mm(attn_ref[...].astype(BF), low, NT).astype(BF)
         dattn_ref[...] = mm(out_weight[...], low).astype(BF)
-
-
-def feed_forward(x, cotangent, attended, gain, out_weight, gate_weight, up_weight, down_weight):
+        gout = mm(attn_ref[...].astype(BF), low, NT).astype(BF)
+        put(27, gout[:, :512])
+        shards[30:32] = jnp.zeros((2, 8, SHARD, 128), BF)
+        put(30, jnp.concatenate([gout[: D // 2, 512:], gout[D // 2 :, 512:]], axis=1))
+        for group in range(27, 32):
+            send(group)
+        for i, ref in enumerate((mine_ref, other_ref)):
+            pltpu.make_async_copy(ref, ref, sems.at[i]).wait()
+
+
+def feed_forward(scalars, x, cotangent, attended, gain, out_weight, gate_weight, up_weight, down_weight):
     whole = lambda *dims: pl.BlockSpec(dims, lambda f: (0,) * len(dims))
     part = pl.BlockSpec((D, FF_BLOCK), lambda f: (0, f))
     return pl.pallas_call(
         mlp_kernel,
         grid=(FF // FF_BLOCK,),
-        out_shape=(
-            shape(D, TOK), shape(D, TOK, dtype=F32), shape(D, TOK), shape(D, D),
-            shape(D, FF), shape(D, FF), shape(D, FF), shape(16, D, dtype=F32),
-        ),
-        in_specs=[whole(D, TOK), whole(D, TOK), whole(D, TOK), whole(D, 1), whole(D, D), part, part, part],
-        out_specs=(whole(D, TOK), whole(D, TOK), whole(D, TOK), whole(D, D), part, part, part, whole(16, D)),
+        out_shape=(shape(D, TOK), shape(D, TOK, dtype=F32), shape(D, TOK), shape(16, D, dtype=F32))
+        + (shape(GROUPS // 2, 8, SHARD, 128),) * 2,
+        in_specs=[smem(), whole(D, TOK), whole(D, TOK), whole(D, TOK), whole(D, 1), whole(D, D), part, part, part],
+        out_specs=(whole(D, TOK), whole(D, TOK), whole(D, TOK), whole(16, D))
+        + (pl.BlockSpec(memory_space=pl.ANY),) * 2,
         scratch_shapes=[
             pltpu.VMEM((D, TOK), F32), pltpu.VMEM((TOK, D), BF), pltpu.VMEM((D, TOK), BF),
             pltpu.VMEM((TOK, D), BF), pltpu.VMEM((D, TOK), F32), pltpu.VMEM((D, TOK), F32),
+            pltpu.VMEM((GROUPS, 8, SHARD, 128), BF), pltpu.SemaphoreType.DMA((2,)),
         ],
         compiler_params=pltpu.CompilerParams(vmem_limit_bytes=56 * 1024 * 1024),
         cost_estimate=pl.CostEstimate(flops=5 * 10**9, bytes_accessed=14 * 10**6, transcendentals=10**6),
         name="feed_forward",
-    )(x, cotangent, attended, gain, out_weight, gate_weight, up_weight, down_weight)
-
-
-def query_tail_kernel(dq_ref, turn_ref, act_ref, weight_ref, gquery_ref, dact_ref):
+    )(scalars, x, cotangent, attended, gain, out_weight, gate_weight, up_weight, down_weight)
+
+
+def early_finish_kernel(shards, gate_ref, up_ref, down_ref, out_ref):
+    block = pl.program_id(0)
+
+    def get(group, k):
+        pieces = []
+        for i in range(D // SHARD):
+            piece = group * 8 + D // SHARD * k + i
+            half, piece = piece // (GROUPS * 4), piece % (GROUPS * 4)
+            pieces.append(shards[piece // 2, half, piece % 2])
+        return jnp.concatenate(pieces, axis=0).astype(F32)
+
+    for kind, ref in enumerate((gate_ref, up_ref, down_ref)):
+        for k in range(4):
+            ref[:, k * 128 : (k + 1) * 128] = get(block * 9 + kind * 3, k)
+
+    @pl.when(block == FF // FF_BLOCK - 1)
+    def _():
+        for k in range(4):
+            out_ref[:, k * 128 : (k + 1) * 128] = get(27, k)
+        rest = get(30, 0)[: D // 2]
+        out_ref[:, 512:] = jnp.concatenate([rest[:, :HD], rest[:, HD:]], axis=0)
+
+
+def early_finish(shards):
+    part = pl.BlockSpec((D, FF_BLOCK), lambda f: (0, f))
+    return pl.pallas_call(
+        early_finish_kernel,
+        grid=(FF // FF_BLOCK,),
+        out_shape=(shape(D, FF, dtype=F32),) * 3 + (shape(D, D, dtype=F32),),
+        in_specs=[pl.BlockSpec(shards.shape, lambda f: (0,) * 5)],
+        out_specs=(part, part, part, pl.BlockSpec((D, D), lambda f: (0, 0))),
+        compiler_params=pltpu.CompilerParams(vmem_limit_bytes=56 * 1024 * 1024),
+        cost_estimate=pl.CostEstimate(flops=10**7, bytes_accessed=19 * 10**6, transcendentals=0),
+        name="early_gradients",
+    )(shards)
+
+
+def late_rows():
+    return 0, 2592, 4320, 4400
+
+
+def pack(buffer, at, values):
+    count = values.shape[0]
+    for k in range(4):
+        buffer[at + k * count : at + (k + 1) * count, :] = values[:, k * 128 : (k + 1) * 128]
+    if count > 16:
+        rest = jnp.concatenate([values[: count // 2, 512:], values[count // 2 :, 512:]], axis=1)
+        buffer[at + 4 * count : at + 4 * count + count // 2, :] = rest
+    else:
+        buffer[at + 4 * count : at + 5 * count, 0:64] = values[:, 512:]
+
+
+def unpack(buffer, at, count):
+    blocks = [buffer[at + k * count : at + (k + 1) * count, :] for k in range(4)]
+    if count > 16:
+        rest = buffer[at + 4 * count : at + 4 * count + count // 2, :]
+        rest = jnp.concatenate([rest[:, :64], rest[:, 64:]], axis=0)
+    else:
+        rest = buffer[at + 4 * count : at + 5 * count, 0:64]
+    return jnp.concatenate(blocks + [rest], axis=1)
+
+
+def late_kernel(
+    scalars, dq_ref, turn_ref, act_ref, weight_ref, key_ref, value_ref, gain_ref, ggain_ref, kv_ref, acts_ref,
+    dkv_mine, dkv_other, dact_ref, mine_ref, other_ref, late, gkv,
+):
+    my_x, my_z, my_c, my_y = scalars[3], scalars[4], scalars[5], scalars[6]
+    gkv[...] = jnp.zeros_like(gkv)
+
+    @pl.loop(0, 16)
+    def _(step):
+        kx, kz = step // 4, step % 4
+        x, z = (my_x + kx) & 3, (my_z + kz) & 3
+        mx, mz = (3 - x - my_x) & 3, (3 - z - my_z) & 3
+        total = None
+        for core, first_ref, second_ref in ((my_c, dkv_mine, dkv_other), (1 - my_c, dkv_other, dkv_mine)):
+            unit = x * 8 + z * 2 + core
+            first, second = first_ref[0, kx, kz], second_ref[1, mz, mx]
+            grads = []
+            for g in range(KVH):
+                rows = slice(g * CHUNK, (g + 1) * CHUNK)
+                grads.append(jnp.concatenate([first[rows], second[rows]], axis=0))
+            turned = turned_back(grads, kv_ref[unit, 0:TOK, 2 * KVW :].astype(F32))
+            product = mm(acts_ref[unit], turned)
+            total = product if total is None else total + product
+        gkv[...] += total
+
     turn = turn_ref[...]
     heads = [rotated(dq_ref[h * HD : (h + 1) * HD, :], turn, -1.0).astype(BF) for h in range(H)]
     low = jnp.concatenate(heads, axis=0)
-    gquery_ref[...] = mm(act_ref[...], low, NT).astype(BF)
-    dact_ref[...] = mm(weight_ref[...], low)
+    weight = weight_ref[...]
+    gquery = mm(act_ref[...], low, NT)
+    dact_ref[...] = mm(weight, low)
+    at_q, at_kv, at_n, at_m = late_rows()
+    late[at_n:, :] = jnp.zeros((32 * LATE_SHARD - at_n, 128), BF)
+    pack(late, at_q, gquery.astype(BF))
+    gain = row_sums(gquery * weight.astype(F32))
+    for g in range(KVH):
+        rows = slice(g * HD, (g + 1) * HD)
+        grad = gkv[:, g * 128 : (g + 1) * 128]
+        late[at_kv + g * D : at_kv + (g + 1) * D, :] = grad.astype(BF)
+        columns = jnp.transpose(jnp.concatenate([key_ref[rows, :], value_ref[rows, :]], axis=0))
+        gain = gain + row_sums(grad * columns.astype(F32))
+    pack(late, at_n, (gain / gain_ref[...]).astype(BF))
+    pack(late, at_m, ggain_ref[...].astype(BF))
+    for x in range(4):
+        for z in range(4):
+            index = ((x - my_x) & 3, (z - my_z) & 3)
+            for target, core in ((mine_ref, my_c), (other_ref, 1 - my_c)):
+                at = ((core * 4 + x) * 4 + z) * LATE_SHARD
+                target[index] = late[pl.ds(pl.multiple_of(at, LATE_SHARD), LATE_SHARD), :]
+
+
+def join_kernel(mine_ref, came_ref, late_mine, late_came, *outs):
+    for k in range(4):
+        for j in range(4):
+            outs[k][j, 0 : KVH * CHUNK, :] = add(mine_ref[0, k, j], came_ref[0, k, j])
+            outs[k][j, KVH * CHUNK :, :] = add(late_mine[k, j], late_came[k, j])
+            outs[4 + k][j] = add(mine_ref[1, k, j], came_ref[1, k, j])
+
+
+def late_finish_kernel(scalars, own_ref, came_ref, gquery_ref, gkey_ref, gvalue_ref, gnorm_ref, gmlp_ref, late):
+    my_x, my_z, my_c = scalars[3], scalars[4], scalars[5]
+    for source, core in ((own_ref, my_c), (came_ref, 1 - my_c)):
+        for x in range(4):
+            for z in range(4):
+                at = ((core * 4 + ((my_x - x) & 3)) * 4 + ((my_z - z) & 3)) * LATE_SHARD
+                late[pl.ds(pl.multiple_of(at, LATE_SHARD), LATE_SHARD), :] = source[x, z]
+    at_q, at_kv, at_n, at_m = late_rows()
+    gquery_ref[...] = unpack(late, at_q, D).astype(F32)
+    for g in range(KVH):
+        grad = jnp.transpose(late[at_kv + g * D : at_kv + (g + 1) * D, :].astype(F32))
+        gkey_ref[g * HD : (g + 1) * HD, :] = grad[:HD]
+        gvalue_ref[g * HD : (g + 1) * HD, :] = grad[HD:]
+    gnorm_ref[...] = unpack(late, at_n, 16).astype(F32)[0:1]
+    gmlp_ref[...] = unpack(late, at_m, 16).astype(F32)[0:1]
 
 
 def tail_kernel(
-    scalars, a0, a1, a2, a3, b0, b1, b2, b3, turn_ref, act_ref, x_ref, gain_ref, key_ref, value_ref, dact_ref, dmid_ref,
-    gquery_ref, ggain_ref, grad_ref, mine_ref, other_ref, late,
+    a0, a1, a2, a3, b0, b1, b2, b3, turn_ref, x_ref, gain_ref, key_ref, value_ref, dact_ref, dmid_ref, grad_ref
 ):
     turn = turn_ref[...]
     summed = []
     for parts in ((a0, a1, a2, a3), (b0, b1, b2, b3)):
-        total = parts[0][...].astype(F32)
+        total = parts[0][0 : KVH * CHUNK, :].astype(F32)
         for part in parts[1:]:
-            total = total + part[...].astype(F32)
+            total = total + part[0 : KVH * CHUNK, :].astype(F32)
         summed.append(total)
     keys, values = [], []
     for g in range(KVH):
-        columns = [jnp.transpose(t[:, g * 128 : (g + 1) * 128]) for t in summed]
+        columns = [jnp.transpose(t[g * CHUNK : (g + 1) * CHUNK, :]) for t in summed]
         columns = jnp.concatenate(columns, axis=1)
         keys.append(rotated(columns[:HD], turn, -1.0).astype(BF))
         values.append(columns[HD:].astype(BF))
     keys, values = jnp.concatenate(keys, axis=0), jnp.concatenate(values, axis=0)
-    act = act_ref[...]
-    half = LATE // 2
-    late[0:D, :] = gquery_ref[...]
-    late[D : D + KVW, :] = mm(keys, act, NT).astype(BF)
-    late[D + KVW : D + 2 * KVW, :] = mm(values, act, NT).astype(BF)
     grads = dact_ref[...] + mm(key_ref[...], keys, TN) + mm(value_ref[...], values, TN)
     x = x_ref[...].astype(F32)
     rms = inverse_rms(x)
     pulled = grads * gain_ref[...]
     inner = jnp.mean(pulled * x, axis=0, keepdims=True)
     grad_ref[...] = (dmid_ref[...] + (pulled * rms - x * (rms * rms * rms * inner))).astype(BF)
-    at = D + 2 * KVW
-    late[at : at + 16, :] = ggain_ref[...].astype(BF)
-    late[at + 16 : at + 32, :] = row_sums(grads * x * rms).astype(BF)
-    late[at + 32 :, :] = jnp.zeros((LATE - at - 32, D), BF)
-    core = scalars[5]
-    mine_ref[...] = late[pl.ds(pl.multiple_of(core * half, half), half), :]
-    other_ref[...] = late[pl.ds(pl.multiple_of((1 - core) * half, half), half), :]
 
 
 def shift(values, axis, by):
@@ -456,69 +622,18 @@
     return jnp.concatenate([values[:, :CHUNK], mirror(values[:, CHUNK:])], axis=1)
 
 
-def add_pick_kernel(count, scalars, *refs):
-    total = refs[0][...].astype(F32)
-    for ref in refs[1:count]:
-        total = total + ref[...].astype(F32)
-    scratch = refs[-1]
-    scratch[...] = total.astype(BF).reshape(scratch.shape)
-    for k, out in enumerate(refs[count:-1]):
-        out[...] = scratch[(scalars[0] + k) & 3]
-
-
-def add_pick(parts, index):
-    rows, width = parts[0].shape
-    out = shape(rows // 4, width)
-    return call(
-        partial(add_pick_kernel, len(parts)), "sum_and_split", (out,) * 4, index, parts,
-        (pltpu.VMEM((4, rows // 4, width), BF),),
-    )
-
-
-def place_kernel(count, scalars, *refs):
-    out = refs[count]
-    for k in range(count):
-        out[(scalars[0] - k + 4) & (count - 1)] = refs[k][...]
-
-
-def place(parts, index):
-    rows, width = parts[0].shape
-    stacked = call(partial(place_kernel, len(parts)), "place", shape(len(parts), rows, width), index, parts)
-    return stacked.reshape(len(parts) * rows, width)
-
-
-def add_placed_kernel(scalars, p0, p1, p2, p3, out, scratch):
-    for k, ref in enumerate((p0, p1, p2, p3)):
-        scratch[(scalars[0] - k + 4) & 3] = ref[...].astype(F32)
-    out[...] = ((scratch[0] + scratch[1]) + (scratch[2] + scratch[3])).astype(BF)
-
-
-def add_placed(parts, index):
-    rows, width = parts[0].shape
-    return call(
-        add_placed_kernel, "sum", shape(rows, width), index, parts, (pltpu.VMEM((4, rows, width), F32),)
-    )
-
-
-def plain_sum_kernel(*refs):
-    total = refs[0][...].astype(F32)
-    for ref in refs[1:-1]:
-        total = total + ref[...].astype(F32)
-    refs[-1][...] = total.astype(refs[-1].dtype)
-
-
-def plain_sum(parts):
-    return call(plain_sum_kernel, "sum", shape(*parts[0].shape), None, parts)
-
-
-def sum_everywhere(mine, other, at):
-    pieces = add_pick([mine, swap(other)], at["x"])
-    pieces = add_pick([pieces[0]] + [shift(pieces[k], "x", k) for k in (1, 2, 3)], at["dp"])
-    small = plain_sum([pieces[0]] + [shift(pieces[k], "dp", k) for k in (1, 2, 3)])
-    small = add_placed([small] + [shift(small, "z", k) for k in (1, 2, 3)], at["z"])
-    part = place([small] + [shift(small, "dp", k) for k in (1, 2, 3)], at["dp"])
-    part = place([part] + [shift(part, "x", k) for k in (1, 2, 3)], at["x"])
-    return place([part, swap(part)], at["core"])
+def add(*parts):
+    parts = [p.astype(F32) for p in parts]
+    total = parts[0] + parts[1] if len(parts) == 2 else (parts[0] + parts[2]) + (parts[1] + parts[3])
+    return total.astype(BF)
+
+
+def spread(parts, axis):
+    return [parts[0]] + [shift(parts[k], axis, k) for k in (1, 2, 3)]
+
+
+def collect(values, axis):
+    return [values] + [shift(values, axis, k) for k in (1, 2, 3)]
 
 
 def turns(places):
@@ -547,26 +662,32 @@
     unit = (axis["x"] * 4 + axis["z"]) * 2 + axis["core"]
     x_own = tokens[0].T
     key_cols, value_cols, down_cols = key_weight.T, value_weight.T, down_weight.T
+    norm_gain_row = norm_gain.reshape(1, D)
     norm_gain = norm_gain.reshape(D, 1)
     mlp_gain = mlp_gain.reshape(D, 1)
 
-    packed = call(
-        keys_kernel, "keys_values", shape(PADROWS, 2 * KVW), None,
+    packed, own_act = call(
+        keys_kernel, "keys_values", (shape(PADROWS, KVC), shape(D, TOK)), None,
         (x_own, norm_gain, turns(positions), key_cols, value_cols, segments),
     )
     gathered = lax.all_gather(packed, SEQ, axis=0, tiled=False)
+    acts = lax.all_gather(own_act, SEQ, axis=0, tiled=False)
+    x_own, segments, positions, packed = lax.optimization_barrier((x_own, segments, positions, packed))
 
     third = TOK * unit + jnp.sum((segments < 2).astype(jnp.int32))
-    marks = jnp.where(segments == 2, third, jnp.where(segments == 1, -1, 0))
-    ints = zigzag(jnp.concatenate([marks, positions], axis=0))
-    marks, places = ints[0:1], ints[1:2]
+    marks = jnp.where(segments == 2, third, jnp.where(segments == 1, -64, 0))
+    ints = jnp.concatenate([positions >> 6, positions & 63, marks >> 6, marks & 63], axis=0)
+    ints = jnp.pad(ints, ((0, 12), (0, 0))).astype(BF)
+    both = zigzag(jnp.concatenate([x_own, cotangent[0].T, ints], axis=0))
+    x, out_grad = both[:D], both[D : 2 * D]
+    ints = both[2 * D :].astype(jnp.int32)
+    places = ints[0:1] * 64 + ints[1:2]
+    marks = ints[2:3] * 64 + ints[3:4]
     marks = jnp.broadcast_to(marks.reshape(2, 1, CHUNK), (2, 8, CHUNK))
-    both = zigzag(jnp.concatenate([x_own, cotangent[0].T], axis=0))
-    x, out_grad = both[:D], both[D:]
     chunk_a, chunk_b = 2 * unit, 2 * UNITS - 1 - 2 * unit
     scalars = jnp.stack([
         (chunk_a > chunk_b).astype(jnp.int32), jnp.minimum(chunk_a, chunk_b), jnp.maximum(chunk_a, chunk_b),
-        axis["x"], axis["z"], axis["core"],
+        axis["x"], axis["z"], axis["core"], axis["dp"],
     ])
     turn = turns(places)
     act, queries = call(
@@ -574,49 +695,66 @@
     )
 
     attended, norm = attend(scalars, marks, queries, gathered)
-    result, dmid, dattn, gout, ggate, gup, gdown, ggain = feed_forward(
-        x, out_grad, attended, mlp_gain, output_weight, gate_weight, up_weight, down_cols
-    )
-    gout, ggate, gup, gdown = lax.psum((gout, ggate, gup, gdown), ALL)
+    result, dmid, dattn, ggain, mine, other = feed_forward(
+        scalars, x, out_grad, attended, mlp_gain, output_weight, gate_weight, up_weight, down_cols
+    )
+
+    early = add(mine, swap(other))
+    early, dattn = lax.optimization_barrier((early, dattn))
+    early = lax.all_to_all(early.reshape(64, 2, SHARD, 128), CHIPS, 0, 0, tiled=True)
 
     dq, mine, other = attend_back(scalars, marks, queries, dattn, attended, norm, gathered)
+    early = jnp.sum(early.astype(F32), axis=0).astype(BF)
+    other, early = lax.optimization_barrier((other, early))
+    early = lax.all_gather(early, ALL, axis=0, tiled=False)
 
     came = swap(other)
-    add = lambda *parts: sum(p.astype(F32) for p in parts).astype(BF)
-    first = [add(mine[0, k], came[0, k]) for k in range(4)]
-    second = [add(mine[1, k], came[1, k]) for k in range(4)]
-    first = [first[0]] + [shift(first[k], "x", k) for k in (1, 2, 3)]
-    second = [second[0]] + [shift(second[k], "z", k) for k in (1, 2, 3)]
-    gquery, dact = call(
-        query_tail_kernel, "queries_back", (shape(D, D), shape(D, TOK, dtype=F32)), None,
-        (dq, turn, act, query_weight),
-    )
-    first = [add(*(p[k] for p in first)) for k in range(4)]
-    second = [add(*(p[k] for p in second)) for k in range(4)]
-    first = [first[0]] + [shift(first[k], "z", k) for k in (1, 2, 3)]
-    second = [second[0]] + [shift(second[k], "x", k) for k in (1, 2, 3)]
-
-    input_grad, mine, other = call(
-        tail_kernel, "tail", (shape(D, TOK), shape(LATE // 2, D), shape(LATE // 2, D)), scalars,
-        (*first, *second, turn, act, x, norm_gain, key_cols, value_cols, dact, dmid, gquery, ggain),
-        (pltpu.VMEM((LATE, D), BF),),
-    )
-    late = sum_everywhere(mine, other, at)
-    result = zigzag(result)
-    input_grad = zigzag(input_grad)
-    at_gain = D + 2 * KVW
+    blocks = shape(4, 4, LATE_SHARD, 128)
+    dact, late_mine, late_other = call(
+        late_kernel, "late_gradients", (shape(D, TOK, dtype=F32), blocks, blocks), scalars,
+        (dq, turn, act, query_weight, key_cols, value_cols, norm_gain_row, ggain, gathered, acts, mine, other),
+        (pltpu.VMEM((32 * LATE_SHARD, 128), BF), pltpu.VMEM((D, 2 * KVW), F32)),
+    )
+    halves = call(
+        join_kernel, "join", (shape(4, KVH * CHUNK + LATE_SHARD, 128),) * 4 + (shape(4, KVH * CHUNK, 128),) * 4, None,
+        (mine, came, late_mine, swap(late_other)),
+    )
+    first_came, second_came = spread(halves[:4], "x"), spread(halves[4:], "z")
+    first = [add(*(c[k] for c in first_came)) for k in range(4)]
+    second = [add(*(c[k] for c in second_came)) for k in range(4)]
+    first, second = lax.optimization_barrier((first, second))
+    first_came, second_came = spread(first, "z"), spread(second, "x")
+    late = add(*(part[KVH * CHUNK :] for part in first_came))
+    late, second_came = lax.optimization_barrier((late, second_came))
+    late_came = collect(late, "dp")
+    input_grad = call(
+        tail_kernel, "tail", shape(D, TOK), None,
+        (*first_came, *second_came, turn, x, norm_gain, key_cols, value_cols, dact, dmid),
+    )
+    late = add(*late_came)
+    late, input_grad, result = lax.optimization_barrier((late, input_grad, result))
+    late = jnp.stack(collect(late, "z"))
+    input_grad, result = zigzag(input_grad), zigzag(result)
+    late = jnp.stack(collect(late, "x"))
+    late = call(
+        late_finish_kernel, "late_finish",
+        (shape(D, D, dtype=F32), shape(KVW, D, dtype=F32), shape(KVW, D, dtype=F32))
+        + (shape(1, D, dtype=F32),) * 2,
+        scalars, (late, swap(late)), (pltpu.VMEM((32 * LATE_SHARD, 128), BF),),
+    )
+    early = early_finish(early.reshape(64, 2, 2, SHARD, 128))
     return (
         result.T[None],
         input_grad.T[None],
-        late[at_gain + 16].astype(F32),
-        late[0:D].astype(F32),
-        late[D : D + KVW].T.astype(F32),
-        late[D + KVW : D + 2 * KVW].T.astype(F32),
-        gout.astype(F32),
-        late[at_gain].astype(F32),
-        ggate.astype(F32),
-        gup.astype(F32),
-        gdown.T.astype(F32),
+        late[3].reshape(D),
+        late[0],
+        late[1].T,
+        late[2].T,
+        early[3],
+        late[4].reshape(D),
+        early[0],
+        early[1],
+        early[2].T,
     )
 
 

time: 355 us -> 325 us (0.915)
  waiting for transfers between devices: 141 us -> 99.4 us
  Pallas kernels: 101 us -> 126 us
  other arithmetic: 25.9 us -> 19.4 us
  local copies, waits for them, and re-layouts: 12.9 us -> 7.95 us
    psum x1 -> x0, waiting for transfers between devices: 40.9 us -> none  [body(): gout, ggate, gup, gdown = lax.psum((gout, ggate, gup, gdown), ALL)]
    pallas_call x13 -> x8, Pallas kernels: 89.4 us -> 105 us  [call(): pl.pallas_call(kernel, out_shape=out_shape, in_specs=specs, out_specs=tup...]
    ppermute x27 -> x21, waiting for transfers between devices: 47 us -> 36.2 us  [shift(): return lax.ppermute(values, axis, [(i, (i + by) % 4) for i in range(4)])]
    all_to_all x0 -> x1, starting transfers between devices: none -> 9.17 us  [body(): lax.all_to_all(early.reshape(64, 2, SHARD, 128), CHIPS, 0, 0, tiled=True)]
    convert_element_type x8 -> x5, other arithmetic: 16.8 us -> 7.82 us  [add(): return total.astype(BF)]
    pallas_call x0 -> x1, Pallas kernels: none -> 8.56 us  [early_finish(): pl.pallas_call(early_finish_kernel, grid=(FF // FF_BLOCK,), out_shape=(sh...]
    ppermute x27 -> x21, starting transfers between devices: 34.3 us -> 25.8 us  [shift(): return lax.ppermute(values, axis, [(i, (i + by) % 4) for i in range(4)])]
    ppermute x4 -> x3, waiting for transfers between devices: 10.5 us -> 15.7 us  [mirror(): return lax.ppermute(values, SEQ, [(i, UNITS - 1 - i) for i in range(UNITS)])]
  transfers between devices with their start and end apart: 36 -> 32, of which waited for: 23 -> 19; matrix products, arithmetic and copies ran while one was open for 7% -> 7% of each run, Pallas kernels for 6% -> 35%
where the time goes in v3:
time: 325 us; the launch traced here: 324 us
  Pallas kernels  126 us (39%)
  waiting for transfers between devices  99.4 us (31%)
  starting transfers between devices  56.6 us (17%)
  other arithmetic  19.4 us (6%)
  between operations  14.7 us (5%)
  local copies, waits for them, and re-layouts  7.95 us (2%)
    pallas_call x8, Pallas kernels, call(): pl.pallas_call(kernel, out_shape=out_shape, in_specs=specs, out_specs=tup...  105 us
    ppermute x21, waiting for transfers between devices, shift(): return lax.ppermute(values, axis, [(i, (i + by) % 4) for i in range(4)])  36.2 us
    all_gather x1, waiting for transfers between devices, body(): gathered = lax.all_gather(packed, SEQ, axis=0, tiled=False)  34 us
    ppermute x21, starting transfers between devices, shift(): return lax.ppermute(values, axis, [(i, (i + by) % 4) for i in range(4)])  25.8 us
    ppermute x3, waiting for transfers between devices, mirror(): return lax.ppermute(values, SEQ, [(i, UNITS - 1 - i) for i in range(UNITS)])  15.7 us
    ppermute x3, starting transfers between devices, mirror(): return lax.ppermute(values, SEQ, [(i, UNITS - 1 - i) for i in range(UNITS)])  12.6 us
    pallas_call x1, Pallas kernels, feed_forward(): pl.pallas_call(mlp_kernel, grid=(FF // FF_BLOCK,), out_shape=(shape(D, TO...  12.1 us
    all_to_all x1, starting transfers between devices, body(): lax.all_to_all(early.reshape(64, 2, SHARD, 128), CHIPS, 0, 0, tiled=True)  9.17 us
  transfers between devices with their start and end apart: 32, of which 19 were waited for; matrix products, arithmetic and copies ran while one was open for 7% of the time, Pallas kernels for 35%

profile of v3, /device:TPU:1, one launch (start us, length us, event | category | flops | bytes accessed | tf_op | source)
XLA Modules:
  0.0 324.1 jit_solution(4106006849041838522)
XLA Ops:
  7.2 0.7 convert_element_type.242
  7.9 1.5 reshape.127.gain_ref
  9.7 0.6 pad_maximum_fusion.5.turn_ref
  10.3 2.5 keys_values.1
  12.9 0.7 all-gather.9.cloned.1.call-update
  13.6 1.3 shift-right-arithmetic_convert_fusion.1
  15.6 0.7 shift-right-arithmetic_convert_fusion
  16.3 1.1 pad_maximum_fusion
  17.5 7.4 %collective-permute-start = (bf16[1168,128]{1,0:T(8,128)(2,1)S(1)}, bf16[1168,128]{1,0:T(8,128)(2,1)S(1)}, u32[]{:S(2)}, u32[]{:S(2)}) collective-permute-start(bf16[1168,128]{1,0:T(8,128)(2,1)S(1)} %get-tuple-element.142), channel_id=1, source_target_pairs={{0,31},{1,30},{2,29},{3,28},{4,27},{5,26},{6,25},{7,24},{8,23},{9,... | collective-permute-start | bytes 897032 | tf_op jit(solution)/shard_map/ppermute | solution.py:618
  24.9 0.9 reshape.128.gain_ref
  26.3 7.4 %collective-permute-done = bf16[1168,128]{1,0:T(8,128)(2,1)S(1)} collective-permute-done((bf16[1168,128]{1,0:T(8,128)(2,1)S(1)}, bf16[1168,128]{1,0:T(8,128)(2,1)S(1)}, u32[]{:S(2)}, u32[]{:S(2)}) %collective-permute-start) | collective-permute-done | bytes 299040 | tf_op jit(solution)/shard_map/ppermute | solution.py:618
  34.6 0.9 pad_maximum_fusion.2
  35.5 2.6 queries.1
  38.1 34.0 %all-gather.7.cloned.1.call-done = bf16[8704,512]{1,0:T(8,128)(2,1)} async-done(((bf16[272,512]{1,0:T(8,128)(2,1)}), bf16[8704,512]{1,0:T(8,128)(2,1)}) %all-gather.7.cloned.1.call-update) | async-done | bytes 8912912 | tf_op jit(solution)/shard_map/all_gather | solution.py:673
  72.7 28.8 %attention_forward.1 = (f32[576,256]{1,0:T(8,128)}, f32[3,8,768]{2,1,0:T(8,128)}) custom-call(s32[7]{0:T(128)} %stack.65.scalars, s32[2,8,128]{2,1,0:T(8,128)} %broadcast_in_dim.31.marks_ref, bf16[576,256]{1,0:T(8,128)(2,1)} %get-tuple-element.73.q_ref, bf16[32,272,512]{2,1,0:T(8,128)(2,1)} %bitcast.61), custom_call_target="tpu_custom_call" | custom-call | flops 20000000000 | bytes 7000000 | tf_op jit(solution)/shard_map/attention_forward/pallas_call | solution.py:63
  101.5 12.1 %feed_forward.1 = (bf16[576,256]{1,0:T(8,128)(2,1)}, f32[576,256]{1,0:T(8,128)}, bf16[576,256]{1,0:T(8,128)(2,1)}, f32[16,576]{1,0:T(8,128)}, bf16[16,8,96,128]{...) custom-call(s32[7]{0:T(128)} %stack.65.scalars, bf16[576,256]{1,0:T(8,128)(2,1)} %get-tuple-element.138.x_ref, ...), custom_call_target="tpu_custom_call" | custom-call | flops 5000000000 | bytes 14000000 | tf_op jit(solution)/shard_map/feed_forward/pallas_call | solution.py:427
  113.8 6.2 %collective-permute-done.1 = bf16[16,8,96,128]{3,2,1,0:T(8,128)(2,1)S(1)} collective-permute-done((bf16[16,8,96,128]{3,2,1,0:T(8,128)(2,1)}, bf16[16,8,96,128]{3,2,1,0:T(8,128)(2,1)S(1)}, u32[]{:S(2)}, u32[]{:S(2)}) %collective-permute-start.1) | collective-permute-done | bytes 3145760 | tf_op jit(solution)/shard_map/ppermute | solution.py:614
  120.0 4.5 %add_convert_fusion = bf16[16,8,96,128]{3,2,1,0:T(8,128)(2,1)} fusion(bf16[16,8,96,128]{3,2,1,0:T(8,128)(2,1)S(1)} %collective-permute-done.1, bf16[16,8,96,128]{3,2,1,0:T(8,128)(2,1)} %get-tuple-element.75), kind=kLoop, calls=%fused_computation | loop fusion | flops 6291456 | bytes 9437184 | tf_op jit(solution)/shard_map/convert_element_type | solution.py:628
  124.5 9.2 %all-to-all-start = ((bf16[64,2,96,128]{3,2,1,0:T(8,128)(2,1)}), bf16[64,2,96,128]{3,2,1,0:T(8,128)(2,1)S(1)}, u32[]{:S(2)}, u32[]{:S(2)}) async-start(bf16[64,2,96,128]{3,2,1,0:T(8,128)(2,1)} %bitcast.59), calls=%async_computation | async-start | bytes 6291456 | tf_op jit(solution)/shard_map/all_to_all | solution.py:704
  133.7 35.0 %attention_backward.1 = (f32[576,256]{1,0:T(8,128)}, bf16[2,4,4,384,128]{4,3,2,1,0:T(8,128)(2,1)}, bf16[2,4,4,384,128]{4,3,2,1,0:T(8,128)(2,1)}) custom-call(s32[7]{0:T(128)} %stack.65.scalars, s32[2,8,128]{2,1,0:T(8,128)} %broadcast_in_dim.31.marks_ref, bf16[576,256]{1,0:T(8,128)(2,1)} %get-tuple-element.73.q_ref, ...), custom_call_target="tpu_custom_call" | custom-call | flops 40000000000 | bytes 24000000 | tf_op jit(solution)/shard_map/attention_backward/pallas_call | solution.py:63
  168.7 4.6 %all-to-all-done = bf16[64,2,96,128]{3,2,1,0:T(8,128)(2,1)S(1)} async-done(((bf16[64,2,96,128]{3,2,1,0:T(8,128)(2,1)}), bf16[64,2,96,128]{3,2,1,0:T(8,128)(2,1)S(1)}, u32[]{:S(2)}, u32[]{:S(2)}) %all-to-all-start) | async-done | bytes 3145760 | tf_op jit(solution)/shard_map/all_to_all | solution.py:704
  173.3 1.1 reduce_sum.22
  174.4 1.7 collective-permute-start.2
  176.6 24.9 %late_gradients.1 = (f32[576,256]{1,0:T(8,128)}, bf16[4,4,144,128]{3,2,1,0:T(8,128)(2,1)}, bf16[4,4,144,128]{3,2,1,0:T(8,128)(2,1)}) custom-call(s32[7]{0:T(128)} %stack.65.scalars, f32[576,256]{1,0:T(8,128)} %get-tuple-element.84.dq_ref, f32[64,256]{1,0:T(8,128)} %pad_maximum_fusion.6.turn_ref, bf16[576,256]{1,0:T(8,128)(2,1)} %get-tuple-element.85.act_ref, ...), custom_call_target="tpu_custom_call" | custom-call | flops 100000000 | bytes 1000000 | tf_op jit(solution)/shard_map/late_gradients/pallas_call | solution.py:63
  201.5 2.2 collective-permute-done.3.late_came
  203.7 0.8 copy-done.3
  204.5 1.0 copy-done
  205.6 5.1 %join.1 = (bf16[4,528,128]{2,1,0:T(8,128)(2,1)}, bf16[4,528,128]{2,1,0:T(8,128)(2,1)}, bf16[4,528,128]{2,1,0:T(8,128)(2,1)}, bf16[4,528,128]{2,1,0:T(8,128)(2,1)...) custom-call(bf16[2,4,4,384,128]{4,3,2,1,0:T(8,128)(2,1)} %get-tuple-, ...), custom_call_target="tpu_custom_call" | custom-call | flops 100000000 | bytes 1000000 | tf_op jit(solution)/shard_map/join/pallas_call | solution.py:63
  210.7 2.1 collective-permute-start.7
  212.8 2.7 collective-permute-start.9
  215.5 1.5 collective-permute-start.4
  217.1 6.6 %collective-permute-done.7 = bf16[4,384,128]{2,1,0:T(8,128)(2,1)S(1)} collective-permute-done((bf16[4,384,128]{2,1,0:T(8,128)(2,1)}, bf16[4,384,128]{2,1,0:T(8,128)(2,1)S(1)}, u32[]{:S(2)}, u32[]{:S(2)}) %collective-permute-start.7) | collective-permute-done | bytes 393248 | tf_op jit(solution)/shard_map/ppermute | solution.py:610
  223.6 2.1 collective-permute-start.6
  225.7 6.8 %collective-permute-done.8 = bf16[4,384,128]{2,1,0:T(8,128)(2,1)S(1)} collective-permute-done((bf16[4,384,128]{2,1,0:T(8,128)(2,1)}, bf16[4,384,128]{2,1,0:T(8,128)(2,1)S(1)}, u32[]{:S(2)}, u32[]{:S(2)}) %collective-permute-start.8) | collective-permute-done | bytes 393248 | tf_op jit(solution)/shard_map/ppermute | solution.py:610
  232.5 1.9 fusion.7
  234.4 12.8 %collective-permute-done.5 = bf16[4,528,128]{2,1,0:T(8,128)(2,1)S(1)} collective-permute-done((bf16[4,528,128]{2,1,0:T(8,128)(2,1)}, bf16[4,528,128]{2,1,0:T(8,128)(2,1)S(1)}, u32[]{:S(2)}, u32[]{:S(2)}) %collective-permute-start.5) | collective-permute-done | bytes 540704 | tf_op jit(solution)/shard_map/ppermute | solution.py:610
  247.2 1.4 fusion.3
  248.8 2.7 collective-permute-start.12
  251.4 0.7 collective-permute-start.13
  252.1 1.7 collective-permute-start.14
  253.9 1.0 collective-permute-done.10.a2
  254.8 0.9 collective-permute-start.15
  255.8 2.4 collective-permute-done.11.a1
  258.2 1.1 collective-permute-done.15.b3
  259.4 1.5 collective-permute-start.16
  261.3 2.2 collective-permute-start.18
  263.6 3.3 %tail.1 = bf16[576,256]{1,0:T(8,128)(2,1)} custom-call(bf16[528,128]{1,0:T(8,128)(2,1)} %copy-done.2, bf16[528,128]{1,0:T(8,128)(2,1)} %copy-done.7, bf16[528,128]{1,0:T(8,128)(2,1)} %copy-done.6, bf16[528,128]{1,0:T(8,128)(2,1)} %copy-done.8, bf16[384,128]{1,0:T(8,128)(2,1)} %get-tuple-element.107.b0, bf16[384,128]{1,0:T(8,128)(2,1)} %copy-done.9, ...), custom_call_target="tpu_custom_call" | custom-call | flops 100000000 | bytes 1000000 | tf_op jit(solution)/shard_map/tail/pallas_call | solution.py:63
  267.1 1.7 collective-permute-start.22
  268.8 2.0 collective-permute-start.23
  272.6 2.7 collective-permute-start.25
  275.4 2.0 collective-permute-done.24
  277.4 2.1 collective-permute-done.25
  279.6 7.0 %collective-permute-start.27 = (bf16[4,4,144,128]{3,2,1,0:T(8,128)(2,1)S(1)}, bf16[4,4,144,128]{3,2,1,0:T(8,128)(2,1)S(1)}, u32[]{:S(2)}, u32[]{:S(2)}) collective-permute-start(bf16[4,4,144,128]{3,2,1,0:T(8,128)(2,1)S(1)} %pad_maximum_fusion.1.own_ref), channel_id=1, source_target_pairs={{0,1},{1,0},{2,3},{3,2},{4,5},{5,4},{6,7},{7,6},{8,9},{9,8},{10,11... | collective-permute-start | bytes 1769480 | tf_op jit(solution)/shard_map/ppermute | solution.py:614
  286.6 1.0 fusion.21
  287.6 5.0 %collective-permute-start.20 = (bf16[576,128]{1,0:T(8,128)(2,1)S(1)}, bf16[576,128]{1,0:T(8,128)(2,1)S(1)}, u32[]{:S(2)}, u32[]{:S(2)}) collective-permute-start(bf16[576,128]{1,0:T(8,128)(2,1)S(1)} %get-tuple-element.144), channel_id=1, source_target_pairs={{0,31},{1,30},{2,29},{3,28},{4,27},{5,26},{6,25},{7,24},{8,23},{9,... | collective-permute-start | bytes 442376 | tf_op jit(solution)/shard_map/ppermute | solution.py:618
  292.9 3.8 %collective-permute-done.20 = bf16[576,128]{1,0:T(8,128)(2,1)S(1)} collective-permute-done((bf16[576,128]{1,0:T(8,128)(2,1)S(1)}, bf16[576,128]{1,0:T(8,128)(2,1)S(1)}, u32[]{:S(2)}, u32[]{:S(2)}) %collective-permute-start.20) | collective-permute-done | bytes 147488 | tf_op jit(solution)/shard_map/ppermute | solution.py:618
  296.7 0.7 maximum_bitcast_fusion.1
  297.4 4.4 %collective-permute-done.19 = bf16[576,128]{1,0:T(8,128)(2,1)S(1)} collective-permute-done((bf16[576,128]{1,0:T(8,128)(2,1)S(1)}, bf16[576,128]{1,0:T(8,128)(2,1)S(1)}, u32[]{:S(2)}, u32[]{:S(2)}) %collective-permute-start.19) | collective-permute-done | bytes 147488 | tf_op jit(solution)/shard_map/ppermute | solution.py:618
  301.9 0.7 maximum_bitcast_fusion
  302.6 0.8 copy-done.4
  303.4 3.0 late_finish.1
  306.5 1.3 reduce.1
  307.7 1.3 reduce.2
  309.0 8.6 %early_gradients.1 = (f32[576,1536]{1,0:T(8,128)}, f32[576,1536]{1,0:T(8,128)}, f32[576,1536]{1,0:T(8,128)}, f32[576,576]{1,0:T(8,128)}) custom-call(bf16[64,2,2,96,128]{4,3,2,1,0:T(8,128)(2,1)} %bitcast.64), custom_call_target="tpu_custom_call" | custom-call | flops 10000000 | bytes 19000000 | tf_op jit(solution)/shard_map/early_gradients/pallas_call | solution.py:471
  (74 shorter events, 6.3 us)
Async XLA Ops:
  7.2 17.7 %copy-start.13 = (f32[576]{0:T(1024)S(1)}, f32[576]{0:T(1024)}, u32[]{:S(2)}) copy-start(f32[576]{0:T(1024)} %param.21) | copy-start | bytes 6916
  7.2 64.9 %all-gather.7.cloned.1.call-start = ((), (), s32[]{:S(2)}) async-start(), calls=%async_computation.1 | async-start | bytes 9191424 | tf_op jit(solution)/shard_map/all_gather | solution.py:673
  12.9 163.8 %all-gather.9.cloned.1.call-start = ((), (), s32[]{:S(2)}) async-start(), calls=%async_computation.2 | async-start | bytes 9732096 | tf_op jit(solution)/shard_map/all_gather | solution.py:674
  17.5 16.3 %collective-permute-start = (bf16[1168,128]{1,0:T(8,128)(2,1)S(1)}, bf16[1168,128]{1,0:T(8,128)(2,1)S(1)}, u32[]{:S(2)}, u32[]{:S(2)}) collective-permute-start(bf16[1168,128]{1,0:T(8,128)(2,1)S(1)} %get-tuple-element.142), channel_id=1, source_target_pairs={{0,31},{1,30},{2,29},{3,28},{4,27},{5,26},{6,25},{7,24},{8,23},{9,... | collective-permute-start | bytes 897032 | tf_op jit(solution)/shard_map/ppermute | solution.py:618
  113.6 6.3 %collective-permute-start.1 = (bf16[16,8,96,128]{3,2,1,0:T(8,128)(2,1)}, bf16[16,8,96,128]{3,2,1,0:T(8,128)(2,1)S(1)}, u32[]{:S(2)}, u32[]{:S(2)}) collective-permute-start(bf16[16,8,96,128]{3,2,1,0:T(8,128)(2,1)} %get-tuple-element.76), channel_id=1, source_target_pairs={{0,1},{1,0},{2,3},{3,2},{4,5},{5,4},{6,7},{7,6},{8,9},{9,8},{10,11... | collective-permute-start | bytes 9437192 | tf_op jit(solution)/shard_map/ppermute | solution.py:614
  124.5 48.8 %all-to-all-start = ((bf16[64,2,96,128]{3,2,1,0:T(8,128)(2,1)}), bf16[64,2,96,128]{3,2,1,0:T(8,128)(2,1)S(1)}, u32[]{:S(2)}, u32[]{:S(2)}) async-start(bf16[64,2,96,128]{3,2,1,0:T(8,128)(2,1)} %bitcast.59), calls=%async_computation | async-start | bytes 6291456 | tf_op jit(solution)/shard_map/all_to_all | solution.py:704
  133.7 175.4 %all-gather.11.cloned.1.call-start = ((), (), s32[]{:S(2)}) async-start(), calls=%async_computation.3 | async-start | bytes 6340608 | tf_op jit(solution)/shard_map/all_gather | solution.py:709
  168.7 7.3 %copy-start.12 = (f32[576]{0:T(1024)S(1)}, f32[576]{0:T(1024)}, u32[]{:S(2)}) copy-start(f32[576]{0:T(1024)} %param.16) | copy-start | bytes 6916
  174.4 29.4 %collective-permute-start.2 = (bf16[2,4,4,384,128]{4,3,2,1,0:T(8,128)(2,1)}, bf16[2,4,4,384,128]{4,3,2,1,0:T(8,128)(2,1)S(1)}, u32[]{:S(2)}, u32[]{:S(2)}) collective-permute-start(bf16[2,4,4,384,128]{4,3,2,1,0:T(8,128)(2,1)} %get-tuple-element.83.dkv_other), channel_id=1, source_target_pairs={{0,1},{1,0},{2,3},{3,2},{4,5},{5,4},{6,7},{7,6},{8,9},{9,8},{10,11... | collective-permute-start | bytes 9437192 | tf_op jit(solution)/shard_map/ppermute | solution.py:614
  201.5 2.2 collective-permute-start.3
  203.7 0.8 copy-start.3
  203.7 1.9 copy-start
  210.7 12.9 %collective-permute-start.7 = (bf16[4,384,128]{2,1,0:T(8,128)(2,1)}, bf16[4,384,128]{2,1,0:T(8,128)(2,1)S(1)}, u32[]{:S(2)}, u32[]{:S(2)}) collective-permute-start(bf16[4,384,128]{2,1,0:T(8,128)(2,1)} %get-tuple-element.95), channel_id=1, source_target_pairs={{0,4},{2,6},{4,0},{6,2},{1,5},{3,7},{5,1},{7,3},{8,12},{10,14},{12... | collective-permute-start | bytes 1179656 | tf_op jit(solution)/shard_map/ppermute | solution.py:610
  212.8 19.7 %collective-permute-start.8 = (bf16[4,384,128]{2,1,0:T(8,128)(2,1)}, bf16[4,384,128]{2,1,0:T(8,128)(2,1)S(1)}, u32[]{:S(2)}, u32[]{:S(2)}) collective-permute-start(bf16[4,384,128]{2,1,0:T(8,128)(2,1)} %get-tuple-element.96), channel_id=1, source_target_pairs={{0,2},{2,4},{4,6},{6,0},{1,3},{3,5},{5,7},{7,1},{8,10},{10,12},{12... | collective-permute-start | bytes 1179656 | tf_op jit(solution)/shard_map/ppermute | solution.py:610
  212.8 19.7 %collective-permute-start.9 = (bf16[4,384,128]{2,1,0:T(8,128)(2,1)}, bf16[4,384,128]{2,1,0:T(8,128)(2,1)S(1)}, u32[]{:S(2)}, u32[]{:S(2)}) collective-permute-start(bf16[4,384,128]{2,1,0:T(8,128)(2,1)} %get-tuple-element.97), channel_id=1, source_target_pairs={{0,6},{2,0},{4,2},{6,4},{1,7},{3,1},{5,3},{7,5},{8,14},{10,8},{12,... | collective-permute-start | bytes 1179656 | tf_op jit(solution)/shard_map/ppermute | solution.py:610
  215.5 18.9 %collective-permute-start.4 = (bf16[4,528,128]{2,1,0:T(8,128)(2,1)}, bf16[4,528,128]{2,1,0:T(8,128)(2,1)S(1)}, u32[]{:S(2)}, u32[]{:S(2)}) collective-permute-start(bf16[4,528,128]{2,1,0:T(8,128)(2,1)} %get-tuple-element.91), channel_id=1, source_target_pairs={{0,16},{8,24},{16,0},{24,8},{1,17},{9,25},{17,1},{25,9},{2,18},{10... | collective-permute-start | bytes 1622024 | tf_op jit(solution)/shard_map/ppermute | solution.py:610
  217.0 30.1 %collective-permute-start.5 = (bf16[4,528,128]{2,1,0:T(8,128)(2,1)}, bf16[4,528,128]{2,1,0:T(8,128)(2,1)S(1)}, u32[]{:S(2)}, u32[]{:S(2)}) collective-permute-start(bf16[4,528,128]{2,1,0:T(8,128)(2,1)} %get-tuple-element.92), channel_id=1, source_target_pairs={{0,8},{8,16},{16,24},{24,0},{1,9},{9,17},{17,25},{25,1},{2,10},{10... | collective-permute-start | bytes 1622024 | tf_op jit(solution)/shard_map/ppermute | solution.py:610
  223.6 23.6 %collective-permute-start.6 = (bf16[4,528,128]{2,1,0:T(8,128)(2,1)}, bf16[4,528,128]{2,1,0:T(8,128)(2,1)S(1)}, u32[]{:S(2)}, u32[]{:S(2)}) collective-permute-start(bf16[4,528,128]{2,1,0:T(8,128)(2,1)} %get-tuple-element.93), channel_id=1, source_target_pairs={{0,24},{8,0},{16,8},{24,16},{1,25},{9,1},{17,9},{25,17},{2,26},{10... | collective-permute-start | bytes 1622024 | tf_op jit(solution)/shard_map/ppermute | solution.py:610
  248.6 15.0 %copy-start.2 = (bf16[528,128]{1,0:T(8,128)(2,1)}, bf16[528,128]{1,0:T(8,128)(2,1)S(1)}, u32[]{:S(2)}) copy-start(bf16[528,128]{1,0:T(8,128)(2,1)S(1)} %get-tuple-element.98.a0) | copy-start | bytes 405508
  248.6 44.0 %copy-start.5 = (bf16[576,256]{1,0:T(8,128)(2,1)S(1)}, bf16[576,256]{1,0:T(8,128)(2,1)}, u32[]{:S(2)}) copy-start(bf16[576,256]{1,0:T(8,128)(2,1)} %get-tuple-element.114) | copy-start | bytes 884740
  248.6 6.2 %collective-permute-start.10 = (bf16[528,128]{1,0:T(8,128)(2,1)S(1)}, bf16[528,128]{1,0:T(8,128)(2,1)S(1)}, u32[]{:S(2)}, u32[]{:S(2)}) collective-permute-start(bf16[528,128]{1,0:T(8,128)(2,1)S(1)} %get-tuple-element.99), channel_id=1, source_target_pairs={{0,4},{2,6},{4,0},{6,2},{1,5},{3,7},{5,1},{7,3},{8,12},{10,14},{12... | collective-permute-start | bytes 405512 | tf_op jit(solution)/shard_map/ppermute | solution.py:610
  248.7 9.5 %collective-permute-start.11 = (bf16[528,128]{1,0:T(8,128)(2,1)S(1)}, bf16[528,128]{1,0:T(8,128)(2,1)S(1)}, u32[]{:S(2)}, u32[]{:S(2)}) collective-permute-start(bf16[528,128]{1,0:T(8,128)(2,1)S(1)} %get-tuple-element.100), channel_id=1, source_target_pairs={{0,2},{2,4},{4,6},{6,0},{1,3},{3,5},{5,7},{7,1},{8,10},{10,12},{12... | collective-permute-start | bytes 405512 | tf_op jit(solution)/shard_map/ppermute | solution.py:610
  248.8 9.4 %collective-permute-start.12 = (bf16[528,128]{1,0:T(8,128)(2,1)S(1)}, bf16[528,128]{1,0:T(8,128)(2,1)S(1)}, u32[]{:S(2)}, u32[]{:S(2)}) collective-permute-start(bf16[528,128]{1,0:T(8,128)(2,1)S(1)} %get-tuple-element.101), channel_id=1, source_target_pairs={{0,6},{2,0},{4,2},{6,4},{1,7},{3,1},{5,3},{7,5},{8,14},{10,8},{12,... | collective-permute-start | bytes 405512 | tf_op jit(solution)/shard_map/ppermute | solution.py:610
  251.4 6.8 %collective-permute-start.13 = (bf16[384,128]{1,0:T(8,128)(2,1)S(1)}, bf16[384,128]{1,0:T(8,128)(2,1)S(1)}, u32[]{:S(2)}, u32[]{:S(2)}) collective-permute-start(bf16[384,128]{1,0:T(8,128)(2,1)S(1)} %get-tuple-element.103), channel_id=1, source_target_pairs={{0,8},{8,16},{16,24},{24,0},{1,9},{9,17},{17,25},{25,1},{2,10},{10... | collective-permute-start | bytes 294920 | tf_op jit(solution)/shard_map/ppermute | solution.py:610
  252.1 6.1 %collective-permute-start.14 = (bf16[384,128]{1,0:T(8,128)(2,1)S(1)}, bf16[384,128]{1,0:T(8,128)(2,1)S(1)}, u32[]{:S(2)}, u32[]{:S(2)}) collective-permute-start(bf16[384,128]{1,0:T(8,128)(2,1)S(1)} %get-tuple-element.104), channel_id=1, source_target_pairs={{0,16},{8,24},{16,0},{24,8},{1,17},{9,25},{17,1},{25,9},{2,18},{10... | collective-permute-start | bytes 294920 | tf_op jit(solution)/shard_map/ppermute | solution.py:610
  254.8 8.7 %copy-start.6 = (bf16[528,128]{1,0:T(8,128)(2,1)}, bf16[528,128]{1,0:T(8,128)(2,1)S(1)}, u32[]{:S(2)}) copy-start(bf16[528,128]{1,0:T(8,128)(2,1)S(1)} %collective-permute-done.10.a2) | copy-start | bytes 405508
  254.8 4.5 %collective-permute-start.15 = (bf16[384,128]{1,0:T(8,128)(2,1)S(1)}, bf16[384,128]{1,0:T(8,128)(2,1)S(1)}, u32[]{:S(2)}, u32[]{:S(2)}) collective-permute-start(bf16[384,128]{1,0:T(8,128)(2,1)S(1)} %get-tuple-element.105), channel_id=1, source_target_pairs={{0,24},{8,0},{16,8},{24,16},{1,25},{9,1},{17,9},{25,17},{2,26},{10... | collective-permute-start | bytes 294920 | tf_op jit(solution)/shard_map/ppermute | solution.py:610
  258.2 5.4 %copy-start.7 = (bf16[528,128]{1,0:T(8,128)(2,1)}, bf16[528,128]{1,0:T(8,128)(2,1)S(1)}, u32[]{:S(2)}) copy-start(bf16[528,128]{1,0:T(8,128)(2,1)S(1)} %collective-permute-done.11.a1) | copy-start | bytes 405508
  258.2 5.4 %copy-start.8 = (bf16[528,128]{1,0:T(8,128)(2,1)}, bf16[528,128]{1,0:T(8,128)(2,1)S(1)}, u32[]{:S(2)}) copy-start(bf16[528,128]{1,0:T(8,128)(2,1)S(1)} %collective-permute-done.12.a3) | copy-start | bytes 405508
  258.2 5.4 %copy-start.9 = (bf16[384,128]{1,0:T(8,128)(2,1)}, bf16[384,128]{1,0:T(8,128)(2,1)S(1)}, u32[]{:S(2)}) copy-start(bf16[384,128]{1,0:T(8,128)(2,1)S(1)} %collective-permute-done.13.b1) | copy-start | bytes 294916
  258.2 5.3 %copy-start.10 = (bf16[384,128]{1,0:T(8,128)(2,1)}, bf16[384,128]{1,0:T(8,128)(2,1)S(1)}, u32[]{:S(2)}) copy-start(bf16[384,128]{1,0:T(8,128)(2,1)S(1)} %collective-permute-done.14.b2) | copy-start | bytes 294916
  259.4 4.2 %copy-start.11 = (bf16[384,128]{1,0:T(8,128)(2,1)}, bf16[384,128]{1,0:T(8,128)(2,1)S(1)}, u32[]{:S(2)}) copy-start(bf16[384,128]{1,0:T(8,128)(2,1)S(1)} %collective-permute-done.15.b3) | copy-start | bytes 294916
  259.4 7.6 %collective-permute-start.16 = (bf16[144,128]{1,0:T(8,128)(2,1)S(1)}, bf16[144,128]{1,0:T(8,128)(2,1)S(1)}, u32[]{:S(2)}, u32[]{:S(2)}) collective-permute-start(bf16[144,128]{1,0:T(8,128)(2,1)S(1)} %add_convert_fusion.10), channel_id=1, source_target_pairs={{0,64},{32,96},{64,0},{96,32},{1,65},{33,97},{65,1},{97,33},{2,66}... | collective-permute-start | bytes 110600 | tf_op jit(solution)/shard_map/ppermute | solution.py:610
  260.9 6.1 %collective-permute-start.17 = (bf16[144,128]{1,0:T(8,128)(2,1)S(1)}, bf16[144,128]{1,0:T(8,128)(2,1)S(1)}, u32[]{:S(2)}, u32[]{:S(2)}) collective-permute-start(bf16[144,128]{1,0:T(8,128)(2,1)S(1)} %add_convert_fusion.10), channel_id=1, source_target_pairs={{0,32},{32,64},{64,96},{96,0},{1,33},{33,65},{65,97},{97,1},{2,34}... | collective-permute-start | bytes 110600 | tf_op jit(solution)/shard_map/ppermute | solution.py:610
  261.3 5.6 %collective-permute-start.18 = (bf16[144,128]{1,0:T(8,128)(2,1)S(1)}, bf16[144,128]{1,0:T(8,128)(2,1)S(1)}, u32[]{:S(2)}, u32[]{:S(2)}) collective-permute-start(bf16[144,128]{1,0:T(8,128)(2,1)S(1)} %add_convert_fusion.10), channel_id=1, source_target_pairs={{0,96},{32,0},{64,32},{96,64},{1,97},{33,1},{65,33},{97,65},{2,98}... | collective-permute-start | bytes 110600 | tf_op jit(solution)/shard_map/ppermute | solution.py:610
  267.0 4.1 %collective-permute-start.21 = (bf16[144,128]{1,0:T(8,128)(2,1)S(1)}, bf16[144,128]{1,0:T(8,128)(2,1)S(1)}, u32[]{:S(2)}, u32[]{:S(2)}) collective-permute-start(bf16[144,128]{1,0:T(8,128)(2,1)S(1)} %add_convert_fusion.9), channel_id=1, source_target_pairs={{0,2},{2,4},{4,6},{6,0},{1,3},{3,5},{5,7},{7,1},{8,10},{10,12},{12... | collective-permute-start | bytes 110600 | tf_op jit(solution)/shard_map/ppermute | solution.py:610
  267.1 4.4 %collective-permute-start.22 = (bf16[144,128]{1,0:T(8,128)(2,1)S(1)}, bf16[144,128]{1,0:T(8,128)(2,1)S(1)}, u32[]{:S(2)}, u32[]{:S(2)}) collective-permute-start(bf16[144,128]{1,0:T(8,128)(2,1)S(1)} %add_convert_fusion.9), channel_id=1, source_target_pairs={{0,4},{2,6},{4,0},{6,2},{1,5},{3,7},{5,1},{7,3},{8,12},{10,14},{12... | collective-permute-start | bytes 110600 | tf_op jit(solution)/shard_map/ppermute | solution.py:610
  268.8 3.3 %collective-permute-start.23 = (bf16[144,128]{1,0:T(8,128)(2,1)S(1)}, bf16[144,128]{1,0:T(8,128)(2,1)S(1)}, u32[]{:S(2)}, u32[]{:S(2)}) collective-permute-start(bf16[144,128]{1,0:T(8,128)(2,1)S(1)} %add_convert_fusion.9), channel_id=1, source_target_pairs={{0,6},{2,0},{4,2},{6,4},{1,7},{3,1},{5,3},{7,5},{8,14},{10,8},{12,... | collective-permute-start | bytes 110600 | tf_op jit(solution)/shard_map/ppermute | solution.py:610
  272.1 5.3 %collective-permute-start.24 = (bf16[4,144,128]{2,1,0:T(8,128)(2,1)S(1)}, bf16[4,144,128]{2,1,0:T(8,128)(2,1)S(1)}, u32[]{:S(2)}, u32[]{:S(2)}) collective-permute-start(bf16[4,144,128]{2,1,0:T(8,128)(2,1)S(1)} %get-tuple-element.148), channel_id=1, source_target_pairs={{0,8},{8,16},{16,24},{24,0},{1,9},{9,17},{17,25},{25,1},{2,10},{10... | collective-permute-start | bytes 442376 | tf_op jit(solution)/shard_map/ppermute | solution.py:610
  272.6 6.8 %collective-permute-start.25 = (bf16[4,144,128]{2,1,0:T(8,128)(2,1)S(1)}, bf16[4,144,128]{2,1,0:T(8,128)(2,1)S(1)}, u32[]{:S(2)}, u32[]{:S(2)}) collective-permute-start(bf16[4,144,128]{2,1,0:T(8,128)(2,1)S(1)} %get-tuple-element.148), channel_id=1, source_target_pairs={{0,16},{8,24},{16,0},{24,8},{1,17},{9,25},{17,1},{25,9},{2,18},{10... | collective-permute-start | bytes 442376 | tf_op jit(solution)/shard_map/ppermute | solution.py:610
  275.3 4.2 %collective-permute-start.26 = (bf16[4,144,128]{2,1,0:T(8,128)(2,1)S(1)}, bf16[4,144,128]{2,1,0:T(8,128)(2,1)S(1)}, u32[]{:S(2)}, u32[]{:S(2)}) collective-permute-start(bf16[4,144,128]{2,1,0:T(8,128)(2,1)S(1)} %get-tuple-element.148), channel_id=1, source_target_pairs={{0,24},{8,0},{16,8},{24,16},{1,25},{9,1},{17,9},{25,17},{2,26},{10... | collective-permute-start | bytes 442376 | tf_op jit(solution)/shard_map/ppermute | solution.py:610
  279.6 23.0 %copy-start.1 = (bf16[4,4,144,128]{3,2,1,0:T(8,128)(2,1)}, bf16[4,4,144,128]{3,2,1,0:T(8,128)(2,1)S(1)}, u32[]{:S(2)}) copy-start(bf16[4,4,144,128]{3,2,1,0:T(8,128)(2,1)S(1)} %pad_maximum_fusion.1.own_ref) | copy-start | bytes 1769476
  279.6 23.0 %collective-permute-start.27 = (bf16[4,4,144,128]{3,2,1,0:T(8,128)(2,1)S(1)}, bf16[4,4,144,128]{3,2,1,0:T(8,128)(2,1)S(1)}, u32[]{:S(2)}, u32[]{:S(2)}) collective-permute-start(bf16[4,4,144,128]{3,2,1,0:T(8,128)(2,1)S(1)} %pad_maximum_fusion.1.own_ref), channel_id=1, source_target_pairs={{0,1},{1,0},{2,3},{3,2},{4,5},{5,4},{6,7},{7,6},{8,9},{9,8},{10,11... | collective-permute-start | bytes 1769480 | tf_op jit(solution)/shard_map/ppermute | solution.py:614
  287.6 9.1 %collective-permute-start.20 = (bf16[576,128]{1,0:T(8,128)(2,1)S(1)}, bf16[576,128]{1,0:T(8,128)(2,1)S(1)}, u32[]{:S(2)}, u32[]{:S(2)}) collective-permute-start(bf16[576,128]{1,0:T(8,128)(2,1)S(1)} %get-tuple-element.144), channel_id=1, source_target_pairs={{0,31},{1,30},{2,29},{3,28},{4,27},{5,26},{6,25},{7,24},{8,23},{9,... | collective-permute-start | bytes 442376 | tf_op jit(solution)/shard_map/ppermute | solution.py:618
  292.6 9.2 %collective-permute-start.19 = (bf16[576,128]{1,0:T(8,128)(2,1)S(1)}, bf16[576,128]{1,0:T(8,128)(2,1)S(1)}, u32[]{:S(2)}, u32[]{:S(2)}) collective-permute-start(bf16[576,128]{1,0:T(8,128)(2,1)S(1)} %get-tuple-element.146), channel_id=1, source_target_pairs={{0,31},{1,30},{2,29},{3,28},{4,27},{5,26},{6,25},{7,24},{8,23},{9,... | collective-permute-start | bytes 442376 | tf_op jit(solution)/shard_map/ppermute | solution.py:618
  302.6 0.8 copy-start.4
Sparse Core Ops, SparseCore 0:
  13.0 59.0 all-gather.6
  74.3 55.0 all-gather.8
  174.5 80.1 all-gather.10
